TPU v7x, 128 devices: a whole 4x4x4 slice. The times are simulated.
128 devices in a mesh: rows: 16 (over z, x_lo, core), pairs: 8 (over x_hi, y).
Axes of the slice: x: 4 (x_hi: 2, x_lo: 2; x = x_hi * 2 + x_lo), y: 4, z: 4, core: 2. Of those that a mesh axis runs over, the one named last changes fastest.
Arguments:
- observed: float32 [24576, 4096], P('rows', 'pairs'), as said below
- estimate: float32 [24576, 4096], P('rows', 'pairs'), may hold values from -0.03827328 to 0.03827328
- mask: int32 [24576, 4096], P('rows', 'pairs'), may hold values from 0 to 1
- threshold: float32 [4096], P('pairs'), may hold values from 0.02 to 0.12
Outputs:
- regrouped: float32 [4096, 24576], P(('rows', 'pairs'))
Inputs may be any that keep to these rules, and one draw needn't show every extreme that they name: observed has entries of order 24576^-1/2.
All inputs are finite; a program needn't handle non-finite values.
Results may differ from a plain program's by a relative error of at most 0.0003.
Values sent between devices are 32-bit elements; how exact they have to be, the bound alone decides.
No kernel may reach another device: no remote copies, remote signals or barrier semaphores. Data moves between devices by JAX's collectives and lax.ppermute only.
A program may use at most 128 MiB of HBM per device.

v0:
```python
import jax
import jax.numpy as jnp
from jax import lax
from jax.sharding import PartitionSpec as P

ROUNDS = 4
NS_STEPS = 3


HI = lax.Precision.HIGHEST


def from_behind(block, axis, distance):
    devices = range(lax.axis_size(axis))
    route = [((i - distance) % len(devices), i) for i in devices]
    return lax.ppermute(block, axis, route)


def whitening_of(gram):
    width = gram.shape[-1]
    eye = jnp.eye(width, dtype=jnp.float32)
    dsum = jnp.diagonal(gram, axis1=-2, axis2=-1) + 1e-06
    inv_root = 1.0 / jnp.sqrt(dsum)
    normed = gram * inv_root[..., :, None] * inv_root[..., None, :]
    fro = jnp.sqrt(jnp.sum(normed * normed, axis=(-2, -1)))
    ymat = normed / fro[..., None, None]
    zmat = jnp.broadcast_to(eye, normed.shape)
    for step in range(NS_STEPS):
        tmat = 1.5 * eye - 0.5 * jnp.einsum("pij,pjk->pik", zmat, ymat, precision=HI)
        ymat = jnp.einsum("pij,pjk->pik", ymat, tmat, precision=HI)
        zmat = jnp.einsum("pij,pjk->pik", tmat, zmat, precision=HI)
    return (
        inv_root[..., :, None]
        * zmat
        * jnp.sqrt(dsum)[..., None, :]
        / jnp.sqrt(fro)[..., None, None]
    )


def on_device(observed, estimate, mask, threshold):
    filled = jnp.where(mask == 1, observed, estimate)
    rows_here, width = filled.shape
    block = width // 4
    for round_index in range(ROUNDS):
        pairs = filled.reshape(rows_here, 2, 2 * block)
        partial_gram = jnp.einsum("rpi,rpj->pij", pairs, pairs, precision=HI)
        gram = lax.psum(partial_gram, "rows")
        whitening = whitening_of(gram)
        pairs = jnp.einsum("rpi,pij->rpj", pairs, whitening, precision=HI)
        quads = pairs.reshape(rows_here, 4, block)
        if round_index + 1 < ROUNDS:
            moved = from_behind(quads[:, 3], "pairs", 1)
            quads = jnp.stack([quads[:, 0], moved, quads[:, 2], quads[:, 1]], axis=1)
        filled = quads.reshape(rows_here, width)
    squares = lax.psum(jnp.sum(filled * filled, axis=0), "rows")
    col_norm = jnp.sqrt(squares + 1e-06)
    factor = jnp.maximum(col_norm - threshold, 0.0) / col_norm
    shrunk_t = (filled * factor[None, :]).T
    count_rows = lax.axis_size("rows")
    count_pairs = lax.axis_size("pairs")
    each_dest = width // (count_rows * count_pairs)
    packed = shrunk_t.reshape(count_rows * count_pairs, each_dest, rows_here)
    landed = lax.all_to_all(packed, ("rows", "pairs"), split_axis=0, concat_axis=1, tiled=True)
    landed = landed.reshape(count_rows, count_pairs, each_dest, rows_here).transpose(2, 1, 0, 3)
    return landed.reshape(each_dest * count_pairs, count_rows * rows_here)


def solution(mesh):
    placed = (P("rows", "pairs"), P("rows", "pairs"), P("rows", "pairs"), P("pairs"))
    return jax.shard_map(
        on_device, mesh=mesh, in_specs=placed, out_specs=P(("rows", "pairs"), None), check_vma=False
    )
```

profile of v0, /device:TPU:0, one launch (start us, length us, event | category | flops | bytes accessed | tf_op | source)
XLA Modules:
  0.0 811.0 jit_solution(9528418893869971841)
XLA Ops:
  6.5 4.9 compare_select_fusion
  11.4 6.2 fusion.2
  18.5 119.8 %all-reduce.5.cloned.1.call-done = f32[2,256,256]{2,1,0:T(8,128)} async-done(((f32[2,256,256]{2,1,0:T(8,128)}), f32[2,256,256]{2,1,0:T(8,128)}) %all-reduce.5.cloned.1.call-update) | async-done | bytes 524304 | tf_op jit(solution)/shard_map/psum | solution.py:47
  138.3 17.5 %copy.34 = f32[2,256,256]{0,2,1:T(8,128)} copy(f32[2,256,256]{2,1,0:T(8,128)} %all-reduce.5.cloned.1.call-done) | data formatting | bytes 1048576 | tf_op jit(solution)/shard_map/psum | solution.py:47
  155.7 3.0 gather_fusion
  158.7 1.6 sqrt_bitcast_fusion.3
  160.3 1.0 copy.35
  161.3 1.4 multiply_reduce_fusion.3
  162.7 1.9 fusion.26
  166.6 1.4 fusion.60
  168.1 1.4 fusion.61
  169.6 1.9 fusion.24
  171.5 1.7 fusion.23
  173.2 5.3 fusion
  178.8 1.6 collective-permute-start
  180.4 21.2 %collective-permute-done = f32[1536,128]{0,1:T(8,128)S(1)} collective-permute-done((f32[1536,128]{0,1:T(8,128)S(1)}, f32[1536,128]{0,1:T(8,128)S(1)}, u32[]{:S(2)}, u32[]{:S(2)}) %collective-permute-start) | collective-permute-done | bytes 786464 | tf_op jit(solution)/shard_map/ppermute | solution.py:16
  201.9 3.9 fusion.62
  206.3 113.6 %all-reduce.7.cloned.1.call-done = f32[2,256,256]{2,1,0:T(8,128)} async-done(((f32[2,256,256]{2,1,0:T(8,128)}), f32[2,256,256]{2,1,0:T(8,128)}) %all-reduce.7.cloned.1.call-update) | async-done | bytes 524304 | tf_op jit(solution)/shard_map/psum | solution.py:47
  319.8 17.3 %copy.41 = f32[2,256,256]{0,2,1:T(8,128)} copy(f32[2,256,256]{2,1,0:T(8,128)} %all-reduce.7.cloned.1.call-done) | data formatting | bytes 1048576 | tf_op jit(solution)/shard_map/psum | solution.py:47
  337.1 3.0 gather_fusion.1
  340.1 1.6 sqrt_bitcast_fusion.2
  341.7 1.0 copy.42
  342.7 1.4 multiply_reduce_fusion.2
  344.1 1.9 fusion.21
  348.0 1.4 fusion.63
  349.4 1.4 fusion.64
  351.0 1.9 fusion.19
  352.8 1.7 fusion.18
  354.6 3.1 fusion.65
  357.9 1.7 collective-permute-start.1
  359.7 21.2 %collective-permute-done.1 = f32[1536,128]{0,1:T(8,128)S(1)} collective-permute-done((f32[1536,128]{0,1:T(8,128)S(1)}, f32[1536,128]{0,1:T(8,128)S(1)}, u32[]{:S(2)}, u32[]{:S(2)}) %collective-permute-start.1) | collective-permute-done | bytes 786464 | tf_op jit(solution)/shard_map/ppermute | solution.py:16
  381.2 3.8 fusion.66
  385.1 114.1 %all-reduce.9.cloned.1.call-done = f32[2,256,256]{2,1,0:T(8,128)} async-done(((f32[2,256,256]{2,1,0:T(8,128)}), f32[2,256,256]{2,1,0:T(8,128)}) %all-reduce.9.cloned.1.call-update) | async-done | bytes 524304 | tf_op jit(solution)/shard_map/psum | solution.py:47
  499.2 17.3 %copy.48 = f32[2,256,256]{0,2,1:T(8,128)} copy(f32[2,256,256]{2,1,0:T(8,128)} %all-reduce.9.cloned.1.call-done) | data formatting | bytes 1048576 | tf_op jit(solution)/shard_map/psum | solution.py:47
  516.5 3.0 gather_fusion.2
  519.4 1.6 sqrt_bitcast_fusion.1
  521.0 1.0 copy.49
  522.0 1.4 multiply_reduce_fusion.1
  523.4 1.9 fusion.16
  527.3 1.5 fusion.67
  528.8 1.4 fusion.68
  530.3 1.9 fusion.14
  532.2 1.7 fusion.13
  533.9 3.1 fusion.69
  537.3 1.8 collective-permute-start.2
  539.0 21.2 %collective-permute-done.2 = f32[1536,128]{0,1:T(8,128)S(1)} collective-permute-done((f32[1536,128]{0,1:T(8,128)S(1)}, f32[1536,128]{0,1:T(8,128)S(1)}, u32[]{:S(2)}, u32[]{:S(2)}) %collective-permute-start.2) | collective-permute-done | bytes 786464 | tf_op jit(solution)/shard_map/ppermute | solution.py:16
  560.5 3.9 fusion.70
  564.4 114.1 %all-reduce.11.cloned.1.call-done = f32[2,256,256]{2,1,0:T(8,128)} async-done(((f32[2,256,256]{2,1,0:T(8,128)}), f32[2,256,256]{2,1,0:T(8,128)}) %all-reduce.11.cloned.1.call-update) | async-done | bytes 524304 | tf_op jit(solution)/shard_map/psum | solution.py:47
  678.5 17.3 %copy.55 = f32[2,256,256]{0,2,1:T(8,128)} copy(f32[2,256,256]{2,1,0:T(8,128)} %all-reduce.11.cloned.1.call-done) | data formatting | bytes 1048576 | tf_op jit(solution)/shard_map/psum | solution.py:47
  695.8 3.0 gather_fusion.3
  698.8 1.6 sqrt_bitcast_fusion
  700.4 1.0 copy.56
  701.4 1.4 multiply_reduce_fusion
  702.8 1.9 fusion.11
  706.7 1.5 fusion.71
  708.1 1.4 fusion.72
  709.7 1.9 fusion.9
  711.5 1.7 fusion.8
  713.3 4.7 fusion.4
  718.0 30.7 %psum.39 = f32[512]{0:T(512)S(1)} all-reduce(f32[512]{0:T(512)S(1)} %bitcast.140), channel_id=1, replica_groups=mesh['rows'=16,'pairs'=8] {'rows'}, use_global_device_ids=true, to_apply=%region_9.10 | all-reduce | flops 512 | bytes 4096 | tf_op jit(solution)/shard_map/psum | solution.py:55
  748.7 2.2 bitcast_multiply_fusion
  750.9 2.1 reshape.107
  753.0 48.4 %all_to_all.4 = f32[128,4,1536]{2,1,0:T(4,128)S(1)} all-to-all(f32[128,4,1536]{2,1,0:T(4,128)} %reshape.107), channel_id=1, replica_groups=mesh['rows'=16,'pairs'=8] {'rows','pairs'}, dimensions={0} | all-to-all | bytes 6291456 | tf_op jit(solution)/shard_map/all_to_all | solution.py:63
  801.4 2.6 copy.61
  (57 shorter events, 11.5 us)
Async XLA Ops:
  6.5 131.7 %all-reduce.5.cloned.1.call-start = ((), (), s32[]{:S(2)}) async-start(), calls=%async_computation.1 | async-start | bytes 1048576 | tf_op jit(solution)/shard_map/psum | solution.py:47
  17.7 302.2 %all-reduce.7.cloned.1.call-start = ((), (), s32[]{:S(2)}) async-start(), calls=%async_computation.2 | async-start | bytes 1048576 | tf_op jit(solution)/shard_map/psum | solution.py:47
  161.3 3.3 copy-start
  161.3 3.9 copy-start.4
  178.8 22.7 %collective-permute-start = (f32[1536,128]{0,1:T(8,128)S(1)}, f32[1536,128]{0,1:T(8,128)S(1)}, u32[]{:S(2)}, u32[]{:S(2)}) collective-permute-start(f32[1536,128]{0,1:T(8,128)S(1)} %get-tuple-element.16), channel_id=1, source_target_pairs={{7,0},{0,1},{1,2},{2,3},{3,4},{4,5},{5,6},{6,7},{15,8},{8,9},{9,10... | collective-permute-start | bytes 2359304 | tf_op jit(solution)/shard_map/ppermute | solution.py:16
  205.7 293.4 %all-reduce.9.cloned.1.call-start = ((), (), s32[]{:S(2)}) async-start(), calls=%async_computation.3 | async-start | bytes 1048576 | tf_op jit(solution)/shard_map/psum | solution.py:47
  342.7 3.3 copy-start.1
  342.7 3.9 copy-start.5
  357.9 22.9 %collective-permute-start.1 = (f32[1536,128]{0,1:T(8,128)S(1)}, f32[1536,128]{0,1:T(8,128)S(1)}, u32[]{:S(2)}, u32[]{:S(2)}) collective-permute-start(f32[1536,128]{0,1:T(8,128)S(1)} %get-tuple-element.12), channel_id=1, source_target_pairs={{7,0},{0,1},{1,2},{2,3},{3,4},{4,5},{5,6},{6,7},{15,8},{8,9},{9,10... | collective-permute-start | bytes 2359304 | tf_op jit(solution)/shard_map/ppermute | solution.py:16
  385.0 293.5 %all-reduce.11.cloned.1.call-start = ((), (), s32[]{:S(2)}) async-start(), calls=%async_computation.4 | async-start | bytes 1048576 | tf_op jit(solution)/shard_map/psum | solution.py:47
  522.0 3.3 copy-start.2
  522.0 3.9 copy-start.6
  537.3 23.0 %collective-permute-start.2 = (f32[1536,128]{0,1:T(8,128)S(1)}, f32[1536,128]{0,1:T(8,128)S(1)}, u32[]{:S(2)}, u32[]{:S(2)}) collective-permute-start(f32[1536,128]{0,1:T(8,128)S(1)} %get-tuple-element.8), channel_id=1, source_target_pairs={{7,0},{0,1},{1,2},{2,3},{3,4},{4,5},{5,6},{6,7},{15,8},{8,9},{9,10... | collective-permute-start | bytes 2359304 | tf_op jit(solution)/shard_map/ppermute | solution.py:16
  701.4 3.3 copy-start.3
  701.4 3.9 copy-start.7
  713.3 35.4 %copy-start.8 = (f32[512]{0:T(512)S(1)}, f32[512]{0:T(512)}, u32[]{:S(2)}) copy-start(f32[512]{0:T(512)} %param.7) | copy-start | bytes 6148
Sparse Core Ops, SparseCore 0:
  17.8 120.4 all-reduce.4
  205.9 113.9 all-reduce.6
  385.2 113.9 all-reduce.8
  564.5 113.9 all-reduce.10
where the time goes:
time: 819 us; the launch traced here: 811 us
  waiting for transfers between devices  525 us (64%)
  local copies, waits for them, and re-layouts  91.1 us (11%)
  blocking collectives  79.1 us (10%)
  matrix products  75.5 us (9%)
  other arithmetic  20.6 us (3%)
  between operations  13.9 us (2%)
    psum x4, waiting for transfers between devices, on_device(): gram = lax.psum(partial_gram, 'rows')  462 us
    psum x4, local copies, waits for them, and re-layouts, on_device(): gram = lax.psum(partial_gram, 'rows')  69.3 us
    ppermute x3, waiting for transfers between devices, from_behind(): return lax.ppermute(block, axis, route)  63.6 us
    all_to_all x1, blocking collectives, on_device(): lax.all_to_all(packed, ('rows', 'pairs'), split_axis=0, concat_axis=1, ti...  48.4 us
    psum x1, blocking collectives, on_device(): squares = lax.psum(jnp.sum(filled * filled, axis=0), 'rows')  30.7 us
    dot_general x4, matrix products, on_device(): partial_gram = jnp.einsum('rpi,rpj->pij', pairs, pairs, precision=HI)  17.7 us
    dot_general x12, matrix products, whitening_of(): jnp.einsum('pij,pjk->pik', zmat, ymat, precision=HI)  17.6 us
  transfers between devices with their start and end apart: 7, of which 7 were waited for; matrix products, arithmetic and copies ran while one was open for 0% of the time, Pallas kernels for 0%

commit v1 on v0

v1 whole, which is shorter than its diff:
```python
import functools

import jax
import jax.numpy as jnp
from jax import lax
from jax.experimental import pallas as pl
from jax.experimental.pallas import tpu as pltpu
from jax.sharding import Mesh, PartitionSpec as P

ROUNDS = 4
BW = 128
PW = 2 * BW
RH = 1536
RB = 2 * RH
CH = 512
AXES = ("zx", "core", "pairs")
F32 = jnp.float32
BF16 = jnp.bfloat16
VMEM = pl.BlockSpec(memory_space=pltpu.VMEM)
SMEM = pl.BlockSpec(memory_space=pltpu.SMEM)
NN = (((1,), (0,)), ((), ()))
NT = (((1,), (1,)), ((), ()))


def params():
    return pltpu.CompilerParams(vmem_limit_bytes=44 * 1024 * 1024)


def cost(flops, moved):
    return pl.CostEstimate(flops=flops, bytes_accessed=moved, transcendentals=0)


def split(x):
    high = x.astype(BF16)
    return high, (x - high.astype(F32)).astype(BF16)


def mxu(a, b, dims=NN):
    return lax.dot_general(a, b, dims, preferred_element_type=F32)


def dot3(a, b):
    (ah, al), (bh, bl) = a, b
    return mxu(ah, bh) + (mxu(ah, bl) + mxu(al, bh))


def fill_kernel(core_ref, obs_ref, est_ref, mask_ref, keep_ref, send_ref):
    filled = jnp.where(mask_ref[...] == 1, obs_ref[...], est_ref[...])
    first = core_ref[0] == 0
    a = filled[:, :PW]
    b = filled[:, PW:]
    keep_ref[...] = jnp.where(first, a, b).T
    send_ref[...] = jnp.where(first, b, a).T


def fill(core, observed, estimate, mask):
    step = 256
    rows = pl.BlockSpec((step, 2 * PW), lambda i: (i, 0))
    out = pl.BlockSpec((PW, step), lambda i: (0, i))
    return pl.pallas_call(
        fill_kernel,
        grid=(RH // step,),
        in_specs=[SMEM, rows, rows, rows],
        out_specs=[out, out],
        out_shape=[jax.ShapeDtypeStruct((PW, RH), F32)] * 2,
        compiler_params=params(),
        cost_estimate=cost(10**6, 15 * 10**6),
        name="fill",
    )(core, observed, estimate, mask)


def gram_parts(x_ref):
    hh = jnp.zeros((PW, PW), F32)
    hl = jnp.zeros((PW, PW), F32)
    for j in range(0, RH, CH):
        h, l = split(x_ref[:, j : j + CH])
        hh += mxu(h, h, NT)
        hl += mxu(h, l, NT)
    return hh, hl


def gram_first_kernel(x_ref, hh_ref, hl_ref):
    hh_ref[...], hl_ref[...] = gram_parts(x_ref)


def gram_second_kernel(x_ref, hh_ref, hl_ref, out_ref):
    hh, hl = gram_parts(x_ref)
    hl += hl_ref[...]
    g = hh + hh_ref[...] + (hl + hl.T)
    out_ref[0:BW] = g[:BW, :BW]
    out_ref[BW : 2 * BW] = g[:BW, BW:]
    out_ref[2 * BW : 3 * BW] = g[BW:, BW:]


def gram_cross_kernel(k_ref, m_ref, out_ref):
    total = jnp.zeros((PW, PW), F32)
    for half in range(2):
        for j in range(0, RH, CH):
            ka = half * RH + j
            ma = (1 - half) * RH + j
            k = jnp.concatenate(split(k_ref[:, ka : ka + CH]), axis=0)
            m = jnp.concatenate(split(m_ref[:, ma : ma + CH]), axis=0)
            total += mxu(k, m, NT)
    out_ref[...] = (total[:BW, :BW] + total[BW:, BW:]) + (total[:BW, BW:] + total[BW:, :BW])


def gram_first(x):
    return pl.pallas_call(
        gram_first_kernel,
        in_specs=[VMEM],
        out_specs=[VMEM] * 2,
        out_shape=[jax.ShapeDtypeStruct((PW, PW), F32)] * 2,
        compiler_params=params(),
        cost_estimate=cost(4 * RH * PW * PW, 3 * 10**6),
        name="gram_first",
    )(x)


def gram_second(x, hh, hl):
    return pl.pallas_call(
        gram_second_kernel,
        in_specs=[VMEM] * 3,
        out_specs=VMEM,
        out_shape=jax.ShapeDtypeStruct((3 * BW, BW), F32),
        compiler_params=params(),
        cost_estimate=cost(4 * RH * PW * PW, 3 * 10**6),
        name="gram_second",
    )(x, hh, hl)


def gram_cross(k, m):
    return pl.pallas_call(
        gram_cross_kernel,
        in_specs=[VMEM] * 2,
        out_specs=VMEM,
        out_shape=jax.ShapeDtypeStruct((BW, BW), F32),
        compiler_params=params(),
        cost_estimate=cost(4 * RH * PW * PW, 3 * 10**6),
        name="gram_cross",
    )(k, m)


def newton(gram):
    at_row = lax.broadcasted_iota(jnp.int32, (PW, PW), 0)
    at_col = lax.broadcasted_iota(jnp.int32, (PW, PW), 1)
    on = at_row == at_col
    diag = jnp.where(on, gram, 0.0)
    d_col = jnp.sum(diag, axis=1, keepdims=True) + 1e-06
    d_row = jnp.sum(diag, axis=0, keepdims=True) + 1e-06
    inv_col = 1.0 / jnp.sqrt(d_col)
    inv_row = 1.0 / jnp.sqrt(d_row)
    normed = gram * inv_col * inv_row
    fro = jnp.sqrt(jnp.sum(jnp.sum(normed * normed, axis=1, keepdims=True), axis=0, keepdims=True))
    y = normed / fro
    three = jnp.where(on, 1.5, 0.0)
    t = three - 0.5 * y
    ts = split(t)
    y = dot3(split(y), ts)
    z, zs = t, ts
    ys = split(y)
    t = three - 0.5 * dot3(zs, ys)
    ts = split(t)
    y = dot3(ys, ts)
    z = dot3(ts, zs)
    ys, zs = split(y), split(z)
    t = three - 0.5 * dot3(zs, ys)
    ts = split(t)
    z = dot3(ts, zs)
    return z, y, t, d_col, d_row, inv_row, fro


def gram_of(g_refs, diag_refs):
    total = (g_refs[0][...] + g_refs[1][...]) + (g_refs[2][...] + g_refs[3][...])
    if diag_refs:
        d0, cross, d1 = diag_refs[0][...], total, diag_refs[1][...]
    else:
        d0, cross, d1 = total[:BW], total[BW : 2 * BW], total[2 * BW :]
    top = jnp.concatenate([d0, cross], axis=1)
    bottom = jnp.concatenate([cross.T, d1], axis=1)
    return jnp.concatenate([top, bottom], axis=0)


def columns(x_refs, first, half, j):
    if first:
        return x_refs[half][:, j : j + CH]
    ka = half * RH + j
    ma = (1 - half) * RH + j
    return jnp.concatenate([x_refs[0][:, ka : ka + CH], x_refs[1][:, ma : ma + CH]], axis=0)


def apply_to(w, x_refs, first, out_ref, offset=None):
    wh, wl = split(w)
    both = jnp.concatenate([wh, wl], axis=0)
    for half in range(2):
        for j in range(0, RH, CH):
            xh, xl = split(columns(x_refs, first, half, j))
            wide = mxu(both, xh)
            value = wide[:BW] + (wide[BW:] + mxu(wh, xl))
            if offset is None:
                out_ref[:, half * RH + j : half * RH + j + CH] = value
            else:
                at = pl.multiple_of((offset if half == 0 else RH - offset) + j, 128)
                out_ref[:, pl.ds(at, CH)] = value


def whiten_kernel(first, *refs):
    n = 4 if first else 6
    g_refs, diag_refs = refs[:4], refs[4:n]
    x_refs = refs[n : n + 2]
    moved_ref, w_ref, z_ref, y_ref, t_ref, d_ref = refs[n + 2 :]
    z, y, t, d_col, d_row, inv_row, fro = newton(gram_of(g_refs, diag_refs))
    wt = jnp.sqrt(d_col) * z.T * (inv_row / jnp.sqrt(fro))
    apply_to(wt[BW:], x_refs, first, moved_ref)
    w_ref[...] = wt[:BW]
    z_ref[...] = z
    y_ref[...] = y
    t_ref[...] = t
    root = jnp.sqrt(d_col) * jnp.sqrt(d_row)
    d_ref[...] = jnp.concatenate([root[:BW, :BW], root[BW:, BW:]], axis=0)


def whiten(grams, diags, xs, first):
    args = [*grams, *diags, *xs]
    return pl.pallas_call(
        functools.partial(whiten_kernel, first),
        in_specs=[VMEM] * len(args),
        out_specs=[VMEM] * 6,
        out_shape=[
            jax.ShapeDtypeStruct((BW, RB), F32),
            jax.ShapeDtypeStruct((BW, PW), F32),
            jax.ShapeDtypeStruct((PW, PW), F32),
            jax.ShapeDtypeStruct((PW, PW), F32),
            jax.ShapeDtypeStruct((PW, PW), F32),
            jax.ShapeDtypeStruct((PW, BW), F32),
        ],
        compiler_params=params(),
        cost_estimate=cost(10**9, 6 * 10**6),
        name="whiten",
    )(*args)


def kept_kernel(first, *refs):
    w_ref, z_ref, y_ref, t_ref, d_ref = refs[:5]
    x_refs = refs[5:7]
    kept_ref, kept_diag_ref, moved_diag_ref = refs[7:]
    zs = split(z_ref[...])
    ys = split(dot3(split(y_ref[...]), split(t_ref[...])))
    new = dot3(ys, zs)
    kept_diag_ref[...] = new[:BW, :BW] * d_ref[:BW]
    moved_diag_ref[...] = new[BW:, BW:] * d_ref[BW:]
    apply_to(w_ref[...], x_refs, first, kept_ref)


def kept_part(w, z, y, t, d, xs, first):
    return pl.pallas_call(
        functools.partial(kept_kernel, first),
        in_specs=[VMEM] * 7,
        out_specs=[VMEM] * 3,
        out_shape=[
            jax.ShapeDtypeStruct((BW, RB), F32),
            jax.ShapeDtypeStruct((BW, BW), F32),
            jax.ShapeDtypeStruct((BW, BW), F32),
        ],
        compiler_params=params(),
        cost_estimate=cost(10**9, 6 * 10**6),
        name="kept",
    )(w, z, y, t, d, *xs)


def by_core(w, even):
    parts = [w[i : i + 32] for i in range(0, PW, 32)]
    evens = jnp.concatenate(parts[0::2], axis=0)
    odds = jnp.concatenate(parts[1::2], axis=0)
    return jnp.where(even, evens, odds)


def last_kernel(core_ref, thr_ref, *refs):
    g_refs, diag_refs, x_refs = refs[:4], refs[4:6], refs[6:8]
    send_ref, w_ref = refs[8:]
    core = core_ref[0]
    z, y, t, d_col, d_row, inv_row, fro = newton(gram_of(g_refs, diag_refs))
    y = dot3(split(y), split(t))
    norm = jnp.sqrt(d_col * jnp.sum(z * y, axis=1, keepdims=True) + 1e-06)
    at_row = lax.broadcasted_iota(jnp.int32, (PW, PW), 0)
    at_col = lax.broadcasted_iota(jnp.int32, (PW, PW), 1)
    thr_row = jnp.where(core == 0, thr_ref[:, :PW], thr_ref[:, PW:])
    thr = jnp.sum(jnp.where(at_row == at_col, thr_row, 0.0), axis=1, keepdims=True)
    factor = jnp.maximum(norm - thr, 0.0) / norm
    wt = (factor * jnp.sqrt(d_col)) * z.T * (inv_row / jnp.sqrt(fro))
    apply_to(by_core(wt, core != 0), x_refs, False, send_ref, core * RH)
    w_ref[...] = by_core(wt, core == 0)


def last(core, thr, grams, diags, xs):
    return pl.pallas_call(
        last_kernel,
        in_specs=[SMEM] + [VMEM] * 9,
        out_specs=[VMEM] * 2,
        out_shape=[jax.ShapeDtypeStruct((BW, RB), F32), jax.ShapeDtypeStruct((BW, PW), F32)],
        compiler_params=params(),
        cost_estimate=cost(10**9, 6 * 10**6),
        name="last",
    )(core, thr, *grams, *diags, *xs)


def last_kept_kernel(core_ref, w_ref, k_ref, m_ref, out_ref):
    apply_to(w_ref[...], (k_ref, m_ref), False, out_ref, core_ref[0] * RH)


def last_kept(core, w, xs):
    return pl.pallas_call(
        last_kept_kernel,
        in_specs=[SMEM] + [VMEM] * 3,
        out_specs=VMEM,
        out_shape=jax.ShapeDtypeStruct((BW, RB), F32),
        compiler_params=params(),
        cost_estimate=cost(10**9, 6 * 10**6),
        name="last_kept",
    )(core, w, *xs)


def to(block, where):
    route = []
    for i in range(8):
        for c in range(2):
            for g in range(8):
                ti, tc, tg = where(i, c, g)
                route.append(((i * 2 + c) * 8 + g, (ti * 2 + tc) * 8 + tg))
    return lax.ppermute(block, AXES, route)


def swap_cores(block):
    return to(block, lambda i, c, g: (i, 1 - c, g))


def onward(block):
    return to(block, lambda i, c, g: (i, 1, g) if c == 0 else (i, 0, (g + 1) % 8))


def reduced(partial):
    pair = partial + to(partial, lambda i, c, g: (i ^ 1, c, g))
    return [pair] + [to(pair, lambda i, c, g, k=k: (i ^ k, c, g)) for k in (2, 4, 6)]


def on_device(observed, estimate, mask, threshold):
    core_index = lax.axis_index("core")
    core = core_index.reshape(1).astype(jnp.int32)
    thr = threshold.reshape(1, -1)
    keep, send = fill(core, observed, estimate, mask)
    got = swap_cores(send)
    grams = reduced(gram_second(got, *gram_first(keep)))
    xs, diags = (keep, got), []
    for round_index in range(ROUNDS - 1):
        first = round_index == 0
        moved, *rest = whiten(grams, diags, xs, first)
        arrived = onward(moved)
        kept, kept_diag, moved_diag = kept_part(*rest, xs, first)
        diags = [kept_diag, onward(moved_diag)]
        xs = (kept, arrived)
        grams = reduced(gram_cross(*xs))
    send, w = last(core, thr, grams, diags, xs)
    got = swap_cores(send)
    keep = last_kept(core, w, xs)
    low = jnp.where(core_index == 0, keep, got)
    high = jnp.where(core_index == 0, got, keep)
    packed = jnp.concatenate([low, high], axis=0).reshape(64, 4, RB)
    landed = lax.all_to_all(packed, ("zx", "pairs"), split_axis=0, concat_axis=0, tiled=True)
    landed = landed.reshape(8, 8, 4, RB).transpose(2, 1, 0, 3)
    return landed.reshape(32, 8 * RB)


def solution(mesh):
    finer = Mesh(mesh.devices.reshape(8, 2, 8), AXES)
    placed = P(("zx", "core"), "pairs")
    return jax.shard_map(
        on_device,
        mesh=finer,
        in_specs=(placed, placed, placed, P("pairs")),
        out_specs=P(AXES, None),
        check_vma=False,
    )
```

time: 819 us -> 221 us (0.27)
  waiting for transfers between devices: 525 us -> 107 us
  local copies, waits for them, and re-layouts: 91.1 us -> 9.41 us
  matrix products: 75.5 us -> 0 us
  blocking collectives: 79.1 us -> 49.7 us
  Pallas kernels: 0 us -> 24.7 us
  starting transfers between devices: 5.64 us -> 26.9 us
  other arithmetic: 20.6 us -> 2 us
  between operations: 13.9 us -> 0.17 us
    psum x4 -> x0, waiting for transfers between devices: 462 us -> none  [on_device(): gram = lax.psum(partial_gram, 'rows')]
    dot_general x40 -> x0, matrix products: 75.5 us -> none  [the longest x4 17.7 us: on_device(): partial_gram = jnp.einsum('rpi,rpj->pij', pairs, pairs, precision=HI)]
    psum x4 -> x0, local copies, waits for them, and re-layouts: 69.3 us -> none  [on_device(): gram = lax.psum(partial_gram, 'rows')]
    ppermute x3 -> x24, waiting for transfers between devices: 63.6 us -> 107 us  [to(): return lax.ppermute(block, AXES, route)]
    psum x1 -> x0, blocking collectives: 30.7 us -> none  [on_device(): squares = lax.psum(jnp.sum(filled * filled, axis=0), 'rows')]
    pallas_call x0 -> x14, Pallas kernels: none -> 24.7 us  [the longest x3 8.37 us: whiten(): pl.pallas_call(functools.partial(whiten_kernel, first), in_specs=[VMEM] *...]
    ppermute x3 -> x24, starting transfers between devices: 5.05 us -> 26.9 us  [to(): return lax.ppermute(block, AXES, route)]
    gather x4 -> x0, local copies, waits for them, and re-layouts: 11.9 us -> none  [whitening_of(): dsum = jnp.diagonal(gram, axis1=-2, axis2=-1) + 1e-06]
  transfers between devices with their start and end apart: 7 -> 24, of which waited for: 7 -> 18; matrix products, arithmetic and copies ran while one was open for 0% -> 0% of each run, Pallas kernels for 0% -> 2%
where the time goes in v1:
time: 221 us; the launch traced here: 220 us
  waiting for transfers between devices  107 us (48%)
  blocking collectives  49.7 us (22%)
  starting transfers between devices  26.9 us (12%)
  Pallas kernels  24.7 us (11%)
  local copies, waits for them, and re-layouts  9.41 us (4%)
    ppermute x24, waiting for transfers between devices, to(): return lax.ppermute(block, AXES, route)  107 us
    all_to_all x1, blocking collectives, on_device(): lax.all_to_all(packed, ('zx', 'pairs'), split_axis=0, concat_axis=0, tile...  49.7 us
    ppermute x24, starting transfers between devices, to(): return lax.ppermute(block, AXES, route)  26.9 us
    pallas_call x3, Pallas kernels, whiten(): pl.pallas_call(functools.partial(whiten_kernel, first), in_specs=[VMEM] *...  8.37 us
  transfers between devices with their start and end apart: 24, of which 18 were waited for; matrix products, arithmetic and copies ran while one was open for 0% of the time, Pallas kernels for 2%

profile of v1, /device:TPU:0, one launch (start us, length us, event | category | flops | bytes accessed | tf_op | source)
XLA Modules:
  0.0 220.3 jit_solution(5098344861320275669)
XLA Ops:
  0.0 1.9 copy-done
  1.9 1.9 copy-done.1
  3.8 4.2 %fill.1 = (f32[256,1536]{1,0:T(8,128)S(1)}, f32[256,1536]{1,0:T(8,128)S(1)}) custom-call(s32[1]{0:T(128)} %bitcast.core_ref, f32[1536,512]{1,0:T(8,128)S(1)} %copy-done, f32[1536,512]{1,0:T(8,128)S(1)} %copy-done.1, s32[1536,512]{1,0:T(8,128)} %mask_ref.1), custom_call_target="tpu_custom_call" | custom-call | flops 1000000 | bytes 15000000 | tf_op jit(solution)/shard_map/fill/pallas_call | solution.py:60
  7.9 0.1 collective-permute-start
  8.0 0.6 gram_first.1
  8.6 2.8 %collective-permute-done.x_ref.refs_5_.refs_6_ = f32[256,1536]{1,0:T(8,128)S(1)} collective-permute-done((f32[256,1536]{1,0:T(8,128)S(1)}, f32[256,1536]{1,0:T(8,128)S(1)}, u32[]{:S(2)}, u32[]{:S(2)}) %collective-permute-start) | collective-permute-done | bytes 1572896 | tf_op jit(solution)/shard_map/ppermute | solution.py:329
  11.4 0.7 gram_second.1
  12.1 1.7 collective-permute-start.1
  13.8 5.4 %collective-permute-done.1 = f32[384,128]{1,0:T(8,128)S(1)} collective-permute-done((f32[384,128]{1,0:T(8,128)S(1)}, f32[384,128]{1,0:T(8,128)S(1)}, u32[]{:S(2)}, u32[]{:S(2)}) %collective-permute-start.1) | collective-permute-done | bytes 196640 | tf_op jit(solution)/shard_map/ppermute | solution.py:329
  19.2 2.1 collective-permute-start.2
  21.3 3.6 %collective-permute-start.3 = (f32[384,128]{1,0:T(8,128)S(1)}, f32[384,128]{1,0:T(8,128)S(1)}, u32[]{:S(2)}, u32[]{:S(2)}) collective-permute-start(f32[384,128]{1,0:T(8,128)S(1)} %add.12.refs_0_), channel_id=1, source_target_pairs={{0,64},{1,65},{2,66},{3,67},{4,68},{5,69},{6,70},{7,71},{8,72},{9,... | collective-permute-start | bytes 589832 | tf_op jit(solution)/shard_map/ppermute | solution.py:329
  24.8 0.0 collective-permute-start.4
  24.8 2.1 collective-permute-done.2.refs_1_
  26.9 6.3 %collective-permute-done.3.refs_2_ = f32[384,128]{1,0:T(8,128)S(1)} collective-permute-done((f32[384,128]{1,0:T(8,128)S(1)}, f32[384,128]{1,0:T(8,128)S(1)}, u32[]{:S(2)}, u32[]{:S(2)}) %collective-permute-start.3) | collective-permute-done | bytes 196640 | tf_op jit(solution)/shard_map/ppermute | solution.py:329
  33.2 2.5 %collective-permute-done.4.refs_3_ = f32[384,128]{1,0:T(8,128)S(1)} collective-permute-done((f32[384,128]{1,0:T(8,128)S(1)}, f32[384,128]{1,0:T(8,128)S(1)}, u32[]{:S(2)}, u32[]{:S(2)}) %collective-permute-start.4) | collective-permute-done | bytes 196640 | tf_op jit(solution)/shard_map/ppermute | solution.py:329
  35.7 2.8 %whiten.3 = (f32[128,3072]{1,0:T(8,128)S(1)}, f32[128,256]{1,0:T(8,128)S(1)}, f32[256,256]{1,0:T(8,128)S(1)}, f32[256,256]{1,0:T(8,128)S(1)}, f32[256,256]{1,0:T(8,128)S(1)}, /*index=5*/f32[256,128]{1,0:T(8,128)S(1)}) custom-call(f32[384,128]{1,0:T(8,128)S(1)} %add.12.refs_0_, f32[384,128]{1,0:T(8,128)S(1)} %collective-permute-done.2.refs_1_, ...), custom_call_target="tpu_custom_call" | custom-call | flops 1000000000 | bytes 6000000 | tf_op jit(solution)/shard_map/whiten/pallas_call | solution.py:224
  38.5 0.1 collective-permute-start.5
  38.6 1.2 kept.3
  39.8 22.2 %collective-permute-done.5.m_ref.refs_7_.refs_6_ = f32[128,3072]{1,0:T(8,128)S(1)} collective-permute-done((f32[128,3072]{1,0:T(8,128)S(1)}, f32[128,3072]{1,0:T(8,128)S(1)}, u32[]{:S(2)}, u32[]{:S(2)}) %collective-permute-start.5) | collective-permute-done | bytes 1572896 | tf_op jit(solution)/shard_map/ppermute | solution.py:329
  62.0 0.7 gram_cross.3
  62.7 1.6 collective-permute-start.6
  64.3 2.8 %collective-permute-done.6 = f32[128,128]{1,0:T(8,128)S(1)} collective-permute-done((f32[128,128]{1,0:T(8,128)S(1)}, f32[128,128]{1,0:T(8,128)S(1)}, u32[]{:S(2)}, u32[]{:S(2)}) %collective-permute-start.6) | collective-permute-done | bytes 65568 | tf_op jit(solution)/shard_map/ppermute | solution.py:329
  67.1 0.1 collective-permute-start.7
  67.2 1.5 collective-permute-start.8
  68.7 3.2 %collective-permute-start.9 = (f32[128,128]{1,0:T(8,128)S(1)}, f32[128,128]{1,0:T(8,128)S(1)}, u32[]{:S(2)}, u32[]{:S(2)}) collective-permute-start(f32[128,128]{1,0:T(8,128)S(1)} %add.13.refs_0_), channel_id=1, source_target_pairs={{0,96},{1,97},{2,98},{3,99},{4,100},{5,101},{6,102},{7,103},{8,104... | collective-permute-start | bytes 196616 | tf_op jit(solution)/shard_map/ppermute | solution.py:329
  71.9 0.0 collective-permute-done.10.refs_5_
  71.9 1.2 collective-permute-done.8.refs_2_
  73.0 1.1 collective-permute-done.9.refs_3_
  74.1 2.8 %whiten.4 = (f32[128,3072]{1,0:T(8,128)S(1)}, f32[128,256]{1,0:T(8,128)S(1)}, f32[256,256]{1,0:T(8,128)S(1)}, f32[256,256]{1,0:T(8,128)S(1)}, f32[256,256]{1,0:T(8,128)S(1)}, /*index=5*/f32[256,128]{1,0:T(8,128)S(1)}) custom-call(f32[128,128]{1,0:T(8,128)S(1)} %add.13.refs_0_, f32[128,128]{1,0:T(8,128)S(1)} %collective-permute-done.7.refs_1_, ...), custom_call_target="tpu_custom_call" | custom-call | flops 1000000000 | bytes 6000000 | tf_op jit(solution)/shard_map/whiten/pallas_call | solution.py:224
  76.9 0.3 collective-permute-start.11
  77.2 1.2 kept.4
  78.4 22.2 %collective-permute-done.11.m_ref.refs_7_.refs_6_ = f32[128,3072]{1,0:T(8,128)S(1)} collective-permute-done((f32[128,3072]{1,0:T(8,128)S(1)}, f32[128,3072]{1,0:T(8,128)S(1)}, u32[]{:S(2)}, u32[]{:S(2)}) %collective-permute-start.11) | collective-permute-done | bytes 1572896 | tf_op jit(solution)/shard_map/ppermute | solution.py:329
  100.6 0.7 gram_cross.4
  101.3 1.6 collective-permute-start.12
  102.9 0.0 collective-permute-start.16
  102.9 2.8 %collective-permute-done.12 = f32[128,128]{1,0:T(8,128)S(1)} collective-permute-done((f32[128,128]{1,0:T(8,128)S(1)}, f32[128,128]{1,0:T(8,128)S(1)}, u32[]{:S(2)}, u32[]{:S(2)}) %collective-permute-start.12) | collective-permute-done | bytes 65568 | tf_op jit(solution)/shard_map/ppermute | solution.py:329
  105.7 0.9 collective-permute-start.13
  106.6 3.8 %collective-permute-start.14 = (f32[128,128]{1,0:T(8,128)S(1)}, f32[128,128]{1,0:T(8,128)S(1)}, u32[]{:S(2)}, u32[]{:S(2)}) collective-permute-start(f32[128,128]{1,0:T(8,128)S(1)} %add.14.refs_0_), channel_id=1, source_target_pairs={{0,64},{1,65},{2,66},{3,67},{4,68},{5,69},{6,70},{7,71},{8,72},{9,... | collective-permute-start | bytes 196616 | tf_op jit(solution)/shard_map/ppermute | solution.py:329
  110.5 0.0 collective-permute-start.15
  110.5 0.0 collective-permute-done.16.refs_5_
  110.5 0.0 collective-permute-done.13.refs_1_
  110.5 2.9 %collective-permute-done.14.refs_2_ = f32[128,128]{1,0:T(8,128)S(1)} collective-permute-done((f32[128,128]{1,0:T(8,128)S(1)}, f32[128,128]{1,0:T(8,128)S(1)}, u32[]{:S(2)}, u32[]{:S(2)}) %collective-permute-start.14) | collective-permute-done | bytes 65568 | tf_op jit(solution)/shard_map/ppermute | solution.py:329
  113.4 2.5 %collective-permute-done.15.refs_3_ = f32[128,128]{1,0:T(8,128)S(1)} collective-permute-done((f32[128,128]{1,0:T(8,128)S(1)}, f32[128,128]{1,0:T(8,128)S(1)}, u32[]{:S(2)}, u32[]{:S(2)}) %collective-permute-start.15) | collective-permute-done | bytes 65568 | tf_op jit(solution)/shard_map/ppermute | solution.py:329
  115.9 2.8 %whiten.5 = (f32[128,3072]{1,0:T(8,128)S(1)}, f32[128,256]{1,0:T(8,128)S(1)}, f32[256,256]{1,0:T(8,128)S(1)}, f32[256,256]{1,0:T(8,128)S(1)}, f32[256,256]{1,0:T(8,128)S(1)}, /*index=5*/f32[256,128]{1,0:T(8,128)S(1)}) custom-call(f32[128,128]{1,0:T(8,128)S(1)} %add.14.refs_0_, f32[128,128]{1,0:T(8,128)S(1)} %collective-permute-done.13.refs_1_, ...), custom_call_target="tpu_custom_call" | custom-call | flops 1000000000 | bytes 6000000 | tf_op jit(solution)/shard_map/whiten/pallas_call | solution.py:224
  118.7 0.1 collective-permute-start.17
  118.8 1.3 kept.5
  120.1 22.9 %collective-permute-done.17.m_ref.refs_7_ = f32[128,3072]{1,0:T(8,128)S(1)} collective-permute-done((f32[128,3072]{1,0:T(8,128)S(1)}, f32[128,3072]{1,0:T(8,128)S(1)}, u32[]{:S(2)}, u32[]{:S(2)}) %collective-permute-start.17) | collective-permute-done | bytes 1572896 | tf_op jit(solution)/shard_map/ppermute | solution.py:329
  143.0 0.7 gram_cross.5
  143.7 1.6 collective-permute-start.18
  145.3 2.8 %collective-permute-done.18 = f32[128,128]{1,0:T(8,128)S(1)} collective-permute-done((f32[128,128]{1,0:T(8,128)S(1)}, f32[128,128]{1,0:T(8,128)S(1)}, u32[]{:S(2)}, u32[]{:S(2)}) %collective-permute-start.18) | collective-permute-done | bytes 65568 | tf_op jit(solution)/shard_map/ppermute | solution.py:329
  148.1 0.1 collective-permute-start.19
  148.2 1.1 collective-permute-start.20
  149.2 3.6 %collective-permute-start.21 = (f32[128,128]{1,0:T(8,128)S(1)}, f32[128,128]{1,0:T(8,128)S(1)}, u32[]{:S(2)}, u32[]{:S(2)}) collective-permute-start(f32[128,128]{1,0:T(8,128)S(1)} %add.15.refs_0_), channel_id=1, source_target_pairs={{0,96},{1,97},{2,98},{3,99},{4,100},{5,101},{6,102},{7,103},{8,104... | collective-permute-start | bytes 196616 | tf_op jit(solution)/shard_map/ppermute | solution.py:329
  152.8 1.2 collective-permute-done.20.refs_2_
  154.0 1.1 collective-permute-done.21.refs_3_
  155.1 4.2 %last.1 = (f32[128,3072]{1,0:T(8,128)}, f32[128,256]{1,0:T(8,128)S(1)}) custom-call(s32[1]{0:T(128)} %bitcast.core_ref, f32[1,512]{1,0:T(1,128)S(1)} %bitcast.6, f32[128,128]{1,0:T(8,128)S(1)} %add.15.refs_0_, f32[128,128]{1,0:T(8,128)S(1)} %collective-permute-done.19.refs_1_, f32[128,128]{1,0:T(8,128)S(1)} %collective-permute-done.20.refs_2_, ...), custom_call_target="tpu_custom_call" | custom-call | flops 1000000000 | bytes 6000000 | tf_op jit(solution)/shard_map/last/pallas_call | solution.py:295
  159.3 0.0 collective-permute-start.23
  159.3 0.8 last_kept.1
  160.1 2.9 %collective-permute-done.23 = f32[128,3072]{1,0:T(8,128)} collective-permute-done((f32[128,3072]{1,0:T(8,128)}, f32[128,3072]{1,0:T(8,128)}, u32[]{:S(2)}, u32[]{:S(2)}) %collective-permute-start.23) | collective-permute-done | bytes 1572896 | tf_op jit(solution)/shard_map/ppermute | solution.py:329
  163.0 1.7 broadcast_select_fusion.1
  164.8 0.2 pad_maximum_fusion
  165.0 2.1 reshape.17
  167.1 49.7 %all_to_all.5 = f32[64,4,3072]{2,1,0:T(4,128)S(1)} all-to-all(f32[64,4,3072]{2,1,0:T(4,128)} %reshape.17), channel_id=1, replica_groups=mesh['zx'=8,'core'=2,'pairs'=8] {'zx','pairs'}, dimensions={0} | all-to-all | bytes 6291456 | tf_op jit(solution)/shard_map/all_to_all | solution.py:367
  216.8 3.5 %copy.5 = f32[8,8,4,3072]{3,1,0,2:T(8,128)} copy(f32[8,8,4,3072]{3,2,1,0:T(4,128)S(1)} %bitcast.7) | data formatting | bytes 6291456 | tf_op jit(solution)/shard_map/reshape | solution.py:368
  (13 shorter events, 0.1 us)
Async XLA Ops:
  0.0 1.9 copy-start
  1.9 1.9 copy-start.1
  7.9 3.5 %collective-permute-start = (f32[256,1536]{1,0:T(8,128)S(1)}, f32[256,1536]{1,0:T(8,128)S(1)}, u32[]{:S(2)}, u32[]{:S(2)}) collective-permute-start(f32[256,1536]{1,0:T(8,128)S(1)} %get-tuple-element.38), channel_id=1, source_target_pairs={{0,8},{1,9},{2,10},{3,11},{4,12},{5,13},{6,14},{7,15},{8,0},{9,1},... | collective-permute-start | bytes 4718600 | tf_op jit(solution)/shard_map/ppermute | solution.py:329
  12.1 7.0 %collective-permute-start.1 = (f32[384,128]{1,0:T(8,128)S(1)}, f32[384,128]{1,0:T(8,128)S(1)}, u32[]{:S(2)}, u32[]{:S(2)}) collective-permute-start(f32[384,128]{1,0:T(8,128)S(1)} %gram_second.1), channel_id=1, source_target_pairs={{0,16},{1,17},{2,18},{3,19},{4,20},{5,21},{6,22},{7,23},{8,24},{9,... | collective-permute-start | bytes 589832 | tf_op jit(solution)/shard_map/ppermute | solution.py:329
  19.2 7.8 %collective-permute-start.2 = (f32[384,128]{1,0:T(8,128)S(1)}, f32[384,128]{1,0:T(8,128)S(1)}, u32[]{:S(2)}, u32[]{:S(2)}) collective-permute-start(f32[384,128]{1,0:T(8,128)S(1)} %add.12.refs_0_), channel_id=1, source_target_pairs={{0,32},{1,33},{2,34},{3,35},{4,36},{5,37},{6,38},{7,39},{8,40},{9,... | collective-permute-start | bytes 589832 | tf_op jit(solution)/shard_map/ppermute | solution.py:329
  21.3 12.0 %collective-permute-start.3 = (f32[384,128]{1,0:T(8,128)S(1)}, f32[384,128]{1,0:T(8,128)S(1)}, u32[]{:S(2)}, u32[]{:S(2)}) collective-permute-start(f32[384,128]{1,0:T(8,128)S(1)} %add.12.refs_0_), channel_id=1, source_target_pairs={{0,64},{1,65},{2,66},{3,67},{4,68},{5,69},{6,70},{7,71},{8,72},{9,... | collective-permute-start | bytes 589832 | tf_op jit(solution)/shard_map/ppermute | solution.py:329
  24.8 10.9 %collective-permute-start.4 = (f32[384,128]{1,0:T(8,128)S(1)}, f32[384,128]{1,0:T(8,128)S(1)}, u32[]{:S(2)}, u32[]{:S(2)}) collective-permute-start(f32[384,128]{1,0:T(8,128)S(1)} %add.12.refs_0_), channel_id=1, source_target_pairs={{0,96},{1,97},{2,98},{3,99},{4,100},{5,101},{6,102},{7,103},{8,104... | collective-permute-start | bytes 589832 | tf_op jit(solution)/shard_map/ppermute | solution.py:329
  38.5 23.5 %collective-permute-start.5 = (f32[128,3072]{1,0:T(8,128)S(1)}, f32[128,3072]{1,0:T(8,128)S(1)}, u32[]{:S(2)}, u32[]{:S(2)}) collective-permute-start(f32[128,3072]{1,0:T(8,128)S(1)} %get-tuple-element.48), channel_id=1, source_target_pairs={{0,8},{1,9},{2,10},{3,11},{4,12},{5,13},{6,14},{7,15},{8,1},{9,2},... | collective-permute-start | bytes 4718600 | tf_op jit(solution)/shard_map/ppermute | solution.py:329
  62.7 4.3 %collective-permute-start.6 = (f32[128,128]{1,0:T(8,128)S(1)}, f32[128,128]{1,0:T(8,128)S(1)}, u32[]{:S(2)}, u32[]{:S(2)}) collective-permute-start(f32[128,128]{1,0:T(8,128)S(1)} %gram_cross.3), channel_id=1, source_target_pairs={{0,16},{1,17},{2,18},{3,19},{4,20},{5,21},{6,22},{7,23},{8,24},{9,... | collective-permute-start | bytes 196616 | tf_op jit(solution)/shard_map/ppermute | solution.py:329
  64.3 7.6 %collective-permute-start.10 = (f32[128,128]{1,0:T(8,128)S(1)}, f32[128,128]{1,0:T(8,128)S(1)}, u32[]{:S(2)}, u32[]{:S(2)}) collective-permute-start(f32[128,128]{1,0:T(8,128)S(1)} %get-tuple-element.50), channel_id=1, source_target_pairs={{0,8},{1,9},{2,10},{3,11},{4,12},{5,13},{6,14},{7,15},{8,1},{9,2},... | collective-permute-start | bytes 196616 | tf_op jit(solution)/shard_map/ppermute | solution.py:329
  67.1 4.8 %collective-permute-start.7 = (f32[128,128]{1,0:T(8,128)S(1)}, f32[128,128]{1,0:T(8,128)S(1)}, u32[]{:S(2)}, u32[]{:S(2)}) collective-permute-start(f32[128,128]{1,0:T(8,128)S(1)} %add.13.refs_0_), channel_id=1, source_target_pairs={{0,32},{1,33},{2,34},{3,35},{4,36},{5,37},{6,38},{7,39},{8,40},{9,... | collective-permute-start | bytes 196616 | tf_op jit(solution)/shard_map/ppermute | solution.py:329
  67.2 5.8 %collective-permute-start.8 = (f32[128,128]{1,0:T(8,128)S(1)}, f32[128,128]{1,0:T(8,128)S(1)}, u32[]{:S(2)}, u32[]{:S(2)}) collective-permute-start(f32[128,128]{1,0:T(8,128)S(1)} %add.13.refs_0_), channel_id=1, source_target_pairs={{0,64},{1,65},{2,66},{3,67},{4,68},{5,69},{6,70},{7,71},{8,72},{9,... | collective-permute-start | bytes 196616 | tf_op jit(solution)/shard_map/ppermute | solution.py:329
  68.7 5.5 %collective-permute-start.9 = (f32[128,128]{1,0:T(8,128)S(1)}, f32[128,128]{1,0:T(8,128)S(1)}, u32[]{:S(2)}, u32[]{:S(2)}) collective-permute-start(f32[128,128]{1,0:T(8,128)S(1)} %add.13.refs_0_), channel_id=1, source_target_pairs={{0,96},{1,97},{2,98},{3,99},{4,100},{5,101},{6,102},{7,103},{8,104... | collective-permute-start | bytes 196616 | tf_op jit(solution)/shard_map/ppermute | solution.py:329
  76.9 23.7 %collective-permute-start.11 = (f32[128,3072]{1,0:T(8,128)S(1)}, f32[128,3072]{1,0:T(8,128)S(1)}, u32[]{:S(2)}, u32[]{:S(2)}) collective-permute-start(f32[128,3072]{1,0:T(8,128)S(1)} %get-tuple-element.57), channel_id=1, source_target_pairs={{0,8},{1,9},{2,10},{3,11},{4,12},{5,13},{6,14},{7,15},{8,1},{9,2},... | collective-permute-start | bytes 4718600 | tf_op jit(solution)/shard_map/ppermute | solution.py:329
  101.3 4.3 %collective-permute-start.12 = (f32[128,128]{1,0:T(8,128)S(1)}, f32[128,128]{1,0:T(8,128)S(1)}, u32[]{:S(2)}, u32[]{:S(2)}) collective-permute-start(f32[128,128]{1,0:T(8,128)S(1)} %gram_cross.4), channel_id=1, source_target_pairs={{0,16},{1,17},{2,18},{3,19},{4,20},{5,21},{6,22},{7,23},{8,24},{9,... | collective-permute-start | bytes 196616 | tf_op jit(solution)/shard_map/ppermute | solution.py:329
  102.9 7.6 %collective-permute-start.16 = (f32[128,128]{1,0:T(8,128)S(1)}, f32[128,128]{1,0:T(8,128)S(1)}, u32[]{:S(2)}, u32[]{:S(2)}) collective-permute-start(f32[128,128]{1,0:T(8,128)S(1)} %get-tuple-element.59), channel_id=1, source_target_pairs={{0,8},{1,9},{2,10},{3,11},{4,12},{5,13},{6,14},{7,15},{8,1},{9,2},... | collective-permute-start | bytes 196616 | tf_op jit(solution)/shard_map/ppermute | solution.py:329
  105.7 4.8 %collective-permute-start.13 = (f32[128,128]{1,0:T(8,128)S(1)}, f32[128,128]{1,0:T(8,128)S(1)}, u32[]{:S(2)}, u32[]{:S(2)}) collective-permute-start(f32[128,128]{1,0:T(8,128)S(1)} %add.14.refs_0_), channel_id=1, source_target_pairs={{0,32},{1,33},{2,34},{3,35},{4,36},{5,37},{6,38},{7,39},{8,40},{9,... | collective-permute-start | bytes 196616 | tf_op jit(solution)/shard_map/ppermute | solution.py:329
  106.6 6.8 %collective-permute-start.14 = (f32[128,128]{1,0:T(8,128)S(1)}, f32[128,128]{1,0:T(8,128)S(1)}, u32[]{:S(2)}, u32[]{:S(2)}) collective-permute-start(f32[128,128]{1,0:T(8,128)S(1)} %add.14.refs_0_), channel_id=1, source_target_pairs={{0,64},{1,65},{2,66},{3,67},{4,68},{5,69},{6,70},{7,71},{8,72},{9,... | collective-permute-start | bytes 196616 | tf_op jit(solution)/shard_map/ppermute | solution.py:329
  110.5 5.5 %collective-permute-start.15 = (f32[128,128]{1,0:T(8,128)S(1)}, f32[128,128]{1,0:T(8,128)S(1)}, u32[]{:S(2)}, u32[]{:S(2)}) collective-permute-start(f32[128,128]{1,0:T(8,128)S(1)} %add.14.refs_0_), channel_id=1, source_target_pairs={{0,96},{1,97},{2,98},{3,99},{4,100},{5,101},{6,102},{7,103},{8,104... | collective-permute-start | bytes 196616 | tf_op jit(solution)/shard_map/ppermute | solution.py:329
  118.7 24.2 %collective-permute-start.17 = (f32[128,3072]{1,0:T(8,128)S(1)}, f32[128,3072]{1,0:T(8,128)S(1)}, u32[]{:S(2)}, u32[]{:S(2)}) collective-permute-start(f32[128,3072]{1,0:T(8,128)S(1)} %get-tuple-element.66), channel_id=1, source_target_pairs={{0,8},{1,9},{2,10},{3,11},{4,12},{5,13},{6,14},{7,15},{8,1},{9,2},... | collective-permute-start | bytes 4718600 | tf_op jit(solution)/shard_map/ppermute | solution.py:329
  143.0 12.1 %copy-start.2 = (f32[512]{0:T(512)S(1)}, f32[512]{0:T(512)}, u32[]{:S(2)}) copy-start(f32[512]{0:T(512)} %param.7) | copy-start | bytes 6148
  143.7 4.3 %collective-permute-start.18 = (f32[128,128]{1,0:T(8,128)S(1)}, f32[128,128]{1,0:T(8,128)S(1)}, u32[]{:S(2)}, u32[]{:S(2)}) collective-permute-start(f32[128,128]{1,0:T(8,128)S(1)} %gram_cross.5), channel_id=1, source_target_pairs={{0,16},{1,17},{2,18},{3,19},{4,20},{5,21},{6,22},{7,23},{8,24},{9,... | collective-permute-start | bytes 196616 | tf_op jit(solution)/shard_map/ppermute | solution.py:329
  145.3 7.6 %collective-permute-start.22 = (f32[128,128]{1,0:T(8,128)S(1)}, f32[128,128]{1,0:T(8,128)S(1)}, u32[]{:S(2)}, u32[]{:S(2)}) collective-permute-start(f32[128,128]{1,0:T(8,128)S(1)} %get-tuple-element.68), channel_id=1, source_target_pairs={{0,8},{1,9},{2,10},{3,11},{4,12},{5,13},{6,14},{7,15},{8,1},{9,2},... | collective-permute-start | bytes 196616 | tf_op jit(solution)/shard_map/ppermute | solution.py:329
  148.1 4.8 %collective-permute-start.19 = (f32[128,128]{1,0:T(8,128)S(1)}, f32[128,128]{1,0:T(8,128)S(1)}, u32[]{:S(2)}, u32[]{:S(2)}) collective-permute-start(f32[128,128]{1,0:T(8,128)S(1)} %add.15.refs_0_), channel_id=1, source_target_pairs={{0,32},{1,33},{2,34},{3,35},{4,36},{5,37},{6,38},{7,39},{8,40},{9,... | collective-permute-start | bytes 196616 | tf_op jit(solution)/shard_map/ppermute | solution.py:329
  148.2 5.8 %collective-permute-start.20 = (f32[128,128]{1,0:T(8,128)S(1)}, f32[128,128]{1,0:T(8,128)S(1)}, u32[]{:S(2)}, u32[]{:S(2)}) collective-permute-start(f32[128,128]{1,0:T(8,128)S(1)} %add.15.refs_0_), channel_id=1, source_target_pairs={{0,64},{1,65},{2,66},{3,67},{4,68},{5,69},{6,70},{7,71},{8,72},{9,... | collective-permute-start | bytes 196616 | tf_op jit(solution)/shard_map/ppermute | solution.py:329
  149.2 5.8 %collective-permute-start.21 = (f32[128,128]{1,0:T(8,128)S(1)}, f32[128,128]{1,0:T(8,128)S(1)}, u32[]{:S(2)}, u32[]{:S(2)}) collective-permute-start(f32[128,128]{1,0:T(8,128)S(1)} %add.15.refs_0_), channel_id=1, source_target_pairs={{0,96},{1,97},{2,98},{3,99},{4,100},{5,101},{6,102},{7,103},{8,104... | collective-permute-start | bytes 196616 | tf_op jit(solution)/shard_map/ppermute | solution.py:329
  159.3 3.8 %collective-permute-start.23 = (f32[128,3072]{1,0:T(8,128)}, f32[128,3072]{1,0:T(8,128)}, u32[]{:S(2)}, u32[]{:S(2)}) collective-permute-start(f32[128,3072]{1,0:T(8,128)} %get-tuple-element.70), channel_id=1, source_target_pairs={{0,8},{1,9},{2,10},{3,11},{4,12},{5,13},{6,14},{7,15},{8,0},{9,1},... | collective-permute-start | bytes 4718600 | tf_op jit(solution)/shard_map/ppermute | solution.py:329

commit v2 on v1

--- a/solution.py
+++ b/solution.py
@@ -22,8 +22,8 @@
 NT = (((1,), (1,)), ((), ()))
 
 
-def params():
-    return pltpu.CompilerParams(vmem_limit_bytes=44 * 1024 * 1024)
+def params(mib=44):
+    return pltpu.CompilerParams(vmem_limit_bytes=mib * 1024 * 1024)
 
 
 def cost(flops, moved):
@@ -63,7 +63,7 @@
         in_specs=[SMEM, rows, rows, rows],
         out_specs=[out, out],
         out_shape=[jax.ShapeDtypeStruct((PW, RH), F32)] * 2,
-        compiler_params=params(),
+        compiler_params=params(60),
         cost_estimate=cost(10**6, 15 * 10**6),
         name="fill",
     )(core, observed, estimate, mask)
@@ -87,9 +87,13 @@
     hh, hl = gram_parts(x_ref)
     hl += hl_ref[...]
     g = hh + hh_ref[...] + (hl + hl.T)
-    out_ref[0:BW] = g[:BW, :BW]
-    out_ref[BW : 2 * BW] = g[:BW, BW:]
-    out_ref[2 * BW : 3 * BW] = g[BW:, BW:]
+    at_row = lax.broadcasted_iota(jnp.int32, (BW, BW), 0)
+    at_col = lax.broadcasted_iota(jnp.int32, (BW, BW), 1)
+    d0, d1 = g[:BW, :BW], g[BW:, BW:]
+    out_ref[0:BW] = g[:BW, BW:]
+    out_ref[BW : 2 * BW] = jnp.where(at_col > at_row, d0, d1)
+    on_diag = jnp.sum(jnp.where(at_col == at_row, d0, 0.0), axis=0, keepdims=True)
+    out_ref[2 * BW :] = jnp.broadcast_to(on_diag, (8, BW))
 
 
 def gram_cross_kernel(k_ref, m_ref, out_ref):
@@ -121,7 +125,7 @@
         gram_second_kernel,
         in_specs=[VMEM] * 3,
         out_specs=VMEM,
-        out_shape=jax.ShapeDtypeStruct((3 * BW, BW), F32),
+        out_shape=jax.ShapeDtypeStruct((2 * BW + 8, BW), F32),
         compiler_params=params(),
         cost_estimate=cost(4 * RH * PW * PW, 3 * 10**6),
         name="gram_second",
@@ -174,7 +178,12 @@
     if diag_refs:
         d0, cross, d1 = diag_refs[0][...], total, diag_refs[1][...]
     else:
-        d0, cross, d1 = total[:BW], total[BW : 2 * BW], total[2 * BW :]
+        cross, both, on_diag = total[:BW], total[BW : 2 * BW], total[2 * BW : 2 * BW + 1]
+        at_row = lax.broadcasted_iota(jnp.int32, (BW, BW), 0)
+        at_col = lax.broadcasted_iota(jnp.int32, (BW, BW), 1)
+        turned = both.T
+        d0 = jnp.where(at_col == at_row, on_diag, jnp.where(at_col > at_row, both, turned))
+        d1 = jnp.where(at_col > at_row, turned, both)
     top = jnp.concatenate([d0, cross], axis=1)
     bottom = jnp.concatenate([cross.T, d1], axis=1)
     return jnp.concatenate([top, bottom], axis=0)
@@ -303,20 +312,23 @@
     )(core, thr, *grams, *diags, *xs)
 
 
-def last_kept_kernel(core_ref, w_ref, k_ref, m_ref, out_ref):
-    apply_to(w_ref[...], (k_ref, m_ref), False, out_ref, core_ref[0] * RH)
-
-
-def last_kept(core, w, xs):
+def last_kept_kernel(core_ref, w_ref, k_ref, m_ref, got_ref, out_ref):
+    core = core_ref[0]
+    mine = pl.multiple_of(core * BW, BW)
+    apply_to(w_ref[...], (k_ref, m_ref), False, out_ref.at[pl.ds(mine, BW)], core * RH)
+    out_ref[pl.ds(pl.multiple_of(BW - mine, BW), BW)] = got_ref[...]
+
+
+def last_kept(core, w, xs, got):
     return pl.pallas_call(
         last_kept_kernel,
-        in_specs=[SMEM] + [VMEM] * 3,
+        in_specs=[SMEM] + [VMEM] * 4,
         out_specs=VMEM,
-        out_shape=jax.ShapeDtypeStruct((BW, RB), F32),
+        out_shape=jax.ShapeDtypeStruct((PW, RB), F32),
         compiler_params=params(),
         cost_estimate=cost(10**9, 6 * 10**6),
         name="last_kept",
-    )(core, w, *xs)
+    )(core, w, *xs, got)
 
 
 def to(block, where):
@@ -360,10 +372,7 @@
         grams = reduced(gram_cross(*xs))
     send, w = last(core, thr, grams, diags, xs)
     got = swap_cores(send)
-    keep = last_kept(core, w, xs)
-    low = jnp.where(core_index == 0, keep, got)
-    high = jnp.where(core_index == 0, got, keep)
-    packed = jnp.concatenate([low, high], axis=0).reshape(64, 4, RB)
+    packed = last_kept(core, w, xs, got).reshape(64, 4, RB)
     landed = lax.all_to_all(packed, ("zx", "pairs"), split_axis=0, concat_axis=0, tiled=True)
     landed = landed.reshape(8, 8, 4, RB).transpose(2, 1, 0, 3)
     return landed.reshape(32, 8 * RB)

time: 221 us -> 209 us (0.946)
  waiting for transfers between devices: 107 us -> 101 us
  local copies, waits for them, and re-layouts: 9.41 us -> 7.04 us
    ppermute x24, waiting for transfers between devices: 107 us -> 101 us  [to(): return lax.ppermute(block, AXES, route)]
    pallas_call x1, Pallas kernels: 4.15 us -> 6.71 us  [fill(): pl.pallas_call(fill_kernel, grid=(RH // step,), in_specs=[SMEM, rows, row...]
    unnamed x6, local copies, waits for them, and re-layouts: 3.78 us -> 1.42 us
  transfers between devices with their start and end apart: 24 -> 24, of which waited for: 18 -> 20; matrix products, arithmetic and copies ran while one was open for 0% -> 0% of each run, Pallas kernels for 2% -> 2%
where the time goes in v2:
time: 209 us; the launch traced here: 208 us
  waiting for transfers between devices  101 us (48%)
  blocking collectives  48.6 us (23%)
  Pallas kernels  26.4 us (13%)
  starting transfers between devices  25.5 us (12%)
  local copies, waits for them, and re-layouts  7.04 us (3%)
    ppermute x24, waiting for transfers between devices, to(): return lax.ppermute(block, AXES, route)  101 us
    all_to_all x1, blocking collectives, on_device(): lax.all_to_all(packed, ('zx', 'pairs'), split_axis=0, concat_axis=0, tile...  48.6 us
    ppermute x24, starting transfers between devices, to(): return lax.ppermute(block, AXES, route)  25.5 us
    pallas_call x3, Pallas kernels, whiten(): pl.pallas_call(functools.partial(whiten_kernel, first), in_specs=[VMEM] *...  8.44 us
    pallas_call x1, Pallas kernels, fill(): pl.pallas_call(fill_kernel, grid=(RH // step,), in_specs=[SMEM, rows, row...  6.71 us
  transfers between devices with their start and end apart: 24, of which 20 were waited for; matrix products, arithmetic and copies ran while one was open for 0% of the time, Pallas kernels for 2%

profile of v2, /device:TPU:0, one launch (start us, length us, event | category | flops | bytes accessed | tf_op | source)
XLA Modules:
  0.0 208.4 jit_solution(12383118396288820252)
XLA Ops:
  0.0 6.7 %fill.1 = (f32[256,1536]{1,0:T(8,128)}, f32[256,1536]{1,0:T(8,128)}) custom-call(s32[1]{0:T(128)} %bitcast.core_ref, f32[1536,512]{1,0:T(8,128)} %obs_ref.1, f32[1536,512]{1,0:T(8,128)} %est_ref.1, s32[1536,512]{1,0:T(8,128)} %mask_ref.1), custom_call_target="tpu_custom_call" | custom-call | flops 1000000 | bytes 15000000 | tf_op jit(solution)/shard_map/fill/pallas_call | solution.py:60
  6.7 0.0 collective-permute-start
  6.7 1.4 copy-done
  8.1 0.6 gram_first.1
  8.7 0.0 copy-start.1
  8.8 1.6 collective-permute-done.x_ref.refs_5_.refs_6_
  10.3 0.7 gram_second.1
  11.0 1.7 collective-permute-start.1
  12.7 4.0 %collective-permute-done.1 = f32[264,128]{1,0:T(8,128)S(1)} collective-permute-done((f32[264,128]{1,0:T(8,128)S(1)}, f32[264,128]{1,0:T(8,128)S(1)}, u32[]{:S(2)}, u32[]{:S(2)}) %collective-permute-start.1) | collective-permute-done | bytes 135200 | tf_op jit(solution)/shard_map/ppermute | solution.py:341
  16.8 4.2 %collective-permute-start.4 = (f32[264,128]{1,0:T(8,128)S(1)}, f32[264,128]{1,0:T(8,128)S(1)}, u32[]{:S(2)}, u32[]{:S(2)}) collective-permute-start(f32[264,128]{1,0:T(8,128)S(1)} %add.12.refs_0_), channel_id=1, source_target_pairs={{0,96},{1,97},{2,98},{3,99},{4,100},{5,101},{6,102},{7,103},{8,104... | collective-permute-start | bytes 405512 | tf_op jit(solution)/shard_map/ppermute | solution.py:341
  21.0 0.0 collective-permute-start.3
  21.0 0.9 collective-permute-start.2
  21.9 4.3 %collective-permute-done.4.refs_3_ = f32[264,128]{1,0:T(8,128)S(1)} collective-permute-done((f32[264,128]{1,0:T(8,128)S(1)}, f32[264,128]{1,0:T(8,128)S(1)}, u32[]{:S(2)}, u32[]{:S(2)}) %collective-permute-start.4) | collective-permute-done | bytes 135200 | tf_op jit(solution)/shard_map/ppermute | solution.py:341
  26.2 2.2 %collective-permute-done.3.refs_2_ = f32[264,128]{1,0:T(8,128)S(1)} collective-permute-done((f32[264,128]{1,0:T(8,128)S(1)}, f32[264,128]{1,0:T(8,128)S(1)}, u32[]{:S(2)}, u32[]{:S(2)}) %collective-permute-start.3) | collective-permute-done | bytes 135200 | tf_op jit(solution)/shard_map/ppermute | solution.py:341
  28.4 0.0 collective-permute-done.2.refs_1_
  28.4 2.9 %whiten.3 = (f32[128,3072]{1,0:T(8,128)S(1)}, f32[128,256]{1,0:T(8,128)S(1)}, f32[256,256]{1,0:T(8,128)S(1)}, f32[256,256]{1,0:T(8,128)S(1)}, f32[256,256]{1,0:T(8,128)S(1)}, /*index=5*/f32[256,128]{1,0:T(8,128)S(1)}) custom-call(f32[264,128]{1,0:T(8,128)S(1)} %add.12.refs_0_, f32[264,128]{1,0:T(8,128)S(1)} %collective-permute-done.2.refs_1_, ...), custom_call_target="tpu_custom_call" | custom-call | flops 1000000000 | bytes 6000000 | tf_op jit(solution)/shard_map/whiten/pallas_call | solution.py:233
  31.3 0.1 collective-permute-start.5
  31.4 1.2 kept.3
  32.6 22.2 %collective-permute-done.5.m_ref.refs_7_.refs_6_ = f32[128,3072]{1,0:T(8,128)S(1)} collective-permute-done((f32[128,3072]{1,0:T(8,128)S(1)}, f32[128,3072]{1,0:T(8,128)S(1)}, u32[]{:S(2)}, u32[]{:S(2)}) %collective-permute-start.5) | collective-permute-done | bytes 1572896 | tf_op jit(solution)/shard_map/ppermute | solution.py:341
  54.8 0.7 gram_cross.3
  55.5 1.6 collective-permute-start.6
  57.1 0.0 collective-permute-start.10
  57.1 2.8 %collective-permute-done.6 = f32[128,128]{1,0:T(8,128)S(1)} collective-permute-done((f32[128,128]{1,0:T(8,128)S(1)}, f32[128,128]{1,0:T(8,128)S(1)}, u32[]{:S(2)}, u32[]{:S(2)}) %collective-permute-start.6) | collective-permute-done | bytes 65568 | tf_op jit(solution)/shard_map/ppermute | solution.py:341
  59.9 2.1 %collective-permute-start.9 = (f32[128,128]{1,0:T(8,128)S(1)}, f32[128,128]{1,0:T(8,128)S(1)}, u32[]{:S(2)}, u32[]{:S(2)}) collective-permute-start(f32[128,128]{1,0:T(8,128)S(1)} %add.13.refs_0_), channel_id=1, source_target_pairs={{0,96},{1,97},{2,98},{3,99},{4,100},{5,101},{6,102},{7,103},{8,104... | collective-permute-start | bytes 196616 | tf_op jit(solution)/shard_map/ppermute | solution.py:341
  62.0 0.3 collective-permute-start.8
  62.3 1.8 collective-permute-start.7
  64.1 0.3 collective-permute-done.10.refs_5_
  64.4 1.0 collective-permute-done.9.refs_3_
  65.5 2.3 %collective-permute-done.8.refs_2_ = f32[128,128]{1,0:T(8,128)S(1)} collective-permute-done((f32[128,128]{1,0:T(8,128)S(1)}, f32[128,128]{1,0:T(8,128)S(1)}, u32[]{:S(2)}, u32[]{:S(2)}) %collective-permute-start.8) | collective-permute-done | bytes 65568 | tf_op jit(solution)/shard_map/ppermute | solution.py:341
  67.8 2.8 %whiten.4 = (f32[128,3072]{1,0:T(8,128)S(1)}, f32[128,256]{1,0:T(8,128)S(1)}, f32[256,256]{1,0:T(8,128)S(1)}, f32[256,256]{1,0:T(8,128)S(1)}, f32[256,256]{1,0:T(8,128)S(1)}, /*index=5*/f32[256,128]{1,0:T(8,128)S(1)}) custom-call(f32[128,128]{1,0:T(8,128)S(1)} %add.13.refs_0_, f32[128,128]{1,0:T(8,128)S(1)} %collective-permute-done.7.refs_1_, ...), custom_call_target="tpu_custom_call" | custom-call | flops 1000000000 | bytes 6000000 | tf_op jit(solution)/shard_map/whiten/pallas_call | solution.py:233
  70.5 0.3 collective-permute-start.11
  70.8 1.2 kept.4
  72.0 22.2 %collective-permute-done.11.m_ref.refs_7_.refs_6_ = f32[128,3072]{1,0:T(8,128)S(1)} collective-permute-done((f32[128,3072]{1,0:T(8,128)S(1)}, f32[128,3072]{1,0:T(8,128)S(1)}, u32[]{:S(2)}, u32[]{:S(2)}) %collective-permute-start.11) | collective-permute-done | bytes 1572896 | tf_op jit(solution)/shard_map/ppermute | solution.py:341
  94.2 0.7 gram_cross.4
  95.0 1.6 collective-permute-start.12
  96.5 0.0 collective-permute-start.16
  96.5 2.8 %collective-permute-done.12 = f32[128,128]{1,0:T(8,128)S(1)} collective-permute-done((f32[128,128]{1,0:T(8,128)S(1)}, f32[128,128]{1,0:T(8,128)S(1)}, u32[]{:S(2)}, u32[]{:S(2)}) %collective-permute-start.12) | collective-permute-done | bytes 65568 | tf_op jit(solution)/shard_map/ppermute | solution.py:341
  99.3 1.3 collective-permute-start.15
  100.7 1.4 collective-permute-start.14
  102.1 1.4 collective-permute-start.13
  103.5 0.3 collective-permute-done.16.refs_5_
  103.8 1.0 collective-permute-done.15.refs_3_
  104.9 1.6 collective-permute-done.14.refs_2_
  106.5 0.0 collective-permute-done.13.refs_1_
  106.5 2.8 %whiten.5 = (f32[128,3072]{1,0:T(8,128)S(1)}, f32[128,256]{1,0:T(8,128)S(1)}, f32[256,256]{1,0:T(8,128)S(1)}, f32[256,256]{1,0:T(8,128)S(1)}, f32[256,256]{1,0:T(8,128)S(1)}, /*index=5*/f32[256,128]{1,0:T(8,128)S(1)}) custom-call(f32[128,128]{1,0:T(8,128)S(1)} %add.14.refs_0_, f32[128,128]{1,0:T(8,128)S(1)} %collective-permute-done.13.refs_1_, ...), custom_call_target="tpu_custom_call" | custom-call | flops 1000000000 | bytes 6000000 | tf_op jit(solution)/shard_map/whiten/pallas_call | solution.py:233
  109.2 0.1 collective-permute-start.17
  109.3 1.2 kept.5
  110.6 22.2 %collective-permute-done.17.m_ref.refs_7_ = f32[128,3072]{1,0:T(8,128)S(1)} collective-permute-done((f32[128,3072]{1,0:T(8,128)S(1)}, f32[128,3072]{1,0:T(8,128)S(1)}, u32[]{:S(2)}, u32[]{:S(2)}) %collective-permute-start.17) | collective-permute-done | bytes 1572896 | tf_op jit(solution)/shard_map/ppermute | solution.py:341
  132.8 0.7 gram_cross.5
  133.5 2.3 %collective-permute-start.18 = (f32[128,128]{1,0:T(8,128)S(1)}, f32[128,128]{1,0:T(8,128)S(1)}, u32[]{:S(2)}, u32[]{:S(2)}) collective-permute-start(f32[128,128]{1,0:T(8,128)S(1)} %gram_cross.5), channel_id=1, source_target_pairs={{0,16},{1,17},{2,18},{3,19},{4,20},{5,21},{6,22},{7,23},{8,24},{9,... | collective-permute-start | bytes 196616 | tf_op jit(solution)/shard_map/ppermute | solution.py:341
  135.8 2.2 %collective-permute-done.18 = f32[128,128]{1,0:T(8,128)S(1)} collective-permute-done((f32[128,128]{1,0:T(8,128)S(1)}, f32[128,128]{1,0:T(8,128)S(1)}, u32[]{:S(2)}, u32[]{:S(2)}) %collective-permute-start.18) | collective-permute-done | bytes 65568 | tf_op jit(solution)/shard_map/ppermute | solution.py:341
  138.0 2.6 %collective-permute-start.21 = (f32[128,128]{1,0:T(8,128)S(1)}, f32[128,128]{1,0:T(8,128)S(1)}, u32[]{:S(2)}, u32[]{:S(2)}) collective-permute-start(f32[128,128]{1,0:T(8,128)S(1)} %add.15.refs_0_), channel_id=1, source_target_pairs={{0,96},{1,97},{2,98},{3,99},{4,100},{5,101},{6,102},{7,103},{8,104... | collective-permute-start | bytes 196616 | tf_op jit(solution)/shard_map/ppermute | solution.py:341
  140.6 1.4 collective-permute-start.20
  142.0 0.2 collective-permute-start.19
  142.2 0.9 collective-permute-done.22.refs_5_
  143.1 0.5 collective-permute-done.21.refs_3_
  143.6 2.8 %collective-permute-done.20.refs_2_ = f32[128,128]{1,0:T(8,128)S(1)} collective-permute-done((f32[128,128]{1,0:T(8,128)S(1)}, f32[128,128]{1,0:T(8,128)S(1)}, u32[]{:S(2)}, u32[]{:S(2)}) %collective-permute-start.20) | collective-permute-done | bytes 65568 | tf_op jit(solution)/shard_map/ppermute | solution.py:341
  146.4 3.0 %last.1 = (f32[128,3072]{1,0:T(8,128)S(1)}, f32[128,256]{1,0:T(8,128)S(1)}) custom-call(s32[1]{0:T(128)} %bitcast.core_ref, f32[1,512]{1,0:T(1,128)S(1)} %bitcast.6, f32[128,128]{1,0:T(8,128)S(1)} %add.15.refs_0_, f32[128,128]{1,0:T(8,128)S(1)} %collective-permute-done.19.refs_1_, f32[128,128]{1,0:T(8,128)S(1)} %collective-permute-done.20.refs_2_, ...), custom_call_target="tpu_custom_call" | custom-call | flops 1000000000 | bytes 6000000 | tf_op jit(solution)/shard_map/last/pallas_call | solution.py:304
  149.4 0.3 collective-permute-start.23
  149.7 3.4 %collective-permute-done.23.got_ref = f32[128,3072]{1,0:T(8,128)S(1)} collective-permute-done((f32[128,3072]{1,0:T(8,128)S(1)}, f32[128,3072]{1,0:T(8,128)S(1)}, u32[]{:S(2)}, u32[]{:S(2)}) %collective-permute-start.23) | collective-permute-done | bytes 1572896 | tf_op jit(solution)/shard_map/ppermute | solution.py:341
  153.1 1.0 last_kept.1
  154.2 2.1 %reshape.17 = f32[64,4,3072]{2,1,0:T(4,128)} reshape(f32[256,3072]{1,0:T(8,128)S(1)} %last_kept.1) | data formatting | bytes 6291456 | tf_op jit(solution)/shard_map/reshape | solution.py:375
  156.3 48.6 %all_to_all.5 = f32[64,4,3072]{2,1,0:T(4,128)S(1)} all-to-all(f32[64,4,3072]{2,1,0:T(4,128)} %reshape.17), channel_id=1, replica_groups=mesh['zx'=8,'core'=2,'pairs'=8] {'zx','pairs'}, dimensions={0} | all-to-all | bytes 6291456 | tf_op jit(solution)/shard_map/all_to_all | solution.py:376
  204.9 3.5 %copy.5 = f32[8,8,4,3072]{3,1,0,2:T(8,128)} copy(f32[8,8,4,3072]{3,2,1,0:T(4,128)S(1)} %bitcast.7) | data formatting | bytes 6291456 | tf_op jit(solution)/shard_map/reshape | solution.py:377
  (11 shorter events, 0.1 us)
Async XLA Ops:
  6.7 3.6 %collective-permute-start = (f32[256,1536]{1,0:T(8,128)}, f32[256,1536]{1,0:T(8,128)S(1)}, u32[]{:S(2)}, u32[]{:S(2)}) collective-permute-start(f32[256,1536]{1,0:T(8,128)} %get-tuple-element.38), channel_id=1, source_target_pairs={{0,8},{1,9},{2,10},{3,11},{4,12},{5,13},{6,14},{7,15},{8,0},{9,1},... | collective-permute-start | bytes 4718600 | tf_op jit(solution)/shard_map/ppermute | solution.py:341
  6.7 1.4 copy-start
  8.7 19.7 %copy-start.1 = (f32[256,1536]{1,0:T(8,128)S(1)}, f32[256,1536]{1,0:T(8,128)}, u32[]{:S(2)}) copy-start(f32[256,1536]{1,0:T(8,128)} %get-tuple-element.39.x_ref.refs_4_.refs_5_) | copy-start | bytes 4718596
  11.0 5.7 %collective-permute-start.1 = (f32[264,128]{1,0:T(8,128)S(1)}, f32[264,128]{1,0:T(8,128)S(1)}, u32[]{:S(2)}, u32[]{:S(2)}) collective-permute-start(f32[264,128]{1,0:T(8,128)S(1)} %gram_second.1), channel_id=1, source_target_pairs={{0,16},{1,17},{2,18},{3,19},{4,20},{5,21},{6,22},{7,23},{8,24},{9,... | collective-permute-start | bytes 405512 | tf_op jit(solution)/shard_map/ppermute | solution.py:341
  16.8 9.4 %collective-permute-start.4 = (f32[264,128]{1,0:T(8,128)S(1)}, f32[264,128]{1,0:T(8,128)S(1)}, u32[]{:S(2)}, u32[]{:S(2)}) collective-permute-start(f32[264,128]{1,0:T(8,128)S(1)} %add.12.refs_0_), channel_id=1, source_target_pairs={{0,96},{1,97},{2,98},{3,99},{4,100},{5,101},{6,102},{7,103},{8,104... | collective-permute-start | bytes 405512 | tf_op jit(solution)/shard_map/ppermute | solution.py:341
  21.0 7.5 %collective-permute-start.3 = (f32[264,128]{1,0:T(8,128)S(1)}, f32[264,128]{1,0:T(8,128)S(1)}, u32[]{:S(2)}, u32[]{:S(2)}) collective-permute-start(f32[264,128]{1,0:T(8,128)S(1)} %add.12.refs_0_), channel_id=1, source_target_pairs={{0,64},{1,65},{2,66},{3,67},{4,68},{5,69},{6,70},{7,71},{8,72},{9,... | collective-permute-start | bytes 405512 | tf_op jit(solution)/shard_map/ppermute | solution.py:341
  21.0 7.5 %collective-permute-start.2 = (f32[264,128]{1,0:T(8,128)S(1)}, f32[264,128]{1,0:T(8,128)S(1)}, u32[]{:S(2)}, u32[]{:S(2)}) collective-permute-start(f32[264,128]{1,0:T(8,128)S(1)} %add.12.refs_0_), channel_id=1, source_target_pairs={{0,32},{1,33},{2,34},{3,35},{4,36},{5,37},{6,38},{7,39},{8,40},{9,... | collective-permute-start | bytes 405512 | tf_op jit(solution)/shard_map/ppermute | solution.py:341
  31.3 23.5 %collective-permute-start.5 = (f32[128,3072]{1,0:T(8,128)S(1)}, f32[128,3072]{1,0:T(8,128)S(1)}, u32[]{:S(2)}, u32[]{:S(2)}) collective-permute-start(f32[128,3072]{1,0:T(8,128)S(1)} %get-tuple-element.48), channel_id=1, source_target_pairs={{0,8},{1,9},{2,10},{3,11},{4,12},{5,13},{6,14},{7,15},{8,1},{9,2},... | collective-permute-start | bytes 4718600 | tf_op jit(solution)/shard_map/ppermute | solution.py:341
  55.5 4.3 %collective-permute-start.6 = (f32[128,128]{1,0:T(8,128)S(1)}, f32[128,128]{1,0:T(8,128)S(1)}, u32[]{:S(2)}, u32[]{:S(2)}) collective-permute-start(f32[128,128]{1,0:T(8,128)S(1)} %gram_cross.3), channel_id=1, source_target_pairs={{0,16},{1,17},{2,18},{3,19},{4,20},{5,21},{6,22},{7,23},{8,24},{9,... | collective-permute-start | bytes 196616 | tf_op jit(solution)/shard_map/ppermute | solution.py:341
  57.1 7.3 %collective-permute-start.10 = (f32[128,128]{1,0:T(8,128)S(1)}, f32[128,128]{1,0:T(8,128)S(1)}, u32[]{:S(2)}, u32[]{:S(2)}) collective-permute-start(f32[128,128]{1,0:T(8,128)S(1)} %get-tuple-element.50), channel_id=1, source_target_pairs={{0,8},{1,9},{2,10},{3,11},{4,12},{5,13},{6,14},{7,15},{8,1},{9,2},... | collective-permute-start | bytes 196616 | tf_op jit(solution)/shard_map/ppermute | solution.py:341
  59.9 5.6 %collective-permute-start.9 = (f32[128,128]{1,0:T(8,128)S(1)}, f32[128,128]{1,0:T(8,128)S(1)}, u32[]{:S(2)}, u32[]{:S(2)}) collective-permute-start(f32[128,128]{1,0:T(8,128)S(1)} %add.13.refs_0_), channel_id=1, source_target_pairs={{0,96},{1,97},{2,98},{3,99},{4,100},{5,101},{6,102},{7,103},{8,104... | collective-permute-start | bytes 196616 | tf_op jit(solution)/shard_map/ppermute | solution.py:341
  62.0 5.8 %collective-permute-start.8 = (f32[128,128]{1,0:T(8,128)S(1)}, f32[128,128]{1,0:T(8,128)S(1)}, u32[]{:S(2)}, u32[]{:S(2)}) collective-permute-start(f32[128,128]{1,0:T(8,128)S(1)} %add.13.refs_0_), channel_id=1, source_target_pairs={{0,64},{1,65},{2,66},{3,67},{4,68},{5,69},{6,70},{7,71},{8,72},{9,... | collective-permute-start | bytes 196616 | tf_op jit(solution)/shard_map/ppermute | solution.py:341
  62.3 5.5 %collective-permute-start.7 = (f32[128,128]{1,0:T(8,128)S(1)}, f32[128,128]{1,0:T(8,128)S(1)}, u32[]{:S(2)}, u32[]{:S(2)}) collective-permute-start(f32[128,128]{1,0:T(8,128)S(1)} %add.13.refs_0_), channel_id=1, source_target_pairs={{0,32},{1,33},{2,34},{3,35},{4,36},{5,37},{6,38},{7,39},{8,40},{9,... | collective-permute-start | bytes 196616 | tf_op jit(solution)/shard_map/ppermute | solution.py:341
  70.5 23.7 %collective-permute-start.11 = (f32[128,3072]{1,0:T(8,128)S(1)}, f32[128,3072]{1,0:T(8,128)S(1)}, u32[]{:S(2)}, u32[]{:S(2)}) collective-permute-start(f32[128,3072]{1,0:T(8,128)S(1)} %get-tuple-element.57), channel_id=1, source_target_pairs={{0,8},{1,9},{2,10},{3,11},{4,12},{5,13},{6,14},{7,15},{8,1},{9,2},... | collective-permute-start | bytes 4718600 | tf_op jit(solution)/shard_map/ppermute | solution.py:341
  95.0 4.3 %collective-permute-start.12 = (f32[128,128]{1,0:T(8,128)S(1)}, f32[128,128]{1,0:T(8,128)S(1)}, u32[]{:S(2)}, u32[]{:S(2)}) collective-permute-start(f32[128,128]{1,0:T(8,128)S(1)} %gram_cross.4), channel_id=1, source_target_pairs={{0,16},{1,17},{2,18},{3,19},{4,20},{5,21},{6,22},{7,23},{8,24},{9,... | collective-permute-start | bytes 196616 | tf_op jit(solution)/shard_map/ppermute | solution.py:341
  96.5 7.3 %collective-permute-start.16 = (f32[128,128]{1,0:T(8,128)S(1)}, f32[128,128]{1,0:T(8,128)S(1)}, u32[]{:S(2)}, u32[]{:S(2)}) collective-permute-start(f32[128,128]{1,0:T(8,128)S(1)} %get-tuple-element.59), channel_id=1, source_target_pairs={{0,8},{1,9},{2,10},{3,11},{4,12},{5,13},{6,14},{7,15},{8,1},{9,2},... | collective-permute-start | bytes 196616 | tf_op jit(solution)/shard_map/ppermute | solution.py:341
  99.3 5.6 %collective-permute-start.15 = (f32[128,128]{1,0:T(8,128)S(1)}, f32[128,128]{1,0:T(8,128)S(1)}, u32[]{:S(2)}, u32[]{:S(2)}) collective-permute-start(f32[128,128]{1,0:T(8,128)S(1)} %add.14.refs_0_), channel_id=1, source_target_pairs={{0,96},{1,97},{2,98},{3,99},{4,100},{5,101},{6,102},{7,103},{8,104... | collective-permute-start | bytes 196616 | tf_op jit(solution)/shard_map/ppermute | solution.py:341
  100.7 5.8 %collective-permute-start.14 = (f32[128,128]{1,0:T(8,128)S(1)}, f32[128,128]{1,0:T(8,128)S(1)}, u32[]{:S(2)}, u32[]{:S(2)}) collective-permute-start(f32[128,128]{1,0:T(8,128)S(1)} %add.14.refs_0_), channel_id=1, source_target_pairs={{0,64},{1,65},{2,66},{3,67},{4,68},{5,69},{6,70},{7,71},{8,72},{9,... | collective-permute-start | bytes 196616 | tf_op jit(solution)/shard_map/ppermute | solution.py:341
  102.1 4.4 %collective-permute-start.13 = (f32[128,128]{1,0:T(8,128)S(1)}, f32[128,128]{1,0:T(8,128)S(1)}, u32[]{:S(2)}, u32[]{:S(2)}) collective-permute-start(f32[128,128]{1,0:T(8,128)S(1)} %add.14.refs_0_), channel_id=1, source_target_pairs={{0,32},{1,33},{2,34},{3,35},{4,36},{5,37},{6,38},{7,39},{8,40},{9,... | collective-permute-start | bytes 196616 | tf_op jit(solution)/shard_map/ppermute | solution.py:341
  109.2 23.5 %collective-permute-start.17 = (f32[128,3072]{1,0:T(8,128)S(1)}, f32[128,3072]{1,0:T(8,128)S(1)}, u32[]{:S(2)}, u32[]{:S(2)}) collective-permute-start(f32[128,3072]{1,0:T(8,128)S(1)} %get-tuple-element.66), channel_id=1, source_target_pairs={{0,8},{1,9},{2,10},{3,11},{4,12},{5,13},{6,14},{7,15},{8,1},{9,2},... | collective-permute-start | bytes 4718600 | tf_op jit(solution)/shard_map/ppermute | solution.py:341
  132.8 13.6 %copy-start.2 = (f32[512]{0:T(512)S(1)}, f32[512]{0:T(512)}, u32[]{:S(2)}) copy-start(f32[512]{0:T(512)} %param.7) | copy-start | bytes 6148
  133.5 4.5 %collective-permute-start.18 = (f32[128,128]{1,0:T(8,128)S(1)}, f32[128,128]{1,0:T(8,128)S(1)}, u32[]{:S(2)}, u32[]{:S(2)}) collective-permute-start(f32[128,128]{1,0:T(8,128)S(1)} %gram_cross.5), channel_id=1, source_target_pairs={{0,16},{1,17},{2,18},{3,19},{4,20},{5,21},{6,22},{7,23},{8,24},{9,... | collective-permute-start | bytes 196616 | tf_op jit(solution)/shard_map/ppermute | solution.py:341
  135.8 7.3 %collective-permute-start.22 = (f32[128,128]{1,0:T(8,128)S(1)}, f32[128,128]{1,0:T(8,128)S(1)}, u32[]{:S(2)}, u32[]{:S(2)}) collective-permute-start(f32[128,128]{1,0:T(8,128)S(1)} %get-tuple-element.68), channel_id=1, source_target_pairs={{0,8},{1,9},{2,10},{3,11},{4,12},{5,13},{6,14},{7,15},{8,1},{9,2},... | collective-permute-start | bytes 196616 | tf_op jit(solution)/shard_map/ppermute | solution.py:341
  138.0 5.6 %collective-permute-start.21 = (f32[128,128]{1,0:T(8,128)S(1)}, f32[128,128]{1,0:T(8,128)S(1)}, u32[]{:S(2)}, u32[]{:S(2)}) collective-permute-start(f32[128,128]{1,0:T(8,128)S(1)} %add.15.refs_0_), channel_id=1, source_target_pairs={{0,96},{1,97},{2,98},{3,99},{4,100},{5,101},{6,102},{7,103},{8,104... | collective-permute-start | bytes 196616 | tf_op jit(solution)/shard_map/ppermute | solution.py:341
  140.6 5.8 %collective-permute-start.20 = (f32[128,128]{1,0:T(8,128)S(1)}, f32[128,128]{1,0:T(8,128)S(1)}, u32[]{:S(2)}, u32[]{:S(2)}) collective-permute-start(f32[128,128]{1,0:T(8,128)S(1)} %add.15.refs_0_), channel_id=1, source_target_pairs={{0,64},{1,65},{2,66},{3,67},{4,68},{5,69},{6,70},{7,71},{8,72},{9,... | collective-permute-start | bytes 196616 | tf_op jit(solution)/shard_map/ppermute | solution.py:341
  142.0 4.3 %collective-permute-start.19 = (f32[128,128]{1,0:T(8,128)S(1)}, f32[128,128]{1,0:T(8,128)S(1)}, u32[]{:S(2)}, u32[]{:S(2)}) collective-permute-start(f32[128,128]{1,0:T(8,128)S(1)} %add.15.refs_0_), channel_id=1, source_target_pairs={{0,32},{1,33},{2,34},{3,35},{4,36},{5,37},{6,38},{7,39},{8,40},{9,... | collective-permute-start | bytes 196616 | tf_op jit(solution)/shard_map/ppermute | solution.py:341
  149.4 3.7 %collective-permute-start.23 = (f32[128,3072]{1,0:T(8,128)S(1)}, f32[128,3072]{1,0:T(8,128)S(1)}, u32[]{:S(2)}, u32[]{:S(2)}) collective-permute-start(f32[128,3072]{1,0:T(8,128)S(1)} %get-tuple-element.70), channel_id=1, source_target_pairs={{0,8},{1,9},{2,10},{3,11},{4,12},{5,13},{6,14},{7,15},{8,0},{9,1},... | collective-permute-start | bytes 4718600 | tf_op jit(solution)/shard_map/ppermute | solution.py:341

commit v3 on v2

--- a/solution.py
+++ b/solution.py
@@ -17,6 +17,7 @@
 F32 = jnp.float32
 BF16 = jnp.bfloat16
 VMEM = pl.BlockSpec(memory_space=pltpu.VMEM)
+ANY = pl.BlockSpec(memory_space=pl.ANY)
 SMEM = pl.BlockSpec(memory_space=pltpu.SMEM)
 NN = (((1,), (0,)), ((), ()))
 NT = (((1,), (1,)), ((), ()))
@@ -96,7 +97,8 @@
     out_ref[2 * BW :] = jnp.broadcast_to(on_diag, (8, BW))
 
 
-def gram_cross_kernel(k_ref, m_ref, out_ref):
+def gram_cross_kernel(k_ref, m_ref, *refs):
+    out_ref = refs[-1]
     total = jnp.zeros((PW, PW), F32)
     for half in range(2):
         for j in range(0, RH, CH):
@@ -132,16 +134,16 @@
     )(x, hh, hl)
 
 
-def gram_cross(k, m):
+def gram_cross(k, m, *arrived):
     return pl.pallas_call(
         gram_cross_kernel,
-        in_specs=[VMEM] * 2,
+        in_specs=[VMEM] * 2 + [ANY] * len(arrived),
         out_specs=VMEM,
         out_shape=jax.ShapeDtypeStruct((BW, BW), F32),
         compiler_params=params(),
         cost_estimate=cost(4 * RH * PW * PW, 3 * 10**6),
         name="gram_cross",
-    )(k, m)
+    )(k, m, *arrived)
 
 
 def newton(gram):
@@ -189,20 +191,25 @@
     return jnp.concatenate([top, bottom], axis=0)
 
 
-def columns(x_refs, first, half, j):
-    if first:
+HALVES = "halves"
+CROSSED = (False, True)
+SHADOW = (True, False)
+PLAIN = (False, False)
+
+
+def columns(x_refs, form, half, j):
+    if form == HALVES:
         return x_refs[half][:, j : j + CH]
-    ka = half * RH + j
-    ma = (1 - half) * RH + j
-    return jnp.concatenate([x_refs[0][:, ka : ka + CH], x_refs[1][:, ma : ma + CH]], axis=0)
-
-
-def apply_to(w, x_refs, first, out_ref, offset=None):
+    ats = [((1 - half) if crossed else half) * RH + j for crossed in form]
+    return jnp.concatenate([x_ref[:, at : at + CH] for x_ref, at in zip(x_refs, ats)], axis=0)
+
+
+def apply_to(w, x_refs, form, out_ref, offset=None):
     wh, wl = split(w)
     both = jnp.concatenate([wh, wl], axis=0)
     for half in range(2):
         for j in range(0, RH, CH):
-            xh, xl = split(columns(x_refs, first, half, j))
+            xh, xl = split(columns(x_refs, form, half, j))
             wide = mxu(both, xh)
             value = wide[:BW] + (wide[BW:] + mxu(wh, xl))
             if offset is None:
@@ -212,15 +219,35 @@
                 out_ref[:, pl.ds(at, CH)] = value
 
 
-def whiten_kernel(first, *refs):
-    n = 4 if first else 6
+BLOCK = jax.ShapeDtypeStruct((BW, RB), F32)
+ROWS_OF_W = jax.ShapeDtypeStruct((BW, PW), F32)
+SQUARE = jax.ShapeDtypeStruct((PW, PW), F32)
+SCALES = jax.ShapeDtypeStruct((PW, BW), F32)
+DIAGONAL = jax.ShapeDtypeStruct((BW, BW), F32)
+
+
+def call(kernel, ins, outs, name, args):
+    return pl.pallas_call(
+        kernel,
+        in_specs=ins,
+        out_specs=[VMEM] * len(outs),
+        out_shape=outs,
+        compiler_params=params(),
+        cost_estimate=cost(10**9, 6 * 10**6),
+        name=name,
+    )(*args)
+
+
+def whiten_kernel(moves, *refs):
+    n = 4 if moves else 6
     g_refs, diag_refs = refs[:4], refs[4:n]
-    x_refs = refs[n : n + 2]
-    moved_ref, w_ref, z_ref, y_ref, t_ref, d_ref = refs[n + 2 :]
+    first_ref, second_ref, z_ref, y_ref, t_ref, d_ref = refs[-6:]
     z, y, t, d_col, d_row, inv_row, fro = newton(gram_of(g_refs, diag_refs))
     wt = jnp.sqrt(d_col) * z.T * (inv_row / jnp.sqrt(fro))
-    apply_to(wt[BW:], x_refs, first, moved_ref)
-    w_ref[...] = wt[:BW]
+    first_ref[...] = wt[:BW]
+    second_ref[...] = wt[BW:]
+    if moves:
+        apply_to(wt[BW:], refs[n : n + 2], HALVES, refs[n + 2])
     z_ref[...] = z
     y_ref[...] = y
     t_ref[...] = t
@@ -228,52 +255,76 @@
     d_ref[...] = jnp.concatenate([root[:BW, :BW], root[BW:, BW:]], axis=0)
 
 
-def whiten(grams, diags, xs, first):
+def whiten(grams, diags, xs=()):
     args = [*grams, *diags, *xs]
-    return pl.pallas_call(
-        functools.partial(whiten_kernel, first),
-        in_specs=[VMEM] * len(args),
-        out_specs=[VMEM] * 6,
-        out_shape=[
-            jax.ShapeDtypeStruct((BW, RB), F32),
-            jax.ShapeDtypeStruct((BW, PW), F32),
-            jax.ShapeDtypeStruct((PW, PW), F32),
-            jax.ShapeDtypeStruct((PW, PW), F32),
-            jax.ShapeDtypeStruct((PW, PW), F32),
-            jax.ShapeDtypeStruct((PW, BW), F32),
-        ],
-        compiler_params=params(),
-        cost_estimate=cost(10**9, 6 * 10**6),
-        name="whiten",
-    )(*args)
-
-
-def kept_kernel(first, *refs):
-    w_ref, z_ref, y_ref, t_ref, d_ref = refs[:5]
-    x_refs = refs[5:7]
-    kept_ref, kept_diag_ref, moved_diag_ref = refs[7:]
-    zs = split(z_ref[...])
+    outs = [ROWS_OF_W, ROWS_OF_W, SQUARE, SQUARE, SQUARE, SCALES]
+    if xs:
+        outs = [BLOCK] + outs
+    return call(functools.partial(whiten_kernel, bool(xs)), [VMEM] * len(args), outs, "whiten", args)
+
+
+def next_diagonals(z_ref, y_ref, t_ref, d_ref):
     ys = split(dot3(split(y_ref[...]), split(t_ref[...])))
-    new = dot3(ys, zs)
-    kept_diag_ref[...] = new[:BW, :BW] * d_ref[:BW]
-    moved_diag_ref[...] = new[BW:, BW:] * d_ref[BW:]
-    apply_to(w_ref[...], x_refs, first, kept_ref)
-
-
-def kept_part(w, z, y, t, d, xs, first):
-    return pl.pallas_call(
-        functools.partial(kept_kernel, first),
-        in_specs=[VMEM] * 7,
-        out_specs=[VMEM] * 3,
-        out_shape=[
-            jax.ShapeDtypeStruct((BW, RB), F32),
-            jax.ShapeDtypeStruct((BW, BW), F32),
-            jax.ShapeDtypeStruct((BW, BW), F32),
-        ],
-        compiler_params=params(),
-        cost_estimate=cost(10**9, 6 * 10**6),
-        name="kept",
-    )(w, z, y, t, d, *xs)
+    new = dot3(ys, split(z_ref[...]))
+    return new[:BW, :BW] * d_ref[:BW], new[BW:, BW:] * d_ref[BW:]
+
+
+def kept_first_kernel(w_ref, z_ref, y_ref, t_ref, d_ref, x0_ref, x1_ref, kept_ref, diag0_ref, diag1_ref):
+    apply_to(w_ref[...], (x0_ref, x1_ref), HALVES, kept_ref)
+    diag0_ref[...], diag1_ref[...] = next_diagonals(z_ref, y_ref, t_ref, d_ref)
+
+
+def kept_first(*args):
+    return call(kept_first_kernel, [VMEM] * 7, [BLOCK, DIAGONAL, DIAGONAL], "kept_first", args)
+
+
+def kept_second_kernel(form, w_ref, z_ref, y_ref, t_ref, d_ref, x0_ref, x1_ref, kept_ref, diag_ref, more_ref):
+    apply_to(w_ref[...], (x0_ref, x1_ref), form, kept_ref)
+    more_ref[:, :BW], diag_ref[...] = next_diagonals(z_ref, y_ref, t_ref, d_ref)
+    more_ref[:, BW:] = w_ref[...]
+
+
+def kept_second(form, *args):
+    more = jax.ShapeDtypeStruct((BW, BW + PW), F32)
+    kernel = functools.partial(kept_second_kernel, form)
+    return call(kernel, [VMEM] * 7, [BLOCK, DIAGONAL, more], "kept_second", args)
+
+
+def on_second_core_kernel(form, core_ref, w_ref, x0_ref, x1_ref, out_ref):
+    @pl.when(core_ref[0] != 0)
+    def _():
+        apply_to(w_ref[...], (x0_ref, x1_ref), form, out_ref)
+
+
+def on_second_core(form, core, w, xs, name):
+    kernel = functools.partial(on_second_core_kernel, form)
+    return call(kernel, [SMEM] + [VMEM] * 3, [BLOCK], name, [core, w, *xs])[0]
+
+
+def combine_kernel(form, core_ref, w_ref, s0_ref, s1_ref, other_ref, kept_ref, *refs):
+    in_ref, out_ref = refs[-2:]
+
+    @pl.when(core_ref[0] == 0)
+    def _():
+        in_ref[:, :RH] = other_ref[:, RH:]
+        in_ref[:, RH:] = other_ref[:, :RH]
+
+    @pl.when(core_ref[0] != 0)
+    def _():
+        apply_to(w_ref[...], (s0_ref, s1_ref), form, in_ref)
+
+    total = jnp.zeros((PW, PW), F32)
+    for j in range(0, RB, CH):
+        a = jnp.concatenate(split(in_ref[:, j : j + CH]), axis=0)
+        b = jnp.concatenate(split(kept_ref[:, j : j + CH]), axis=0)
+        total += mxu(a, b, NT)
+    out_ref[...] = (total[:BW, :BW] + total[BW:, BW:]) + (total[:BW, BW:] + total[BW:, :BW])
+
+
+def combine(form, core, w, shadow, other, kept):
+    kernel = functools.partial(combine_kernel, form)
+    args = [core, w, *shadow, other, kept]
+    return call(kernel, [SMEM] + [VMEM] * 5, [BLOCK, DIAGONAL], "combine", args)
 
 
 def by_core(w, even):
@@ -296,7 +347,7 @@
     thr = jnp.sum(jnp.where(at_row == at_col, thr_row, 0.0), axis=1, keepdims=True)
     factor = jnp.maximum(norm - thr, 0.0) / norm
     wt = (factor * jnp.sqrt(d_col)) * z.T * (inv_row / jnp.sqrt(fro))
-    apply_to(by_core(wt, core != 0), x_refs, False, send_ref, core * RH)
+    apply_to(by_core(wt, core != 0), x_refs, PLAIN, send_ref, core * RH)
     w_ref[...] = by_core(wt, core == 0)
 
 
@@ -315,7 +366,7 @@
 def last_kept_kernel(core_ref, w_ref, k_ref, m_ref, got_ref, out_ref):
     core = core_ref[0]
     mine = pl.multiple_of(core * BW, BW)
-    apply_to(w_ref[...], (k_ref, m_ref), False, out_ref.at[pl.ds(mine, BW)], core * RH)
+    apply_to(w_ref[...], (k_ref, m_ref), PLAIN, out_ref.at[pl.ds(mine, BW)], core * RH)
     out_ref[pl.ds(pl.multiple_of(BW - mine, BW), BW)] = got_ref[...]
 
 
@@ -336,8 +387,10 @@
     for i in range(8):
         for c in range(2):
             for g in range(8):
-                ti, tc, tg = where(i, c, g)
-                route.append(((i * 2 + c) * 8 + g, (ti * 2 + tc) * 8 + tg))
+                goal = where(i, c, g)
+                if goal is not None:
+                    ti, tc, tg = goal
+                    route.append(((i * 2 + c) * 8 + g, (ti * 2 + tc) * 8 + tg))
     return lax.ppermute(block, AXES, route)
 
 
@@ -347,6 +400,18 @@
 
 def onward(block):
     return to(block, lambda i, c, g: (i, 1, g) if c == 0 else (i, 0, (g + 1) % 8))
+
+
+def backward(block):
+    return to(block, lambda i, c, g: (i, 1, (g - 1) % 8) if c == 0 else (i, 0, g))
+
+
+def behind(block, core):
+    return to(block, lambda i, c, g: (i, 1, (g - 1) % 8) if c == core else None)
+
+
+def beside(block):
+    return to(block, lambda i, c, g: (i, 0, g) if c == 1 else None)
 
 
 def reduced(partial):
@@ -355,26 +420,37 @@
 
 
 def on_device(observed, estimate, mask, threshold):
-    core_index = lax.axis_index("core")
-    core = core_index.reshape(1).astype(jnp.int32)
-    thr = threshold.reshape(1, -1)
+    core = lax.axis_index("core").reshape(1).astype(jnp.int32)
+    thr = to(threshold.reshape(1, -1), lambda i, c, g: (i, c, (g - 1) % 8))
     keep, send = fill(core, observed, estimate, mask)
     got = swap_cores(send)
     grams = reduced(gram_second(got, *gram_first(keep)))
-    xs, diags = (keep, got), []
-    for round_index in range(ROUNDS - 1):
-        first = round_index == 0
-        moved, *rest = whiten(grams, diags, xs, first)
-        arrived = onward(moved)
-        kept, kept_diag, moved_diag = kept_part(*rest, xs, first)
-        diags = [kept_diag, onward(moved_diag)]
-        xs = (kept, arrived)
-        grams = reduced(gram_cross(*xs))
-    send, w = last(core, thr, grams, diags, xs)
+    second, w0, _, *rest = whiten(grams, [], (keep, got))
+    joined = onward(second)
+    first, diag0, diag1 = kept_first(w0, *rest, keep, got)
+    shadow, shadow_form = (behind(first, 0), second), SHADOW
+    diags = [diag0, onward(diag1)]
+    xs, form = (first, joined), CROSSED
+    partial = gram_cross(first, joined, shadow[0], thr)
+    for round_index in range(1, ROUNDS - 1):
+        w0, w1, *rest = whiten(reduced(partial), diags)
+        w_shadow = behind(w0, 0)
+        given = on_second_core(form, core, w0, xs, "given")
+        other = beside(given)
+        kept, diag1, more = kept_second(form, w1, *rest, *xs)
+        more = backward(more)
+        joined, partial = combine(shadow_form, core, w_shadow, shadow, other, kept)
+        diags = [more[:, :BW], diag1]
+        xs, form = (joined, kept), PLAIN
+        if round_index + 2 < ROUNDS:
+            moved = on_second_core(shadow_form, core, more[:, BW:], shadow, "shadow")
+            shadow, shadow_form = (to(given, lambda i, c, g: (i, 1, (g - 1) % 8) if c == 1 else None), moved), PLAIN
+    send, w = last(core, thr, reduced(partial), diags, xs)
     got = swap_cores(send)
     packed = last_kept(core, w, xs, got).reshape(64, 4, RB)
     landed = lax.all_to_all(packed, ("zx", "pairs"), split_axis=0, concat_axis=0, tiled=True)
-    landed = landed.reshape(8, 8, 4, RB).transpose(2, 1, 0, 3)
+    landed = landed.reshape(8, 8, 4, RB)
+    landed = jnp.roll(landed, 1, axis=1).transpose(2, 1, 0, 3)
     return landed.reshape(32, 8 * RB)
 
 

time: 209 us -> 199 us (0.952)
  waiting for transfers between devices: 101 us -> 63.3 us
  starting transfers between devices: 25.5 us -> 50.4 us
  blocking collectives: 48.6 us -> 50.9 us
  other arithmetic: 0.05 us -> 2.34 us
    ppermute x24 -> x29, waiting for transfers between devices: 101 us -> 63.3 us  [to(): return lax.ppermute(block, AXES, route)]
    ppermute x24 -> x29, starting transfers between devices: 25.5 us -> 50.4 us  [to(): return lax.ppermute(block, AXES, route)]
    reshape x1 -> x0, local copies, waits for them, and re-layouts: 3.49 us -> none  [on_device(): landed = landed.reshape(8, 8, 4, RB).transpose(2, 1, 0, 3)]
    concatenate x0 -> x1, other arithmetic: none -> 2.29 us  [on_device(): landed = jnp.roll(landed, 1, axis=1).transpose(2, 1, 0, 3)]
    all_to_all x1, blocking collectives: 48.6 us -> 50.9 us  [on_device(): lax.all_to_all(packed, ('zx', 'pairs'), split_axis=0, concat_axis=0, tile...]
    pallas_call x9 -> x12, Pallas kernels: 14.3 us -> 13.3 us  [the longest x11 12.5 us: call(): pl.pallas_call(kernel, in_specs=ins, out_specs=[VMEM] * len(outs), out_sh...]
  transfers between devices with their start and end apart: 24 -> 29, of which waited for: 20 -> 18; matrix products, arithmetic and copies ran while one was open for 0% -> 0% of each run, Pallas kernels for 2% -> 3%
where the time goes in v3:
time: 199 us
  waiting for transfers between devices  63.3 us (32%)
  blocking collectives  50.9 us (26%)
  starting transfers between devices  50.4 us (25%)
  Pallas kernels  25.4 us (13%)
  local copies, waits for them, and re-layouts  5.9 us (3%)
  other arithmetic  2.34 us (1%)
    ppermute x29, waiting for transfers between devices, to(): return lax.ppermute(block, AXES, route)  63.3 us
    all_to_all x1, blocking collectives, on_device(): lax.all_to_all(packed, ('zx', 'pairs'), split_axis=0, concat_axis=0, tile...  50.9 us
    ppermute x29, starting transfers between devices, to(): return lax.ppermute(block, AXES, route)  50.4 us
    pallas_call x11, Pallas kernels, call(): pl.pallas_call(kernel, in_specs=ins, out_specs=[VMEM] * len(outs), out_sh...  12.5 us
    pallas_call x1, Pallas kernels, fill(): pl.pallas_call(fill_kernel, grid=(RH // step,), in_specs=[SMEM, rows, row...  6.73 us
  transfers between devices with their start and end apart: 29, of which 18 were waited for; matrix products, arithmetic and copies ran while one was open for 0% of the time, Pallas kernels for 3%

profile of v3, /device:TPU:0, one launch (start us, length us, event | category | flops | bytes accessed | tf_op | source)
XLA Modules:
  0.0 198.6 jit_solution(2810707480482742320)
XLA Ops:
  0.0 6.7 %fill.1 = (f32[256,1536]{1,0:T(8,128)}, f32[256,1536]{1,0:T(8,128)}) custom-call(s32[1]{0:T(128)} %bitcast.core_ref, f32[1536,512]{1,0:T(8,128)} %obs_ref.1, f32[1536,512]{1,0:T(8,128)} %est_ref.1, s32[1536,512]{1,0:T(8,128)} %mask_ref.1), custom_call_target="tpu_custom_call" | custom-call | flops 1000000 | bytes 15000000 | tf_op jit(solution)/shard_map/fill/pallas_call | solution.py:61
  6.7 1.4 copy-done
  8.1 0.6 gram_first.1
  8.8 1.6 collective-permute-done.1.x_ref.refs_5_.x1_ref
  10.4 0.7 gram_second.1
  11.1 1.6 collective-permute-start.2
  12.7 4.0 %collective-permute-done.2 = f32[264,128]{1,0:T(8,128)S(1)} collective-permute-done((f32[264,128]{1,0:T(8,128)S(1)}, f32[264,128]{1,0:T(8,128)S(1)}, u32[]{:S(2)}, u32[]{:S(2)}) %collective-permute-start.2) | collective-permute-done | bytes 135200 | tf_op jit(solution)/shard_map/ppermute | solution.py:394
  16.8 4.2 %collective-permute-start.5 = (f32[264,128]{1,0:T(8,128)S(1)}, f32[264,128]{1,0:T(8,128)S(1)}, u32[]{:S(2)}, u32[]{:S(2)}) collective-permute-start(f32[264,128]{1,0:T(8,128)S(1)} %add.12.refs_0_), channel_id=1, source_target_pairs={{0,96},{1,97},{2,98},{3,99},{4,100},{5,101},{6,102},{7,103},{8,104... | collective-permute-start | bytes 405512 | tf_op jit(solution)/shard_map/ppermute | solution.py:394
  21.0 0.9 collective-permute-start.3
  21.9 4.3 %collective-permute-done.5.refs_3_ = f32[264,128]{1,0:T(8,128)S(1)} collective-permute-done((f32[264,128]{1,0:T(8,128)S(1)}, f32[264,128]{1,0:T(8,128)S(1)}, u32[]{:S(2)}, u32[]{:S(2)}) %collective-permute-start.5) | collective-permute-done | bytes 135200 | tf_op jit(solution)/shard_map/ppermute | solution.py:394
  26.2 2.2 %collective-permute-done.4.refs_2_ = f32[264,128]{1,0:T(8,128)S(1)} collective-permute-done((f32[264,128]{1,0:T(8,128)S(1)}, f32[264,128]{1,0:T(8,128)S(1)}, u32[]{:S(2)}, u32[]{:S(2)}) %collective-permute-start.4) | collective-permute-done | bytes 135200 | tf_op jit(solution)/shard_map/ppermute | solution.py:394
  28.5 3.0 %whiten.3 = (f32[128,3072]{1,0:T(8,128)S(1)}, f32[128,256]{1,0:T(8,128)S(1)}, f32[128,256]{1,0:T(8,128)}, f32[256,256]{1,0:T(8,128)S(1)}, f32[256,256]{1,0:T(8,1...) custom-call(f32[264,128]{1,0:T(8,128)S(1)} %add.12.refs_0_, f32[264,128]{1,0:T(8,128)S(1)} %collective-permute-done.3.refs_1_, ...), custom_call_target="tpu_custom_call" | custom-call | flops 1000000000 | bytes 6000000 | tf_op jit(solution)/shard_map/whiten/pallas_call | solution.py:230
  31.5 1.3 kept_first.1
  32.8 4.4 %collective-permute-start.7 = (f32[128,3072]{1,0:T(8,128)S(1)}, f32[128,3072]{1,0:T(8,128)S(1)}, u32[]{:S(2)}, u32[]{:S(2)}) collective-permute-start(f32[128,3072]{1,0:T(8,128)S(1)} %get-tuple-element.51.k_ref.x0_ref), channel_id=1, source_target_pairs={{0,15},{1,8},{2,9},{3,10},{4,11},{5,12},{6,13},{7,14},{16,31},{17,... | collective-permute-start | bytes 4718600 | tf_op jit(solution)/shard_map/ppermute | solution.py:394
  37.2 0.1 collective-permute-start.6
  37.3 2.5 %collective-permute-start = (f32[1,512]{1,0:T(1,128)S(1)}, f32[1,512]{1,0:T(1,128)S(1)}, u32[]{:S(2)}, u32[]{:S(2)}) collective-permute-start(f32[1,512]{1,0:T(1,128)S(1)} %bitcast.8), channel_id=1, source_target_pairs={{0,7},{1,0},{2,1},{3,2},{4,3},{5,4},{6,5},{7,6},{8,15},{9,8},{10,9... | collective-permute-start | bytes 6152 | tf_op jit(solution)/shard_map/ppermute | solution.py:394
  39.9 15.2 %collective-permute-done.refs_1_.thr_ref = f32[1,512]{1,0:T(1,128)S(1)} collective-permute-done((f32[1,512]{1,0:T(1,128)S(1)}, f32[1,512]{1,0:T(1,128)S(1)}, u32[]{:S(2)}, u32[]{:S(2)}) %collective-permute-start) | collective-permute-done | bytes 2080 | tf_op jit(solution)/shard_map/ppermute | solution.py:394
  55.1 5.7 %collective-permute-done.6.m_ref.x1_ref = f32[128,3072]{1,0:T(8,128)S(1)} collective-permute-done((f32[128,3072]{1,0:T(8,128)S(1)}, f32[128,3072]{1,0:T(8,128)S(1)}, u32[]{:S(2)}, u32[]{:S(2)}) %collective-permute-start.6) | collective-permute-done | bytes 1572896 | tf_op jit(solution)/shard_map/ppermute | solution.py:394
  60.7 0.7 gram_cross.1
  61.5 0.7 collective-permute-start.8
  62.1 3.7 %collective-permute-done.8 = f32[128,128]{1,0:T(8,128)S(1)} collective-permute-done((f32[128,128]{1,0:T(8,128)S(1)}, f32[128,128]{1,0:T(8,128)S(1)}, u32[]{:S(2)}, u32[]{:S(2)}) %collective-permute-start.8) | collective-permute-done | bytes 65568 | tf_op jit(solution)/shard_map/ppermute | solution.py:394
  65.8 3.8 %collective-permute-start.11 = (f32[128,128]{1,0:T(8,128)S(1)}, f32[128,128]{1,0:T(8,128)S(1)}, u32[]{:S(2)}, u32[]{:S(2)}) collective-permute-start(f32[128,128]{1,0:T(8,128)S(1)} %add.13.refs_0_), channel_id=1, source_target_pairs={{0,96},{1,97},{2,98},{3,99},{4,100},{5,101},{6,102},{7,103},{8,104... | collective-permute-start | bytes 196616 | tf_op jit(solution)/shard_map/ppermute | solution.py:394
  69.6 0.9 collective-permute-start.9
  70.6 1.6 collective-permute-done.11.refs_3_
  72.1 3.3 %collective-permute-done.10.refs_2_ = f32[128,128]{1,0:T(8,128)S(1)} collective-permute-done((f32[128,128]{1,0:T(8,128)S(1)}, f32[128,128]{1,0:T(8,128)S(1)}, u32[]{:S(2)}, u32[]{:S(2)}) %collective-permute-start.10) | collective-permute-done | bytes 65568 | tf_op jit(solution)/shard_map/ppermute | solution.py:394
  75.4 1.9 whiten.4
  77.4 1.3 collective-permute-start.14
  78.7 4.0 %collective-permute-start.13 = (f32[128,256]{1,0:T(8,128)S(1)}, f32[128,256]{1,0:T(8,128)S(1)}, u32[]{:S(2)}, u32[]{:S(2)}) collective-permute-start(f32[128,256]{1,0:T(8,128)S(1)} %get-tuple-element.55.w_ref), channel_id=1, source_target_pairs={{0,15},{1,8},{2,9},{3,10},{4,11},{5,12},{6,13},{7,14},{16,31},{17,... | collective-permute-start | bytes 393224 | tf_op jit(solution)/shard_map/ppermute | solution.py:394
  82.7 1.3 kept_second.2
  84.0 0.1 collective-permute-start.19
  84.1 0.9 collective-permute-done.13.w_ref
  85.0 0.8 combine.2
  85.8 1.1 collective-permute-start.15
  86.9 3.3 %collective-permute-done.15 = f32[128,128]{1,0:T(8,128)S(1)} collective-permute-done((f32[128,128]{1,0:T(8,128)S(1)}, f32[128,128]{1,0:T(8,128)S(1)}, u32[]{:S(2)}, u32[]{:S(2)}) %collective-permute-start.15) | collective-permute-done | bytes 65568 | tf_op jit(solution)/shard_map/ppermute | solution.py:394
  90.2 2.2 %collective-permute-start.18 = (f32[128,128]{1,0:T(8,128)S(1)}, f32[128,128]{1,0:T(8,128)S(1)}, u32[]{:S(2)}, u32[]{:S(2)}) collective-permute-start(f32[128,128]{1,0:T(8,128)S(1)} %add.14.refs_0_), channel_id=1, source_target_pairs={{0,96},{1,97},{2,98},{3,99},{4,100},{5,101},{6,102},{7,103},{8,104... | collective-permute-start | bytes 196616 | tf_op jit(solution)/shard_map/ppermute | solution.py:394
  92.4 0.1 collective-permute-start.17
  92.5 1.8 collective-permute-start.16
  94.3 0.7 collective-permute-start.21
  95.1 1.2 collective-permute-done.18.refs_3_
  96.3 2.3 %collective-permute-done.17.refs_2_ = f32[128,128]{1,0:T(8,128)S(1)} collective-permute-done((f32[128,128]{1,0:T(8,128)S(1)}, f32[128,128]{1,0:T(8,128)S(1)}, u32[]{:S(2)}, u32[]{:S(2)}) %collective-permute-start.17) | collective-permute-done | bytes 65568 | tf_op jit(solution)/shard_map/ppermute | solution.py:394
  98.7 1.9 whiten.5
  100.6 1.3 collective-permute-start.22
  101.9 6.1 %collective-permute-start.20 = (f32[128,256]{1,0:T(8,128)S(1)}, f32[128,256]{1,0:T(8,128)S(1)}, u32[]{:S(2)}, u32[]{:S(2)}) collective-permute-start(f32[128,256]{1,0:T(8,128)S(1)} %get-tuple-element.65.w_ref), channel_id=1, source_target_pairs={{0,15},{1,8},{2,9},{3,10},{4,11},{5,12},{6,13},{7,14},{16,31},{17,... | collective-permute-start | bytes 393224 | tf_op jit(solution)/shard_map/ppermute | solution.py:394
  108.1 1.3 kept_second.3
  109.4 0.4 collective-permute-start.27
  109.8 2.2 %collective-permute-done.20.w_ref = f32[128,256]{1,0:T(8,128)S(1)} collective-permute-done((f32[128,256]{1,0:T(8,128)S(1)}, f32[128,256]{1,0:T(8,128)S(1)}, u32[]{:S(2)}, u32[]{:S(2)}) %collective-permute-start.20) | collective-permute-done | bytes 131104 | tf_op jit(solution)/shard_map/ppermute | solution.py:394
  112.0 0.8 combine.3
  112.8 0.5 collective-permute-start.23
  113.3 5.1 %collective-permute-done.23 = f32[128,128]{1,0:T(8,128)S(1)} collective-permute-done((f32[128,128]{1,0:T(8,128)S(1)}, f32[128,128]{1,0:T(8,128)S(1)}, u32[]{:S(2)}, u32[]{:S(2)}) %collective-permute-start.23) | collective-permute-done | bytes 65568 | tf_op jit(solution)/shard_map/ppermute | solution.py:394
  118.5 2.1 %collective-permute-start.26 = (f32[128,128]{1,0:T(8,128)S(1)}, f32[128,128]{1,0:T(8,128)S(1)}, u32[]{:S(2)}, u32[]{:S(2)}) collective-permute-start(f32[128,128]{1,0:T(8,128)S(1)} %add.15.refs_0_), channel_id=1, source_target_pairs={{0,96},{1,97},{2,98},{3,99},{4,100},{5,101},{6,102},{7,103},{8,104... | collective-permute-start | bytes 196616 | tf_op jit(solution)/shard_map/ppermute | solution.py:394
  120.6 1.1 collective-permute-start.25
  121.7 1.0 collective-permute-start.24
  122.7 1.4 collective-permute-done.26.refs_3_
  124.1 2.3 %collective-permute-done.25.refs_2_ = f32[128,128]{1,0:T(8,128)S(1)} collective-permute-done((f32[128,128]{1,0:T(8,128)S(1)}, f32[128,128]{1,0:T(8,128)S(1)}, u32[]{:S(2)}, u32[]{:S(2)}) %collective-permute-start.25) | collective-permute-done | bytes 65568 | tf_op jit(solution)/shard_map/ppermute | solution.py:394
  126.3 3.1 %last.1 = (f32[128,3072]{1,0:T(8,128)S(1)}, f32[128,256]{1,0:T(8,128)S(1)}) custom-call(s32[1]{0:T(128)} %bitcast.core_ref, f32[1,512]{1,0:T(1,128)S(1)} %collective-permute-done.refs_1_.thr_ref, f32[128,128]{1,0:T(8,128)S(1)} %add.15.refs_0_, f32[128,128]{1,0:T(8,128)S(1)} %collective-permute-done.24.refs_1_, ...), custom_call_target="tpu_custom_call" | custom-call | flops 1000000000 | bytes 6000000 | tf_op jit(solution)/shard_map/last/pallas_call | solution.py:355
  129.4 7.4 %collective-permute-start.28 = (f32[128,3072]{1,0:T(8,128)S(1)}, f32[128,3072]{1,0:T(8,128)S(1)}, u32[]{:S(2)}, u32[]{:S(2)}) collective-permute-start(f32[128,3072]{1,0:T(8,128)S(1)} %get-tuple-element.78), channel_id=1, source_target_pairs={{0,8},{1,9},{2,10},{3,11},{4,12},{5,13},{6,14},{7,15},{8,0},{9,1},... | collective-permute-start | bytes 4718600 | tf_op jit(solution)/shard_map/ppermute | solution.py:394
  136.8 3.0 %collective-permute-done.28.got_ref = f32[128,3072]{1,0:T(8,128)S(1)} collective-permute-done((f32[128,3072]{1,0:T(8,128)S(1)}, f32[128,3072]{1,0:T(8,128)S(1)}, u32[]{:S(2)}, u32[]{:S(2)}) %collective-permute-start.28) | collective-permute-done | bytes 1572896 | tf_op jit(solution)/shard_map/ppermute | solution.py:394
  139.9 1.1 last_kept.1
  140.9 2.1 %reshape.17 = f32[64,4,3072]{2,1,0:T(4,128)} reshape(f32[256,3072]{1,0:T(8,128)S(1)} %last_kept.1) | data formatting | bytes 6291456 | tf_op jit(solution)/shard_map/reshape | solution.py:450
  143.1 50.9 %all_to_all.5 = f32[64,4,3072]{2,1,0:T(4,128)S(1)} all-to-all(f32[64,4,3072]{2,1,0:T(4,128)} %reshape.17), channel_id=1, replica_groups=mesh['zx'=8,'core'=2,'pairs'=8] {'zx','pairs'}, dimensions={0} | all-to-all | bytes 6291456 | tf_op jit(solution)/shard_map/all_to_all | solution.py:451
  194.0 0.3 slice.26
  194.3 0.4 copy.7
  194.7 1.6 copy.8
  196.3 2.3 %pad_maximum_fusion = f32[8,8,4,3072]{3,1,0,2:T(8,128)} fusion(f32[8,7,4,3072]{3,1,0,2:T(8,128)S(1)} %copy.8, f32[8,1,4,3072]{3,1,0,2:T(1,128)S(1)} %copy.7), kind=kLoop, calls=%fused_computation | loop fusion | flops 786432 | bytes 6291456 | tf_op jit(solution)/shard_map/jit(_roll_static)/concatenate | solution.py:453
  (31 shorter events, 0.2 us)
Async XLA Ops:
  6.7 3.6 %collective-permute-start.1 = (f32[256,1536]{1,0:T(8,128)}, f32[256,1536]{1,0:T(8,128)S(1)}, u32[]{:S(2)}, u32[]{:S(2)}) collective-permute-start(f32[256,1536]{1,0:T(8,128)} %get-tuple-element.42), channel_id=1, source_target_pairs={{0,8},{1,9},{2,10},{3,11},{4,12},{5,13},{6,14},{7,15},{8,0},{9,1},... | collective-permute-start | bytes 4718600 | tf_op jit(solution)/shard_map/ppermute | solution.py:394
  6.7 1.4 copy-start
  8.8 19.7 %copy-start.1 = (f32[256,1536]{1,0:T(8,128)S(1)}, f32[256,1536]{1,0:T(8,128)}, u32[]{:S(2)}) copy-start(f32[256,1536]{1,0:T(8,128)} %get-tuple-element.43.x_ref.refs_4_.x0_ref) | copy-start | bytes 4718596
  11.1 5.7 %collective-permute-start.2 = (f32[264,128]{1,0:T(8,128)S(1)}, f32[264,128]{1,0:T(8,128)S(1)}, u32[]{:S(2)}, u32[]{:S(2)}) collective-permute-start(f32[264,128]{1,0:T(8,128)S(1)} %gram_second.1), channel_id=1, source_target_pairs={{0,16},{1,17},{2,18},{3,19},{4,20},{5,21},{6,22},{7,23},{8,24},{9,... | collective-permute-start | bytes 405512 | tf_op jit(solution)/shard_map/ppermute | solution.py:394
  16.8 9.5 %collective-permute-start.5 = (f32[264,128]{1,0:T(8,128)S(1)}, f32[264,128]{1,0:T(8,128)S(1)}, u32[]{:S(2)}, u32[]{:S(2)}) collective-permute-start(f32[264,128]{1,0:T(8,128)S(1)} %add.12.refs_0_), channel_id=1, source_target_pairs={{0,96},{1,97},{2,98},{3,99},{4,100},{5,101},{6,102},{7,103},{8,104... | collective-permute-start | bytes 405512 | tf_op jit(solution)/shard_map/ppermute | solution.py:394
  21.0 7.5 %collective-permute-start.4 = (f32[264,128]{1,0:T(8,128)S(1)}, f32[264,128]{1,0:T(8,128)S(1)}, u32[]{:S(2)}, u32[]{:S(2)}) collective-permute-start(f32[264,128]{1,0:T(8,128)S(1)} %add.12.refs_0_), channel_id=1, source_target_pairs={{0,64},{1,65},{2,66},{3,67},{4,68},{5,69},{6,70},{7,71},{8,72},{9,... | collective-permute-start | bytes 405512 | tf_op jit(solution)/shard_map/ppermute | solution.py:394
  21.0 7.5 %collective-permute-start.3 = (f32[264,128]{1,0:T(8,128)S(1)}, f32[264,128]{1,0:T(8,128)S(1)}, u32[]{:S(2)}, u32[]{:S(2)}) collective-permute-start(f32[264,128]{1,0:T(8,128)S(1)} %add.12.refs_0_), channel_id=1, source_target_pairs={{0,32},{1,33},{2,34},{3,35},{4,36},{5,37},{6,38},{7,39},{8,40},{9,... | collective-permute-start | bytes 405512 | tf_op jit(solution)/shard_map/ppermute | solution.py:394
  31.5 5.8 %copy-start.2 = (f32[512]{0:T(512)S(1)}, f32[512]{0:T(512)}, u32[]{:S(2)}) copy-start(f32[512]{0:T(512)} %param.7) | copy-start | bytes 6148
  32.8 22.3 %collective-permute-start.7 = (f32[128,3072]{1,0:T(8,128)S(1)}, f32[128,3072]{1,0:T(8,128)S(1)}, u32[]{:S(2)}, u32[]{:S(2)}) collective-permute-start(f32[128,3072]{1,0:T(8,128)S(1)} %get-tuple-element.51.k_ref.x0_ref), channel_id=1, source_target_pairs={{0,15},{1,8},{2,9},{3,10},{4,11},{5,12},{6,13},{7,14},{16,31},{17,... | collective-permute-start | bytes 4718600 | tf_op jit(solution)/shard_map/ppermute | solution.py:394
  37.2 23.5 %collective-permute-start.6 = (f32[128,3072]{1,0:T(8,128)S(1)}, f32[128,3072]{1,0:T(8,128)S(1)}, u32[]{:S(2)}, u32[]{:S(2)}) collective-permute-start(f32[128,3072]{1,0:T(8,128)S(1)} %get-tuple-element.52.s1_ref.x1_ref), channel_id=1, source_target_pairs={{0,8},{1,9},{2,10},{3,11},{4,12},{5,13},{6,14},{7,15},{8,1},{9,2},... | collective-permute-start | bytes 4718600 | tf_op jit(solution)/shard_map/ppermute | solution.py:394
  37.3 17.8 %collective-permute-start = (f32[1,512]{1,0:T(1,128)S(1)}, f32[1,512]{1,0:T(1,128)S(1)}, u32[]{:S(2)}, u32[]{:S(2)}) collective-permute-start(f32[1,512]{1,0:T(1,128)S(1)} %bitcast.8), channel_id=1, source_target_pairs={{0,7},{1,0},{2,1},{3,2},{4,3},{5,4},{6,5},{7,6},{8,15},{9,8},{10,9... | collective-permute-start | bytes 6152 | tf_op jit(solution)/shard_map/ppermute | solution.py:394
  61.5 4.3 %collective-permute-start.8 = (f32[128,128]{1,0:T(8,128)S(1)}, f32[128,128]{1,0:T(8,128)S(1)}, u32[]{:S(2)}, u32[]{:S(2)}) collective-permute-start(f32[128,128]{1,0:T(8,128)S(1)} %gram_cross.1), channel_id=1, source_target_pairs={{0,16},{1,17},{2,18},{3,19},{4,20},{5,21},{6,22},{7,23},{8,24},{9,... | collective-permute-start | bytes 196616 | tf_op jit(solution)/shard_map/ppermute | solution.py:394
  62.1 8.4 %collective-permute-start.12 = (f32[128,128]{1,0:T(8,128)S(1)}, f32[128,128]{1,0:T(8,128)S(1)}, u32[]{:S(2)}, u32[]{:S(2)}) collective-permute-start(f32[128,128]{1,0:T(8,128)S(1)} %get-tuple-element.54), channel_id=1, source_target_pairs={{0,8},{1,9},{2,10},{3,11},{4,12},{5,13},{6,14},{7,15},{8,1},{9,2},... | collective-permute-start | bytes 196616 | tf_op jit(solution)/shard_map/ppermute | solution.py:394
  65.8 6.3 %collective-permute-start.11 = (f32[128,128]{1,0:T(8,128)S(1)}, f32[128,128]{1,0:T(8,128)S(1)}, u32[]{:S(2)}, u32[]{:S(2)}) collective-permute-start(f32[128,128]{1,0:T(8,128)S(1)} %add.13.refs_0_), channel_id=1, source_target_pairs={{0,96},{1,97},{2,98},{3,99},{4,100},{5,101},{6,102},{7,103},{8,104... | collective-permute-start | bytes 196616 | tf_op jit(solution)/shard_map/ppermute | solution.py:394
  69.6 5.8 %collective-permute-start.10 = (f32[128,128]{1,0:T(8,128)S(1)}, f32[128,128]{1,0:T(8,128)S(1)}, u32[]{:S(2)}, u32[]{:S(2)}) collective-permute-start(f32[128,128]{1,0:T(8,128)S(1)} %add.13.refs_0_), channel_id=1, source_target_pairs={{0,64},{1,65},{2,66},{3,67},{4,68},{5,69},{6,70},{7,71},{8,72},{9,... | collective-permute-start | bytes 196616 | tf_op jit(solution)/shard_map/ppermute | solution.py:394
  69.6 5.8 %collective-permute-start.9 = (f32[128,128]{1,0:T(8,128)S(1)}, f32[128,128]{1,0:T(8,128)S(1)}, u32[]{:S(2)}, u32[]{:S(2)}) collective-permute-start(f32[128,128]{1,0:T(8,128)S(1)} %add.13.refs_0_), channel_id=1, source_target_pairs={{0,32},{1,33},{2,34},{3,35},{4,36},{5,37},{6,38},{7,39},{8,40},{9,... | collective-permute-start | bytes 196616 | tf_op jit(solution)/shard_map/ppermute | solution.py:394
  77.4 7.6 %collective-permute-start.14 = (f32[128,3072]{1,0:T(8,128)S(1)}, f32[128,3072]{1,0:T(8,128)S(1)}, u32[]{:S(2)}, u32[]{:S(2)}) collective-permute-start(f32[128,3072]{1,0:T(8,128)S(1)} %given.2), channel_id=1, source_target_pairs={{8,0},{9,1},{10,2},{11,3},{12,4},{13,5},{14,6},{15,7},{24,16},{25,... | collective-permute-start | bytes 4718600 | tf_op jit(solution)/shard_map/ppermute | solution.py:394
  78.7 6.3 %collective-permute-start.13 = (f32[128,256]{1,0:T(8,128)S(1)}, f32[128,256]{1,0:T(8,128)S(1)}, u32[]{:S(2)}, u32[]{:S(2)}) collective-permute-start(f32[128,256]{1,0:T(8,128)S(1)} %get-tuple-element.55.w_ref), channel_id=1, source_target_pairs={{0,15},{1,8},{2,9},{3,10},{4,11},{5,12},{6,13},{7,14},{16,31},{17,... | collective-permute-start | bytes 393224 | tf_op jit(solution)/shard_map/ppermute | solution.py:394
  84.0 11.1 %collective-permute-start.19 = (f32[128,384]{1,0:T(8,128)S(1)}, f32[128,384]{1,0:T(8,128)S(1)}, u32[]{:S(2)}, u32[]{:S(2)}) collective-permute-start(f32[128,384]{1,0:T(8,128)S(1)} %get-tuple-element.63), channel_id=1, source_target_pairs={{0,15},{1,8},{2,9},{3,10},{4,11},{5,12},{6,13},{7,14},{8,0},{9,1},... | collective-permute-start | bytes 589832 | tf_op jit(solution)/shard_map/ppermute | solution.py:394
  85.8 4.3 %collective-permute-start.15 = (f32[128,128]{1,0:T(8,128)S(1)}, f32[128,128]{1,0:T(8,128)S(1)}, u32[]{:S(2)}, u32[]{:S(2)}) collective-permute-start(f32[128,128]{1,0:T(8,128)S(1)} %get-tuple-element.62), channel_id=1, source_target_pairs={{0,16},{1,17},{2,18},{3,19},{4,20},{5,21},{6,22},{7,23},{8,24},{9,... | collective-permute-start | bytes 196616 | tf_op jit(solution)/shard_map/ppermute | solution.py:394
  90.2 6.2 %collective-permute-start.18 = (f32[128,128]{1,0:T(8,128)S(1)}, f32[128,128]{1,0:T(8,128)S(1)}, u32[]{:S(2)}, u32[]{:S(2)}) collective-permute-start(f32[128,128]{1,0:T(8,128)S(1)} %add.14.refs_0_), channel_id=1, source_target_pairs={{0,96},{1,97},{2,98},{3,99},{4,100},{5,101},{6,102},{7,103},{8,104... | collective-permute-start | bytes 196616 | tf_op jit(solution)/shard_map/ppermute | solution.py:394
  92.4 6.3 %collective-permute-start.17 = (f32[128,128]{1,0:T(8,128)S(1)}, f32[128,128]{1,0:T(8,128)S(1)}, u32[]{:S(2)}, u32[]{:S(2)}) collective-permute-start(f32[128,128]{1,0:T(8,128)S(1)} %add.14.refs_0_), channel_id=1, source_target_pairs={{0,64},{1,65},{2,66},{3,67},{4,68},{5,69},{6,70},{7,71},{8,72},{9,... | collective-permute-start | bytes 196616 | tf_op jit(solution)/shard_map/ppermute | solution.py:394
  92.5 6.1 %collective-permute-start.16 = (f32[128,128]{1,0:T(8,128)S(1)}, f32[128,128]{1,0:T(8,128)S(1)}, u32[]{:S(2)}, u32[]{:S(2)}) collective-permute-start(f32[128,128]{1,0:T(8,128)S(1)} %add.14.refs_0_), channel_id=1, source_target_pairs={{0,32},{1,33},{2,34},{3,35},{4,36},{5,37},{6,38},{7,39},{8,40},{9,... | collective-permute-start | bytes 196616 | tf_op jit(solution)/shard_map/ppermute | solution.py:394
  94.3 15.4 %collective-permute-start.21 = (f32[128,3072]{1,0:T(8,128)S(1)}, f32[128,3072]{1,0:T(8,128)S(1)}, u32[]{:S(2)}, u32[]{:S(2)}) collective-permute-start(f32[128,3072]{1,0:T(8,128)S(1)} %given.2), channel_id=1, source_target_pairs={{8,15},{9,8},{10,9},{11,10},{12,11},{13,12},{14,13},{15,14},{24,31... | collective-permute-start | bytes 4718600 | tf_op jit(solution)/shard_map/ppermute | solution.py:394
  100.6 11.4 %collective-permute-start.22 = (f32[128,3072]{1,0:T(8,128)S(1)}, f32[128,3072]{1,0:T(8,128)S(1)}, u32[]{:S(2)}, u32[]{:S(2)}) collective-permute-start(f32[128,3072]{1,0:T(8,128)S(1)} %given.3), channel_id=1, source_target_pairs={{8,0},{9,1},{10,2},{11,3},{12,4},{13,5},{14,6},{15,7},{24,16},{25,... | collective-permute-start | bytes 4718600 | tf_op jit(solution)/shard_map/ppermute | solution.py:394
  101.9 10.1 %collective-permute-start.20 = (f32[128,256]{1,0:T(8,128)S(1)}, f32[128,256]{1,0:T(8,128)S(1)}, u32[]{:S(2)}, u32[]{:S(2)}) collective-permute-start(f32[128,256]{1,0:T(8,128)S(1)} %get-tuple-element.65.w_ref), channel_id=1, source_target_pairs={{0,15},{1,8},{2,9},{3,10},{4,11},{5,12},{6,13},{7,14},{16,31},{17,... | collective-permute-start | bytes 393224 | tf_op jit(solution)/shard_map/ppermute | solution.py:394
  109.4 13.3 %collective-permute-start.27 = (f32[128,384]{1,0:T(8,128)S(1)}, f32[128,384]{1,0:T(8,128)S(1)}, u32[]{:S(2)}, u32[]{:S(2)}) collective-permute-start(f32[128,384]{1,0:T(8,128)S(1)} %get-tuple-element.74), channel_id=1, source_target_pairs={{0,15},{1,8},{2,9},{3,10},{4,11},{5,12},{6,13},{7,14},{8,0},{9,1},... | collective-permute-start | bytes 589832 | tf_op jit(solution)/shard_map/ppermute | solution.py:394
  112.8 5.7 %collective-permute-start.23 = (f32[128,128]{1,0:T(8,128)S(1)}, f32[128,128]{1,0:T(8,128)S(1)}, u32[]{:S(2)}, u32[]{:S(2)}) collective-permute-start(f32[128,128]{1,0:T(8,128)S(1)} %get-tuple-element.73), channel_id=1, source_target_pairs={{0,16},{1,17},{2,18},{3,19},{4,20},{5,21},{6,22},{7,23},{8,24},{9,... | collective-permute-start | bytes 196616 | tf_op jit(solution)/shard_map/ppermute | solution.py:394
  118.5 5.6 %collective-permute-start.26 = (f32[128,128]{1,0:T(8,128)S(1)}, f32[128,128]{1,0:T(8,128)S(1)}, u32[]{:S(2)}, u32[]{:S(2)}) collective-permute-start(f32[128,128]{1,0:T(8,128)S(1)} %add.15.refs_0_), channel_id=1, source_target_pairs={{0,96},{1,97},{2,98},{3,99},{4,100},{5,101},{6,102},{7,103},{8,104... | collective-permute-start | bytes 196616 | tf_op jit(solution)/shard_map/ppermute | solution.py:394
  120.6 5.8 %collective-permute-start.25 = (f32[128,128]{1,0:T(8,128)S(1)}, f32[128,128]{1,0:T(8,128)S(1)}, u32[]{:S(2)}, u32[]{:S(2)}) collective-permute-start(f32[128,128]{1,0:T(8,128)S(1)} %add.15.refs_0_), channel_id=1, source_target_pairs={{0,64},{1,65},{2,66},{3,67},{4,68},{5,69},{6,70},{7,71},{8,72},{9,... | collective-permute-start | bytes 196616 | tf_op jit(solution)/shard_map/ppermute | solution.py:394
  121.7 4.6 %collective-permute-start.24 = (f32[128,128]{1,0:T(8,128)S(1)}, f32[128,128]{1,0:T(8,128)S(1)}, u32[]{:S(2)}, u32[]{:S(2)}) collective-permute-start(f32[128,128]{1,0:T(8,128)S(1)} %add.15.refs_0_), channel_id=1, source_target_pairs={{0,32},{1,33},{2,34},{3,35},{4,36},{5,37},{6,38},{7,39},{8,40},{9,... | collective-permute-start | bytes 196616 | tf_op jit(solution)/shard_map/ppermute | solution.py:394
  129.4 10.4 %collective-permute-start.28 = (f32[128,3072]{1,0:T(8,128)S(1)}, f32[128,3072]{1,0:T(8,128)S(1)}, u32[]{:S(2)}, u32[]{:S(2)}) collective-permute-start(f32[128,3072]{1,0:T(8,128)S(1)} %get-tuple-element.78), channel_id=1, source_target_pairs={{0,8},{1,9},{2,10},{3,11},{4,12},{5,13},{6,14},{7,15},{8,0},{9,1},... | collective-permute-start | bytes 4718600 | tf_op jit(solution)/shard_map/ppermute | solution.py:394

commit v4 on v3

--- a/solution.py
+++ b/solution.py
@@ -7,7 +7,6 @@
 from jax.experimental.pallas import tpu as pltpu
 from jax.sharding import Mesh, PartitionSpec as P
 
-ROUNDS = 4
 BW = 128
 PW = 2 * BW
 RH = 1536
@@ -28,7 +27,7 @@
 
 
 def cost(flops, moved):
-    return pl.CostEstimate(flops=flops, bytes_accessed=moved, transcendentals=0)
+    return pl.CostEstimate(flops=flops * 30, bytes_accessed=moved, transcendentals=0)
 
 
 def split(x):
@@ -197,11 +196,23 @@
 PLAIN = (False, False)
 
 
+PIECES = (RB,)
+
+
+def rows_of(x_ref, at):
+    if isinstance(x_ref, list):
+        for piece in x_ref:
+            if at < piece.shape[1]:
+                return piece[:, at : at + CH]
+            at -= piece.shape[1]
+    return x_ref[:, at : at + CH]
+
+
 def columns(x_refs, form, half, j):
     if form == HALVES:
         return x_refs[half][:, j : j + CH]
     ats = [((1 - half) if crossed else half) * RH + j for crossed in form]
-    return jnp.concatenate([x_ref[:, at : at + CH] for x_ref, at in zip(x_refs, ats)], axis=0)
+    return jnp.concatenate([rows_of(x_ref, at) for x_ref, at in zip(x_refs, ats)], axis=0)
 
 
 def apply_to(w, x_refs, form, out_ref, offset=None):
@@ -238,16 +249,18 @@
     )(*args)
 
 
-def whiten_kernel(moves, *refs):
-    n = 4 if moves else 6
+def whiten_kernel(first_round, *refs):
+    n = 4 if first_round else 6
     g_refs, diag_refs = refs[:4], refs[4:n]
     first_ref, second_ref, z_ref, y_ref, t_ref, d_ref = refs[-6:]
     z, y, t, d_col, d_row, inv_row, fro = newton(gram_of(g_refs, diag_refs))
     wt = jnp.sqrt(d_col) * z.T * (inv_row / jnp.sqrt(fro))
-    first_ref[...] = wt[:BW]
-    second_ref[...] = wt[BW:]
-    if moves:
-        apply_to(wt[BW:], refs[n : n + 2], HALVES, refs[n + 2])
+    if first_round:
+        apply_to(wt[BW:], refs[n : n + 2], HALVES, second_ref)
+        apply_to(wt[:BW], refs[n : n + 2], HALVES, first_ref)
+    else:
+        first_ref[...] = wt[:BW]
+        second_ref[...] = wt[BW:]
     z_ref[...] = z
     y_ref[...] = y
     t_ref[...] = t
@@ -255,12 +268,11 @@
     d_ref[...] = jnp.concatenate([root[:BW, :BW], root[BW:, BW:]], axis=0)
 
 
-def whiten(grams, diags, xs=()):
-    args = [*grams, *diags, *xs]
-    outs = [ROWS_OF_W, ROWS_OF_W, SQUARE, SQUARE, SQUARE, SCALES]
-    if xs:
-        outs = [BLOCK] + outs
-    return call(functools.partial(whiten_kernel, bool(xs)), [VMEM] * len(args), outs, "whiten", args)
+def whiten(grams, diags, xs=(), arrived=()):
+    args = [*grams, *diags, *xs, *arrived]
+    ins = [VMEM] * (len(args) - len(arrived)) + [ANY] * len(arrived)
+    outs = [BLOCK if xs else ROWS_OF_W] * 2 + [SQUARE, SQUARE, SQUARE, SCALES]
+    return call(functools.partial(whiten_kernel, bool(xs)), ins, outs, "whiten", args)
 
 
 def next_diagonals(z_ref, y_ref, t_ref, d_ref):
@@ -269,13 +281,12 @@
     return new[:BW, :BW] * d_ref[:BW], new[BW:, BW:] * d_ref[BW:]
 
 
-def kept_first_kernel(w_ref, z_ref, y_ref, t_ref, d_ref, x0_ref, x1_ref, kept_ref, diag0_ref, diag1_ref):
-    apply_to(w_ref[...], (x0_ref, x1_ref), HALVES, kept_ref)
+def diagonals_kernel(z_ref, y_ref, t_ref, d_ref, diag0_ref, diag1_ref):
     diag0_ref[...], diag1_ref[...] = next_diagonals(z_ref, y_ref, t_ref, d_ref)
 
 
-def kept_first(*args):
-    return call(kept_first_kernel, [VMEM] * 7, [BLOCK, DIAGONAL, DIAGONAL], "kept_first", args)
+def diagonals(*args):
+    return call(diagonals_kernel, [VMEM] * 4, [DIAGONAL, DIAGONAL], "diagonals", args)
 
 
 def kept_second_kernel(form, w_ref, z_ref, y_ref, t_ref, d_ref, x0_ref, x1_ref, kept_ref, diag_ref, more_ref):
@@ -290,18 +301,25 @@
     return call(kernel, [VMEM] * 7, [BLOCK, DIAGONAL, more], "kept_second", args)
 
 
-def on_second_core_kernel(form, core_ref, w_ref, x0_ref, x1_ref, out_ref):
+def on_second_core_kernel(form, core_ref, w_ref, x0_ref, x1_ref, out_ref, *piece_refs):
     @pl.when(core_ref[0] != 0)
     def _():
         apply_to(w_ref[...], (x0_ref, x1_ref), form, out_ref)
-
-
-def on_second_core(form, core, w, xs, name):
+        at = 0
+        for piece_ref in piece_refs:
+            piece_ref[...] = out_ref[:, at : at + piece_ref.shape[1]]
+            at += piece_ref.shape[1]
+
+
+def on_second_core(form, core, w, xs, name, pieces=()):
     kernel = functools.partial(on_second_core_kernel, form)
-    return call(kernel, [SMEM] + [VMEM] * 3, [BLOCK], name, [core, w, *xs])[0]
-
-
-def combine_kernel(form, core_ref, w_ref, s0_ref, s1_ref, other_ref, kept_ref, *refs):
+    outs = [BLOCK] + [jax.ShapeDtypeStruct((BW, piece), F32) for piece in pieces]
+    return call(kernel, [SMEM] + [VMEM] * 3, outs, name, [core, w, *xs])
+
+
+def combine_kernel(form, n, core_ref, w_ref, *refs):
+    s0_ref = list(refs[:n])
+    s1_ref, other_ref, kept_ref = refs[n : n + 3]
     in_ref, out_ref = refs[-2:]
 
     @pl.when(core_ref[0] == 0)
@@ -321,10 +339,12 @@
     out_ref[...] = (total[:BW, :BW] + total[BW:, BW:]) + (total[:BW, BW:] + total[BW:, :BW])
 
 
-def combine(form, core, w, shadow, other, kept):
-    kernel = functools.partial(combine_kernel, form)
-    args = [core, w, *shadow, other, kept]
-    return call(kernel, [SMEM] + [VMEM] * 5, [BLOCK, DIAGONAL], "combine", args)
+def combine(form, core, w, shadow, other, kept, *arrived):
+    pieces, second = shadow
+    kernel = functools.partial(combine_kernel, form, len(pieces))
+    args = [core, w, *pieces, second, other, kept, *arrived]
+    ins = [SMEM] + [VMEM] * (len(pieces) + 4) + [ANY] * len(arrived)
+    return call(kernel, ins, [BLOCK, DIAGONAL], "combine", args)
 
 
 def by_core(w, even):
@@ -425,26 +445,33 @@
     keep, send = fill(core, observed, estimate, mask)
     got = swap_cores(send)
     grams = reduced(gram_second(got, *gram_first(keep)))
-    second, w0, _, *rest = whiten(grams, [], (keep, got))
+    first, second, *rest = whiten(grams, [], (keep, got))
     joined = onward(second)
-    first, diag0, diag1 = kept_first(w0, *rest, keep, got)
-    shadow, shadow_form = (behind(first, 0), second), SHADOW
+    back = behind(first, 0)
+    diag0, diag1 = diagonals(*rest)
     diags = [diag0, onward(diag1)]
-    xs, form = (first, joined), CROSSED
-    partial = gram_cross(first, joined, shadow[0], thr)
-    for round_index in range(1, ROUNDS - 1):
-        w0, w1, *rest = whiten(reduced(partial), diags)
-        w_shadow = behind(w0, 0)
-        given = on_second_core(form, core, w0, xs, "given")
-        other = beside(given)
-        kept, diag1, more = kept_second(form, w1, *rest, *xs)
-        more = backward(more)
-        joined, partial = combine(shadow_form, core, w_shadow, shadow, other, kept)
-        diags = [more[:, :BW], diag1]
-        xs, form = (joined, kept), PLAIN
-        if round_index + 2 < ROUNDS:
-            moved = on_second_core(shadow_form, core, more[:, BW:], shadow, "shadow")
-            shadow, shadow_form = (to(given, lambda i, c, g: (i, 1, (g - 1) % 8) if c == 1 else None), moved), PLAIN
+    partial = gram_cross(first, joined, back, thr)
+    xs = (first, joined)
+    w0, w1, *rest = whiten(reduced(partial), diags)
+    w_shadow = behind(w0, 0)
+    (given,) = on_second_core(CROSSED, core, w0, xs, "given")
+    other = beside(given)
+    pieces = [behind(given, 1)]
+    kept, diag1, more = kept_second(CROSSED, w1, *rest, *xs)
+    more = backward(more)
+    joined, partial = combine(SHADOW, core, w_shadow, ([back], second), other, kept)
+    (moved,) = on_second_core(SHADOW, core, more[:, BW:], (back, second), "shadow")
+    diags = [more[:, :BW], diag1]
+    xs = (joined, kept)
+    w0, w1, *rest = whiten(reduced(partial), diags)
+    w_shadow = behind(w0, 0)
+    (given,) = on_second_core(PLAIN, core, w0, xs, "given")
+    other = beside(given)
+    kept, diag1, more = kept_second(PLAIN, w1, *rest, *xs)
+    more = backward(more)
+    joined, partial = combine(PLAIN, core, w_shadow, (pieces, moved), other, kept)
+    diags = [more[:, :BW], diag1]
+    xs = (joined, kept)
     send, w = last(core, thr, reduced(partial), diags, xs)
     got = swap_cores(send)
     packed = last_kept(core, w, xs, got).reshape(64, 4, RB)

time: 199 us -> 187 us (0.940)
  waiting for transfers between devices: 63.3 us -> 53.2 us
    ppermute x29, waiting for transfers between devices: 63.3 us -> 53.2 us  [to(): return lax.ppermute(block, AXES, route)]
  transfers between devices with their start and end apart: 29 -> 29, of which waited for: 18 -> 20; matrix products, arithmetic and copies ran while one was open for 0% -> 0% of each run, Pallas kernels for 3% -> 4%
where the time goes in v4:
time: 187 us
  waiting for transfers between devices  53.2 us (28%)
  blocking collectives  50.3 us (27%)
  starting transfers between devices  49.5 us (26%)
  Pallas kernels  25.3 us (14%)
  local copies, waits for them, and re-layouts  5.91 us (3%)
  other arithmetic  2.34 us (1%)
    ppermute x29, waiting for transfers between devices, to(): return lax.ppermute(block, AXES, route)  53.2 us
    all_to_all x1, blocking collectives, on_device(): lax.all_to_all(packed, ('zx', 'pairs'), split_axis=0, concat_axis=0, tile...  50.3 us
    ppermute x29, starting transfers between devices, to(): return lax.ppermute(block, AXES, route)  49.5 us
    pallas_call x11, Pallas kernels, call(): pl.pallas_call(kernel, in_specs=ins, out_specs=[VMEM] * len(outs), out_sh...  12.4 us
    pallas_call x1, Pallas kernels, fill(): pl.pallas_call(fill_kernel, grid=(RH // step,), in_specs=[SMEM, rows, row...  6.72 us
  transfers between devices with their start and end apart: 29, of which 20 were waited for; matrix products, arithmetic and copies ran while one was open for 0% of the time, Pallas kernels for 4%

profile of v4, /device:TPU:0, one launch (start us, length us, event | category | flops | bytes accessed | tf_op | source)
XLA Modules:
  0.0 186.8 jit_solution(6636027366481889893)
XLA Ops:
  0.0 6.7 %fill.1 = (f32[256,1536]{1,0:T(8,128)}, f32[256,1536]{1,0:T(8,128)}) custom-call(s32[1]{0:T(128)} %bitcast.core_ref, f32[1536,512]{1,0:T(8,128)} %obs_ref.1, f32[1536,512]{1,0:T(8,128)} %est_ref.1, s32[1536,512]{1,0:T(8,128)} %mask_ref.1), custom_call_target="tpu_custom_call" | custom-call | flops 30000000 | bytes 15000000 | tf_op jit(solution)/shard_map/fill/pallas_call | solution.py:60
  6.7 1.4 copy-done
  8.1 0.6 gram_first.1
  8.8 1.6 collective-permute-done.1.x_ref.refs_5_
  10.3 0.7 gram_second.1
  11.0 1.6 collective-permute-start.2
  12.7 4.0 %collective-permute-done.2 = f32[264,128]{1,0:T(8,128)S(1)} collective-permute-done((f32[264,128]{1,0:T(8,128)S(1)}, f32[264,128]{1,0:T(8,128)S(1)}, u32[]{:S(2)}, u32[]{:S(2)}) %collective-permute-start.2) | collective-permute-done | bytes 135200 | tf_op jit(solution)/shard_map/ppermute | solution.py:414
  16.8 4.2 %collective-permute-start.5 = (f32[264,128]{1,0:T(8,128)S(1)}, f32[264,128]{1,0:T(8,128)S(1)}, u32[]{:S(2)}, u32[]{:S(2)}) collective-permute-start(f32[264,128]{1,0:T(8,128)S(1)} %add.12.refs_0_), channel_id=1, source_target_pairs={{0,96},{1,97},{2,98},{3,99},{4,100},{5,101},{6,102},{7,103},{8,104... | collective-permute-start | bytes 405512 | tf_op jit(solution)/shard_map/ppermute | solution.py:414
  21.0 0.9 collective-permute-start.3
  21.9 4.3 %collective-permute-done.5.refs_3_ = f32[264,128]{1,0:T(8,128)S(1)} collective-permute-done((f32[264,128]{1,0:T(8,128)S(1)}, f32[264,128]{1,0:T(8,128)S(1)}, u32[]{:S(2)}, u32[]{:S(2)}) %collective-permute-start.5) | collective-permute-done | bytes 135200 | tf_op jit(solution)/shard_map/ppermute | solution.py:414
  26.2 2.2 %collective-permute-done.4.refs_2_ = f32[264,128]{1,0:T(8,128)S(1)} collective-permute-done((f32[264,128]{1,0:T(8,128)S(1)}, f32[264,128]{1,0:T(8,128)S(1)}, u32[]{:S(2)}, u32[]{:S(2)}) %collective-permute-start.4) | collective-permute-done | bytes 135200 | tf_op jit(solution)/shard_map/ppermute | solution.py:414
  28.5 3.6 %whiten.3 = (f32[128,3072]{1,0:T(8,128)S(1)}, f32[128,3072]{1,0:T(8,128)S(1)}, f32[256,256]{1,0:T(8,128)S(1)}, f32[256,256]{1,0:T(8,128)S(1)}, f32[256,256]{1,0:T(8,128)S(1)}, /*index=5*/f32[256,128]{1,0:T(8,128)S(1)}) custom-call(f32[264,128]{1,0:T(8,128)S(1)} %add.12.refs_0_, f32[264,128]{1,0:T(8,128)S(1)} %collective-permute-done.3.refs_1_, ...), custom_call_target="tpu_custom_call" | custom-call | flops 30000001024 | bytes 6000000 | tf_op jit(solution)/shard_map/whiten/pallas_call | solution.py:241
  32.2 7.3 %collective-permute-start.7 = (f32[128,3072]{1,0:T(8,128)S(1)}, f32[128,3072]{1,0:T(8,128)S(1)}, u32[]{:S(2)}, u32[]{:S(2)}) collective-permute-start(f32[128,3072]{1,0:T(8,128)S(1)} %get-tuple-element.45.k_ref.x0_ref), channel_id=1, source_target_pairs={{0,15},{1,8},{2,9},{3,10},{4,11},{5,12},{6,13},{7,14},{16,31},{17,... | collective-permute-start | bytes 4718600 | tf_op jit(solution)/shard_map/ppermute | solution.py:414
  39.5 1.9 %collective-permute-start = (f32[1,512]{1,0:T(1,128)S(1)}, f32[1,512]{1,0:T(1,128)S(1)}, u32[]{:S(2)}, u32[]{:S(2)}) collective-permute-start(f32[1,512]{1,0:T(1,128)S(1)} %bitcast.8), channel_id=1, source_target_pairs={{0,7},{1,0},{2,1},{3,2},{4,3},{5,4},{6,5},{7,6},{8,15},{9,8},{10,9... | collective-permute-start | bytes 6152 | tf_op jit(solution)/shard_map/ppermute | solution.py:414
  41.5 15.9 %collective-permute-done.refs_1_.thr_ref = f32[1,512]{1,0:T(1,128)S(1)} collective-permute-done((f32[1,512]{1,0:T(1,128)S(1)}, f32[1,512]{1,0:T(1,128)S(1)}, u32[]{:S(2)}, u32[]{:S(2)}) %collective-permute-start) | collective-permute-done | bytes 2080 | tf_op jit(solution)/shard_map/ppermute | solution.py:414
  57.4 0.7 gram_cross.1
  58.1 1.6 collective-permute-start.8
  59.8 0.6 diagonals.1
  60.5 2.0 %collective-permute-done.8 = f32[128,128]{1,0:T(8,128)S(1)} collective-permute-done((f32[128,128]{1,0:T(8,128)S(1)}, f32[128,128]{1,0:T(8,128)S(1)}, u32[]{:S(2)}, u32[]{:S(2)}) %collective-permute-start.8) | collective-permute-done | bytes 65568 | tf_op jit(solution)/shard_map/ppermute | solution.py:414
  62.5 2.1 %collective-permute-start.11 = (f32[128,128]{1,0:T(8,128)S(1)}, f32[128,128]{1,0:T(8,128)S(1)}, u32[]{:S(2)}, u32[]{:S(2)}) collective-permute-start(f32[128,128]{1,0:T(8,128)S(1)} %add.13.refs_0_), channel_id=1, source_target_pairs={{0,96},{1,97},{2,98},{3,99},{4,100},{5,101},{6,102},{7,103},{8,104... | collective-permute-start | bytes 196616 | tf_op jit(solution)/shard_map/ppermute | solution.py:414
  64.6 0.3 collective-permute-start.10
  64.9 1.8 collective-permute-start.9
  66.7 1.7 collective-permute-done.12.refs_5_
  68.4 2.0 %collective-permute-done.10.refs_2_ = f32[128,128]{1,0:T(8,128)S(1)} collective-permute-done((f32[128,128]{1,0:T(8,128)S(1)}, f32[128,128]{1,0:T(8,128)S(1)}, u32[]{:S(2)}, u32[]{:S(2)}) %collective-permute-start.10) | collective-permute-done | bytes 65568 | tf_op jit(solution)/shard_map/ppermute | solution.py:414
  70.3 1.9 %whiten.4 = (f32[128,256]{1,0:T(8,128)S(1)}, f32[128,256]{1,0:T(8,128)S(1)}, f32[256,256]{1,0:T(8,128)S(1)}, f32[256,256]{1,0:T(8,128)S(1)}, f32[256,256]{1,0:T(8,128)S(1)}, /*index=5*/f32[256,128]{1,0:T(8,128)S(1)}) custom-call(f32[128,128]{1,0:T(8,128)S(1)} %add.13.refs_0_, f32[128,128]{1,0:T(8,128)S(1)} %collective-permute-done.9.refs_1_, ...), custom_call_target="tpu_custom_call" | custom-call | flops 30000001024 | bytes 6000000 | tf_op jit(solution)/shard_map/whiten/pallas_call | solution.py:241
  72.3 5.2 %collective-permute-start.13 = (f32[128,256]{1,0:T(8,128)S(1)}, f32[128,256]{1,0:T(8,128)S(1)}, u32[]{:S(2)}, u32[]{:S(2)}) collective-permute-start(f32[128,256]{1,0:T(8,128)S(1)} %get-tuple-element.53.w_ref), channel_id=1, source_target_pairs={{0,15},{1,8},{2,9},{3,10},{4,11},{5,12},{6,13},{7,14},{16,31},{17,... | collective-permute-start | bytes 393224 | tf_op jit(solution)/shard_map/ppermute | solution.py:414
  77.5 1.5 collective-permute-start.14
  79.0 1.3 kept_second.2
  80.3 3.8 %collective-permute-start.19 = (f32[128,384]{1,0:T(8,128)S(1)}, f32[128,384]{1,0:T(8,128)S(1)}, u32[]{:S(2)}, u32[]{:S(2)}) collective-permute-start(f32[128,384]{1,0:T(8,128)S(1)} %get-tuple-element.61), channel_id=1, source_target_pairs={{0,15},{1,8},{2,9},{3,10},{4,11},{5,12},{6,13},{7,14},{8,0},{9,1},... | collective-permute-start | bytes 589832 | tf_op jit(solution)/shard_map/ppermute | solution.py:414
  84.1 0.8 combine.2
  84.9 1.1 collective-permute-start.15
  86.1 0.7 collective-permute-start.21
  86.8 1.2 collective-permute-done.19
  88.0 2.2 %collective-permute-done.15 = f32[128,128]{1,0:T(8,128)S(1)} collective-permute-done((f32[128,128]{1,0:T(8,128)S(1)}, f32[128,128]{1,0:T(8,128)S(1)}, u32[]{:S(2)}, u32[]{:S(2)}) %collective-permute-start.15) | collective-permute-done | bytes 65568 | tf_op jit(solution)/shard_map/ppermute | solution.py:414
  90.2 1.3 collective-permute-start.18
  91.5 1.4 collective-permute-start.17
  92.9 1.4 collective-permute-start.16
  94.4 2.8 %collective-permute-done.18.refs_3_ = f32[128,128]{1,0:T(8,128)S(1)} collective-permute-done((f32[128,128]{1,0:T(8,128)S(1)}, f32[128,128]{1,0:T(8,128)S(1)}, u32[]{:S(2)}, u32[]{:S(2)}) %collective-permute-start.18) | collective-permute-done | bytes 65568 | tf_op jit(solution)/shard_map/ppermute | solution.py:414
  97.1 0.7 collective-permute-done.17.refs_2_
  98.1 1.9 %whiten.5 = (f32[128,256]{1,0:T(8,128)S(1)}, f32[128,256]{1,0:T(8,128)S(1)}, f32[256,256]{1,0:T(8,128)S(1)}, f32[256,256]{1,0:T(8,128)S(1)}, f32[256,256]{1,0:T(8,128)S(1)}, /*index=5*/f32[256,128]{1,0:T(8,128)S(1)}) custom-call(f32[128,128]{1,0:T(8,128)S(1)} %add.14.refs_0_, f32[128,128]{1,0:T(8,128)S(1)} %collective-permute-done.16.refs_1_, ...), custom_call_target="tpu_custom_call" | custom-call | flops 30000001024 | bytes 6000000 | tf_op jit(solution)/shard_map/whiten/pallas_call | solution.py:241
  100.0 3.5 %collective-permute-start.20 = (f32[128,256]{1,0:T(8,128)S(1)}, f32[128,256]{1,0:T(8,128)S(1)}, u32[]{:S(2)}, u32[]{:S(2)}) collective-permute-start(f32[128,256]{1,0:T(8,128)S(1)} %get-tuple-element.63.w_ref), channel_id=1, source_target_pairs={{0,15},{1,8},{2,9},{3,10},{4,11},{5,12},{6,13},{7,14},{16,31},{17,... | collective-permute-start | bytes 393224 | tf_op jit(solution)/shard_map/ppermute | solution.py:414
  103.6 1.3 collective-permute-start.22
  104.9 1.3 kept_second.3
  106.2 0.5 collective-permute-start.27
  106.6 0.9 collective-permute-done.20.w_ref
  107.5 1.4 collective-permute-done.22.refs_2_
  108.9 0.8 combine.3
  109.7 1.1 collective-permute-start.23
  110.8 3.2 %collective-permute-done.23 = f32[128,128]{1,0:T(8,128)S(1)} collective-permute-done((f32[128,128]{1,0:T(8,128)S(1)}, f32[128,128]{1,0:T(8,128)S(1)}, u32[]{:S(2)}, u32[]{:S(2)}) %collective-permute-start.23) | collective-permute-done | bytes 65568 | tf_op jit(solution)/shard_map/ppermute | solution.py:414
  114.1 1.9 %collective-permute-start.26 = (f32[128,128]{1,0:T(8,128)S(1)}, f32[128,128]{1,0:T(8,128)S(1)}, u32[]{:S(2)}, u32[]{:S(2)}) collective-permute-start(f32[128,128]{1,0:T(8,128)S(1)} %add.15.refs_0_), channel_id=1, source_target_pairs={{0,96},{1,97},{2,98},{3,99},{4,100},{5,101},{6,102},{7,103},{8,104... | collective-permute-start | bytes 196616 | tf_op jit(solution)/shard_map/ppermute | solution.py:414
  116.0 1.1 collective-permute-start.25
  117.1 1.2 collective-permute-start.24
  118.3 1.4 collective-permute-done.26.refs_3_
  119.6 2.3 %collective-permute-done.25.refs_2_ = f32[128,128]{1,0:T(8,128)S(1)} collective-permute-done((f32[128,128]{1,0:T(8,128)S(1)}, f32[128,128]{1,0:T(8,128)S(1)}, u32[]{:S(2)}, u32[]{:S(2)}) %collective-permute-start.25) | collective-permute-done | bytes 65568 | tf_op jit(solution)/shard_map/ppermute | solution.py:414
  122.1 3.1 %last.1 = (f32[128,3072]{1,0:T(8,128)S(1)}, f32[128,256]{1,0:T(8,128)S(1)}) custom-call(s32[1]{0:T(128)} %bitcast.core_ref, f32[1,512]{1,0:T(1,128)S(1)} %copy-done.3, f32[128,128]{1,0:T(8,128)S(1)} %add.15.refs_0_, f32[128,128]{1,0:T(8,128)S(1)} %collective-permute-done.24.refs_1_, f32[128,128]{1,0:T(8,128)S(1)} %collective-permute-done.25.refs_2_, ...), custom_call_target="tpu_custom_call" | custom-call | flops 30000001024 | bytes 6000000 | tf_op jit(solution)/shard_map/last/pallas_call | solution.py:375
  125.2 0.4 collective-permute-start.28
  125.6 3.1 %collective-permute-done.28.got_ref = f32[128,3072]{1,0:T(8,128)S(1)} collective-permute-done((f32[128,3072]{1,0:T(8,128)S(1)}, f32[128,3072]{1,0:T(8,128)S(1)}, u32[]{:S(2)}, u32[]{:S(2)}) %collective-permute-start.28) | collective-permute-done | bytes 1572896 | tf_op jit(solution)/shard_map/ppermute | solution.py:414
  128.6 1.1 last_kept.1
  129.7 2.1 %reshape.17 = f32[64,4,3072]{2,1,0:T(4,128)} reshape(f32[256,3072]{1,0:T(8,128)S(1)} %last_kept.1) | data formatting | bytes 6291456 | tf_op jit(solution)/shard_map/reshape | solution.py:477
  131.9 50.3 %all_to_all.5 = f32[64,4,3072]{2,1,0:T(4,128)S(1)} all-to-all(f32[64,4,3072]{2,1,0:T(4,128)} %reshape.17), channel_id=1, replica_groups=mesh['zx'=8,'core'=2,'pairs'=8] {'zx','pairs'}, dimensions={0} | all-to-all | bytes 6291456 | tf_op jit(solution)/shard_map/all_to_all | solution.py:478
  182.2 0.3 slice.26
  182.5 0.4 copy.7
  182.9 1.6 copy.8
  184.5 2.3 %pad_maximum_fusion = f32[8,8,4,3072]{3,1,0,2:T(8,128)} fusion(f32[8,7,4,3072]{3,1,0,2:T(8,128)S(1)} %copy.8, f32[8,1,4,3072]{3,1,0,2:T(1,128)S(1)} %copy.7), kind=kLoop, calls=%fused_computation | loop fusion | flops 786432 | bytes 6291456 | tf_op jit(solution)/shard_map/jit(_roll_static)/concatenate | solution.py:480
  (35 shorter events, 0.7 us)
Async XLA Ops:
  6.7 3.6 %collective-permute-start.1 = (f32[256,1536]{1,0:T(8,128)}, f32[256,1536]{1,0:T(8,128)S(1)}, u32[]{:S(2)}, u32[]{:S(2)}) collective-permute-start(f32[256,1536]{1,0:T(8,128)} %get-tuple-element.41), channel_id=1, source_target_pairs={{0,8},{1,9},{2,10},{3,11},{4,12},{5,13},{6,14},{7,15},{8,0},{9,1},... | collective-permute-start | bytes 4718600 | tf_op jit(solution)/shard_map/ppermute | solution.py:414
  6.7 1.4 copy-start
  10.3 18.1 %copy-start.1 = (f32[256,1536]{1,0:T(8,128)S(1)}, f32[256,1536]{1,0:T(8,128)}, u32[]{:S(2)}) copy-start(f32[256,1536]{1,0:T(8,128)} %get-tuple-element.42.x_ref.refs_4_) | copy-start | bytes 4718596
  11.0 5.7 %collective-permute-start.2 = (f32[264,128]{1,0:T(8,128)S(1)}, f32[264,128]{1,0:T(8,128)S(1)}, u32[]{:S(2)}, u32[]{:S(2)}) collective-permute-start(f32[264,128]{1,0:T(8,128)S(1)} %gram_second.1), channel_id=1, source_target_pairs={{0,16},{1,17},{2,18},{3,19},{4,20},{5,21},{6,22},{7,23},{8,24},{9,... | collective-permute-start | bytes 405512 | tf_op jit(solution)/shard_map/ppermute | solution.py:414
  16.8 22.8 %copy-start.4 = (f32[512]{0:T(512)S(1)}, f32[512]{0:T(512)}, u32[]{:S(2)}) copy-start(f32[512]{0:T(512)} %param.7) | copy-start | bytes 6148
  16.8 9.5 %collective-permute-start.5 = (f32[264,128]{1,0:T(8,128)S(1)}, f32[264,128]{1,0:T(8,128)S(1)}, u32[]{:S(2)}, u32[]{:S(2)}) collective-permute-start(f32[264,128]{1,0:T(8,128)S(1)} %add.12.refs_0_), channel_id=1, source_target_pairs={{0,96},{1,97},{2,98},{3,99},{4,100},{5,101},{6,102},{7,103},{8,104... | collective-permute-start | bytes 405512 | tf_op jit(solution)/shard_map/ppermute | solution.py:414
  21.0 7.5 %collective-permute-start.4 = (f32[264,128]{1,0:T(8,128)S(1)}, f32[264,128]{1,0:T(8,128)S(1)}, u32[]{:S(2)}, u32[]{:S(2)}) collective-permute-start(f32[264,128]{1,0:T(8,128)S(1)} %add.12.refs_0_), channel_id=1, source_target_pairs={{0,64},{1,65},{2,66},{3,67},{4,68},{5,69},{6,70},{7,71},{8,72},{9,... | collective-permute-start | bytes 405512 | tf_op jit(solution)/shard_map/ppermute | solution.py:414
  21.0 7.5 %collective-permute-start.3 = (f32[264,128]{1,0:T(8,128)S(1)}, f32[264,128]{1,0:T(8,128)S(1)}, u32[]{:S(2)}, u32[]{:S(2)}) collective-permute-start(f32[264,128]{1,0:T(8,128)S(1)} %add.12.refs_0_), channel_id=1, source_target_pairs={{0,32},{1,33},{2,34},{3,35},{4,36},{5,37},{6,38},{7,39},{8,40},{9,... | collective-permute-start | bytes 405512 | tf_op jit(solution)/shard_map/ppermute | solution.py:414
  32.1 25.3 %collective-permute-start.6 = (f32[128,3072]{1,0:T(8,128)S(1)}, f32[128,3072]{1,0:T(8,128)S(1)}, u32[]{:S(2)}, u32[]{:S(2)}) collective-permute-start(f32[128,3072]{1,0:T(8,128)S(1)} %get-tuple-element.46.refs_1_.x1_ref), channel_id=1, source_target_pairs={{0,8},{1,9},{2,10},{3,11},{4,12},{5,13},{6,14},{7,15},{8,1},{9,2},... | collective-permute-start | bytes 4718600 | tf_op jit(solution)/shard_map/ppermute | solution.py:414
  32.2 25.2 %collective-permute-start.7 = (f32[128,3072]{1,0:T(8,128)S(1)}, f32[128,3072]{1,0:T(8,128)S(1)}, u32[]{:S(2)}, u32[]{:S(2)}) collective-permute-start(f32[128,3072]{1,0:T(8,128)S(1)} %get-tuple-element.45.k_ref.x0_ref), channel_id=1, source_target_pairs={{0,15},{1,8},{2,9},{3,10},{4,11},{5,12},{6,13},{7,14},{16,31},{17,... | collective-permute-start | bytes 4718600 | tf_op jit(solution)/shard_map/ppermute | solution.py:414
  39.5 17.8 %collective-permute-start = (f32[1,512]{1,0:T(1,128)S(1)}, f32[1,512]{1,0:T(1,128)S(1)}, u32[]{:S(2)}, u32[]{:S(2)}) collective-permute-start(f32[1,512]{1,0:T(1,128)S(1)} %bitcast.8), channel_id=1, source_target_pairs={{0,7},{1,0},{2,1},{3,2},{4,3},{5,4},{6,5},{7,6},{8,15},{9,8},{10,9... | collective-permute-start | bytes 6152 | tf_op jit(solution)/shard_map/ppermute | solution.py:414
  57.4 0.8 copy-start.2
  58.1 4.3 %collective-permute-start.8 = (f32[128,128]{1,0:T(8,128)S(1)}, f32[128,128]{1,0:T(8,128)S(1)}, u32[]{:S(2)}, u32[]{:S(2)}) collective-permute-start(f32[128,128]{1,0:T(8,128)S(1)} %gram_cross.1), channel_id=1, source_target_pairs={{0,16},{1,17},{2,18},{3,19},{4,20},{5,21},{6,22},{7,23},{8,24},{9,... | collective-permute-start | bytes 196616 | tf_op jit(solution)/shard_map/ppermute | solution.py:414
  60.4 8.0 %collective-permute-start.12 = (f32[128,128]{1,0:T(8,128)S(1)}, f32[128,128]{1,0:T(8,128)S(1)}, u32[]{:S(2)}, u32[]{:S(2)}) collective-permute-start(f32[128,128]{1,0:T(8,128)S(1)} %get-tuple-element.52), channel_id=1, source_target_pairs={{0,8},{1,9},{2,10},{3,11},{4,12},{5,13},{6,14},{7,15},{8,1},{9,2},... | collective-permute-start | bytes 196616 | tf_op jit(solution)/shard_map/ppermute | solution.py:414
  62.5 5.9 %collective-permute-start.11 = (f32[128,128]{1,0:T(8,128)S(1)}, f32[128,128]{1,0:T(8,128)S(1)}, u32[]{:S(2)}, u32[]{:S(2)}) collective-permute-start(f32[128,128]{1,0:T(8,128)S(1)} %add.13.refs_0_), channel_id=1, source_target_pairs={{0,96},{1,97},{2,98},{3,99},{4,100},{5,101},{6,102},{7,103},{8,104... | collective-permute-start | bytes 196616 | tf_op jit(solution)/shard_map/ppermute | solution.py:414
  64.6 5.8 %collective-permute-start.10 = (f32[128,128]{1,0:T(8,128)S(1)}, f32[128,128]{1,0:T(8,128)S(1)}, u32[]{:S(2)}, u32[]{:S(2)}) collective-permute-start(f32[128,128]{1,0:T(8,128)S(1)} %add.13.refs_0_), channel_id=1, source_target_pairs={{0,64},{1,65},{2,66},{3,67},{4,68},{5,69},{6,70},{7,71},{8,72},{9,... | collective-permute-start | bytes 196616 | tf_op jit(solution)/shard_map/ppermute | solution.py:414
  64.9 5.4 %collective-permute-start.9 = (f32[128,128]{1,0:T(8,128)S(1)}, f32[128,128]{1,0:T(8,128)S(1)}, u32[]{:S(2)}, u32[]{:S(2)}) collective-permute-start(f32[128,128]{1,0:T(8,128)S(1)} %add.13.refs_0_), channel_id=1, source_target_pairs={{0,32},{1,33},{2,34},{3,35},{4,36},{5,37},{6,38},{7,39},{8,40},{9,... | collective-permute-start | bytes 196616 | tf_op jit(solution)/shard_map/ppermute | solution.py:414
  72.3 11.8 %collective-permute-start.13 = (f32[128,256]{1,0:T(8,128)S(1)}, f32[128,256]{1,0:T(8,128)S(1)}, u32[]{:S(2)}, u32[]{:S(2)}) collective-permute-start(f32[128,256]{1,0:T(8,128)S(1)} %get-tuple-element.53.w_ref), channel_id=1, source_target_pairs={{0,15},{1,8},{2,9},{3,10},{4,11},{5,12},{6,13},{7,14},{16,31},{17,... | collective-permute-start | bytes 393224 | tf_op jit(solution)/shard_map/ppermute | solution.py:414
  77.5 6.6 %collective-permute-start.14 = (f32[128,3072]{1,0:T(8,128)S(1)}, f32[128,3072]{1,0:T(8,128)S(1)}, u32[]{:S(2)}, u32[]{:S(2)}) collective-permute-start(f32[128,3072]{1,0:T(8,128)S(1)} %given.2), channel_id=1, source_target_pairs={{8,0},{9,1},{10,2},{11,3},{12,4},{13,5},{14,6},{15,7},{24,16},{25,... | collective-permute-start | bytes 4718600 | tf_op jit(solution)/shard_map/ppermute | solution.py:414
  80.3 7.7 %collective-permute-start.19 = (f32[128,384]{1,0:T(8,128)S(1)}, f32[128,384]{1,0:T(8,128)S(1)}, u32[]{:S(2)}, u32[]{:S(2)}) collective-permute-start(f32[128,384]{1,0:T(8,128)S(1)} %get-tuple-element.61), channel_id=1, source_target_pairs={{0,15},{1,8},{2,9},{3,10},{4,11},{5,12},{6,13},{7,14},{8,0},{9,1},... | collective-permute-start | bytes 589832 | tf_op jit(solution)/shard_map/ppermute | solution.py:414
  84.9 5.2 %collective-permute-start.15 = (f32[128,128]{1,0:T(8,128)S(1)}, f32[128,128]{1,0:T(8,128)S(1)}, u32[]{:S(2)}, u32[]{:S(2)}) collective-permute-start(f32[128,128]{1,0:T(8,128)S(1)} %get-tuple-element.60), channel_id=1, source_target_pairs={{0,16},{1,17},{2,18},{3,19},{4,20},{5,21},{6,22},{7,23},{8,24},{9,... | collective-permute-start | bytes 196616 | tf_op jit(solution)/shard_map/ppermute | solution.py:414
  86.1 20.6 %collective-permute-start.21 = (f32[128,3072]{1,0:T(8,128)S(1)}, f32[128,3072]{1,0:T(8,128)S(1)}, u32[]{:S(2)}, u32[]{:S(2)}) collective-permute-start(f32[128,3072]{1,0:T(8,128)S(1)} %given.2), channel_id=1, source_target_pairs={{8,15},{9,8},{10,9},{11,10},{12,11},{13,12},{14,13},{15,14},{24,31... | collective-permute-start | bytes 4718600 | tf_op jit(solution)/shard_map/ppermute | solution.py:414
  90.2 6.9 %collective-permute-start.18 = (f32[128,128]{1,0:T(8,128)S(1)}, f32[128,128]{1,0:T(8,128)S(1)}, u32[]{:S(2)}, u32[]{:S(2)}) collective-permute-start(f32[128,128]{1,0:T(8,128)S(1)} %add.14.refs_0_), channel_id=1, source_target_pairs={{0,96},{1,97},{2,98},{3,99},{4,100},{5,101},{6,102},{7,103},{8,104... | collective-permute-start | bytes 196616 | tf_op jit(solution)/shard_map/ppermute | solution.py:414
  91.5 6.3 %collective-permute-start.17 = (f32[128,128]{1,0:T(8,128)S(1)}, f32[128,128]{1,0:T(8,128)S(1)}, u32[]{:S(2)}, u32[]{:S(2)}) collective-permute-start(f32[128,128]{1,0:T(8,128)S(1)} %add.14.refs_0_), channel_id=1, source_target_pairs={{0,64},{1,65},{2,66},{3,67},{4,68},{5,69},{6,70},{7,71},{8,72},{9,... | collective-permute-start | bytes 196616 | tf_op jit(solution)/shard_map/ppermute | solution.py:414
  92.9 5.1 %collective-permute-start.16 = (f32[128,128]{1,0:T(8,128)S(1)}, f32[128,128]{1,0:T(8,128)S(1)}, u32[]{:S(2)}, u32[]{:S(2)}) collective-permute-start(f32[128,128]{1,0:T(8,128)S(1)} %add.14.refs_0_), channel_id=1, source_target_pairs={{0,32},{1,33},{2,34},{3,35},{4,36},{5,37},{6,38},{7,39},{8,40},{9,... | collective-permute-start | bytes 196616 | tf_op jit(solution)/shard_map/ppermute | solution.py:414
  100.0 7.5 %collective-permute-start.20 = (f32[128,256]{1,0:T(8,128)S(1)}, f32[128,256]{1,0:T(8,128)S(1)}, u32[]{:S(2)}, u32[]{:S(2)}) collective-permute-start(f32[128,256]{1,0:T(8,128)S(1)} %get-tuple-element.63.w_ref), channel_id=1, source_target_pairs={{0,15},{1,8},{2,9},{3,10},{4,11},{5,12},{6,13},{7,14},{16,31},{17,... | collective-permute-start | bytes 393224 | tf_op jit(solution)/shard_map/ppermute | solution.py:414
  103.6 5.3 %collective-permute-start.22 = (f32[128,3072]{1,0:T(8,128)S(1)}, f32[128,3072]{1,0:T(8,128)S(1)}, u32[]{:S(2)}, u32[]{:S(2)}) collective-permute-start(f32[128,3072]{1,0:T(8,128)S(1)} %given.3), channel_id=1, source_target_pairs={{8,0},{9,1},{10,2},{11,3},{12,4},{13,5},{14,6},{15,7},{24,16},{25,... | collective-permute-start | bytes 4718600 | tf_op jit(solution)/shard_map/ppermute | solution.py:414
  106.2 12.1 %collective-permute-start.27 = (f32[128,384]{1,0:T(8,128)S(1)}, f32[128,384]{1,0:T(8,128)S(1)}, u32[]{:S(2)}, u32[]{:S(2)}) collective-permute-start(f32[128,384]{1,0:T(8,128)S(1)} %get-tuple-element.72), channel_id=1, source_target_pairs={{0,15},{1,8},{2,9},{3,10},{4,11},{5,12},{6,13},{7,14},{8,0},{9,1},... | collective-permute-start | bytes 589832 | tf_op jit(solution)/shard_map/ppermute | solution.py:414
  108.9 13.2 %copy-start.3 = (f32[1,512]{1,0:T(1,128)S(1)}, f32[1,512]{1,0:T(1,128)}, u32[]{:S(2)}) copy-start(f32[1,512]{1,0:T(1,128)} %copy-done.2) | copy-start | bytes 6148
  109.7 4.3 %collective-permute-start.23 = (f32[128,128]{1,0:T(8,128)S(1)}, f32[128,128]{1,0:T(8,128)S(1)}, u32[]{:S(2)}, u32[]{:S(2)}) collective-permute-start(f32[128,128]{1,0:T(8,128)S(1)} %get-tuple-element.71), channel_id=1, source_target_pairs={{0,16},{1,17},{2,18},{3,19},{4,20},{5,21},{6,22},{7,23},{8,24},{9,... | collective-permute-start | bytes 196616 | tf_op jit(solution)/shard_map/ppermute | solution.py:414
  114.1 5.6 %collective-permute-start.26 = (f32[128,128]{1,0:T(8,128)S(1)}, f32[128,128]{1,0:T(8,128)S(1)}, u32[]{:S(2)}, u32[]{:S(2)}) collective-permute-start(f32[128,128]{1,0:T(8,128)S(1)} %add.15.refs_0_), channel_id=1, source_target_pairs={{0,96},{1,97},{2,98},{3,99},{4,100},{5,101},{6,102},{7,103},{8,104... | collective-permute-start | bytes 196616 | tf_op jit(solution)/shard_map/ppermute | solution.py:414
  116.0 5.9 %collective-permute-start.25 = (f32[128,128]{1,0:T(8,128)S(1)}, f32[128,128]{1,0:T(8,128)S(1)}, u32[]{:S(2)}, u32[]{:S(2)}) collective-permute-start(f32[128,128]{1,0:T(8,128)S(1)} %add.15.refs_0_), channel_id=1, source_target_pairs={{0,64},{1,65},{2,66},{3,67},{4,68},{5,69},{6,70},{7,71},{8,72},{9,... | collective-permute-start | bytes 196616 | tf_op jit(solution)/shard_map/ppermute | solution.py:414
  117.1 5.0 %collective-permute-start.24 = (f32[128,128]{1,0:T(8,128)S(1)}, f32[128,128]{1,0:T(8,128)S(1)}, u32[]{:S(2)}, u32[]{:S(2)}) collective-permute-start(f32[128,128]{1,0:T(8,128)S(1)} %add.15.refs_0_), channel_id=1, source_target_pairs={{0,32},{1,33},{2,34},{3,35},{4,36},{5,37},{6,38},{7,39},{8,40},{9,... | collective-permute-start | bytes 196616 | tf_op jit(solution)/shard_map/ppermute | solution.py:414
  125.2 3.5 %collective-permute-start.28 = (f32[128,3072]{1,0:T(8,128)S(1)}, f32[128,3072]{1,0:T(8,128)S(1)}, u32[]{:S(2)}, u32[]{:S(2)}) collective-permute-start(f32[128,3072]{1,0:T(8,128)S(1)} %get-tuple-element.76), channel_id=1, source_target_pairs={{0,8},{1,9},{2,10},{3,11},{4,12},{5,13},{6,14},{7,15},{8,0},{9,1},... | collective-permute-start | bytes 4718600 | tf_op jit(solution)/shard_map/ppermute | solution.py:414

commit v5 on v4

--- a/solution.py
+++ b/solution.py
@@ -54,7 +54,7 @@
 
 
 def fill(core, observed, estimate, mask):
-    step = 256
+    step = 512
     rows = pl.BlockSpec((step, 2 * PW), lambda i: (i, 0))
     out = pl.BlockSpec((PW, step), lambda i: (0, i))
     return pl.pallas_call(
@@ -63,7 +63,7 @@
         in_specs=[SMEM, rows, rows, rows],
         out_specs=[out, out],
         out_shape=[jax.ShapeDtypeStruct((PW, RH), F32)] * 2,
-        compiler_params=params(60),
+        compiler_params=params(50),
         cost_estimate=cost(10**6, 15 * 10**6),
         name="fill",
     )(core, observed, estimate, mask)
@@ -385,9 +385,20 @@
 
 def last_kept_kernel(core_ref, w_ref, k_ref, m_ref, got_ref, out_ref):
     core = core_ref[0]
-    mine = pl.multiple_of(core * BW, BW)
-    apply_to(w_ref[...], (k_ref, m_ref), PLAIN, out_ref.at[pl.ds(mine, BW)], core * RH)
-    out_ref[pl.ds(pl.multiple_of(BW - mine, BW), BW)] = got_ref[...]
+    wh, wl = split(w_ref[...])
+    both = jnp.concatenate([wh, wl], axis=0)
+    mine, other = core * 32, 32 - core * 32
+    for half in range(2):
+        for j in range(0, RH, CH):
+            xh, xl = split(columns((k_ref, m_ref), PLAIN, half, j))
+            wide = mxu(both, xh)
+            value = wide[:BW] + (wide[BW:] + mxu(wh, xl))
+            at = pl.multiple_of((core * RH if half == 0 else RH - core * RH) + j, 128)
+            for d in range(32):
+                out_ref[mine + d, :, pl.ds(at, CH)] = value[4 * d : 4 * d + 4]
+    for j in range(0, RB, CH):
+        for d in range(32):
+            out_ref[other + d, :, j : j + CH] = got_ref[4 * d : 4 * d + 4, j : j + CH]
 
 
 def last_kept(core, w, xs, got):
@@ -395,7 +406,7 @@
         last_kept_kernel,
         in_specs=[SMEM] + [VMEM] * 4,
         out_specs=VMEM,
-        out_shape=jax.ShapeDtypeStruct((PW, RB), F32),
+        out_shape=jax.ShapeDtypeStruct((64, 4, RB), F32),
         compiler_params=params(),
         cost_estimate=cost(10**9, 6 * 10**6),
         name="last_kept",
@@ -474,7 +485,7 @@
     xs = (joined, kept)
     send, w = last(core, thr, reduced(partial), diags, xs)
     got = swap_cores(send)
-    packed = last_kept(core, w, xs, got).reshape(64, 4, RB)
+    packed = last_kept(core, w, xs, got)
     landed = lax.all_to_all(packed, ("zx", "pairs"), split_axis=0, concat_axis=0, tiled=True)
     landed = landed.reshape(8, 8, 4, RB)
     landed = jnp.roll(landed, 1, axis=1).transpose(2, 1, 0, 3)

time: 187 us -> 183 us (0.979)
  local copies, waits for them, and re-layouts: 5.91 us -> 3.79 us
  Pallas kernels: 25.3 us -> 23.3 us
    transpose x0 -> x1, local copies, waits for them, and re-layouts: none -> 3.49 us  [on_device(): landed = jnp.roll(landed, 1, axis=1).transpose(2, 1, 0, 3)]
    unnamed x12 -> x6, local copies, waits for them, and re-layouts: 3.45 us -> 0.01 us
    concatenate x1 -> x0, other arithmetic: 2.29 us -> none  [on_device(): landed = jnp.roll(landed, 1, axis=1).transpose(2, 1, 0, 3)]
    reshape x1 -> x0, local copies, waits for them, and re-layouts: 2.14 us -> none  [on_device(): packed = last_kept(core, w, xs, got).reshape(64, 4, RB)]
    pallas_call x1, Pallas kernels: 6.72 us -> 4.65 us  [fill(): pl.pallas_call(fill_kernel, grid=(RH // step,), in_specs=[SMEM, rows, row...]
where the time goes in v5:
time: 183 us; the launch traced here: 182 us
  waiting for transfers between devices  54.5 us (30%)
  blocking collectives  49.9 us (27%)
  starting transfers between devices  49.6 us (27%)
  Pallas kernels  23.3 us (13%)
  local copies, waits for them, and re-layouts  3.79 us (2%)
    ppermute x29, waiting for transfers between devices, to(): return lax.ppermute(block, AXES, route)  54.5 us
    all_to_all x1, blocking collectives, on_device(): lax.all_to_all(packed, ('zx', 'pairs'), split_axis=0, concat_axis=0, tile...  49.9 us
    ppermute x29, starting transfers between devices, to(): return lax.ppermute(block, AXES, route)  49.6 us
    pallas_call x11, Pallas kernels, call(): pl.pallas_call(kernel, in_specs=ins, out_specs=[VMEM] * len(outs), out_sh...  12.5 us
    pallas_call x1, Pallas kernels, fill(): pl.pallas_call(fill_kernel, grid=(RH // step,), in_specs=[SMEM, rows, row...  4.65 us
  transfers between devices with their start and end apart: 29, of which 20 were waited for; matrix products, arithmetic and copies ran while one was open for 0% of the time, Pallas kernels for 4%

profile of v5, /device:TPU:0, one launch (start us, length us, event | category | flops | bytes accessed | tf_op | source)
XLA Modules:
  0.0 182.4 jit_solution(5692573896122846260)
XLA Ops:
  0.0 4.6 %fill.1 = (f32[256,1536]{1,0:T(8,128)S(1)}, f32[256,1536]{1,0:T(8,128)S(1)}) custom-call(s32[1]{0:T(128)} %bitcast.core_ref, f32[1536,512]{1,0:T(8,128)} %obs_ref.1, f32[1536,512]{1,0:T(8,128)} %est_ref.1, s32[1536,512]{1,0:T(8,128)} %mask_ref.1), custom_call_target="tpu_custom_call" | custom-call | flops 30000000 | bytes 15000000 | tf_op jit(solution)/shard_map/fill/pallas_call | solution.py:60
  4.7 0.1 collective-permute-start.1
  4.8 0.6 gram_first.1
  5.4 2.8 %collective-permute-done.1.x_ref.refs_5_ = f32[256,1536]{1,0:T(8,128)S(1)} collective-permute-done((f32[256,1536]{1,0:T(8,128)S(1)}, f32[256,1536]{1,0:T(8,128)S(1)}, u32[]{:S(2)}, u32[]{:S(2)}) %collective-permute-start.1) | collective-permute-done | bytes 1572896 | tf_op jit(solution)/shard_map/ppermute | solution.py:425
  8.1 0.7 gram_second.1
  8.8 1.7 collective-permute-start.2
  10.5 4.0 %collective-permute-done.2 = f32[264,128]{1,0:T(8,128)S(1)} collective-permute-done((f32[264,128]{1,0:T(8,128)S(1)}, f32[264,128]{1,0:T(8,128)S(1)}, u32[]{:S(2)}, u32[]{:S(2)}) %collective-permute-start.2) | collective-permute-done | bytes 135200 | tf_op jit(solution)/shard_map/ppermute | solution.py:425
  14.6 4.2 %collective-permute-start.5 = (f32[264,128]{1,0:T(8,128)S(1)}, f32[264,128]{1,0:T(8,128)S(1)}, u32[]{:S(2)}, u32[]{:S(2)}) collective-permute-start(f32[264,128]{1,0:T(8,128)S(1)} %add.12.refs_0_), channel_id=1, source_target_pairs={{0,96},{1,97},{2,98},{3,99},{4,100},{5,101},{6,102},{7,103},{8,104... | collective-permute-start | bytes 405512 | tf_op jit(solution)/shard_map/ppermute | solution.py:425
  18.8 0.9 collective-permute-start.3
  19.7 4.3 %collective-permute-done.5.refs_3_ = f32[264,128]{1,0:T(8,128)S(1)} collective-permute-done((f32[264,128]{1,0:T(8,128)S(1)}, f32[264,128]{1,0:T(8,128)S(1)}, u32[]{:S(2)}, u32[]{:S(2)}) %collective-permute-start.5) | collective-permute-done | bytes 135200 | tf_op jit(solution)/shard_map/ppermute | solution.py:425
  24.0 2.2 %collective-permute-done.4.refs_2_ = f32[264,128]{1,0:T(8,128)S(1)} collective-permute-done((f32[264,128]{1,0:T(8,128)S(1)}, f32[264,128]{1,0:T(8,128)S(1)}, u32[]{:S(2)}, u32[]{:S(2)}) %collective-permute-start.4) | collective-permute-done | bytes 135200 | tf_op jit(solution)/shard_map/ppermute | solution.py:425
  26.3 3.7 %whiten.3 = (f32[128,3072]{1,0:T(8,128)S(1)}, f32[128,3072]{1,0:T(8,128)S(1)}, f32[256,256]{1,0:T(8,128)S(1)}, f32[256,256]{1,0:T(8,128)S(1)}, f32[256,256]{1,0:T(8,128)S(1)}, /*index=5*/f32[256,128]{1,0:T(8,128)S(1)}) custom-call(f32[264,128]{1,0:T(8,128)S(1)} %add.12.refs_0_, f32[264,128]{1,0:T(8,128)S(1)} %collective-permute-done.3.refs_1_, ...), custom_call_target="tpu_custom_call" | custom-call | flops 30000001024 | bytes 6000000 | tf_op jit(solution)/shard_map/whiten/pallas_call | solution.py:241
  30.0 7.3 %collective-permute-start.7 = (f32[128,3072]{1,0:T(8,128)S(1)}, f32[128,3072]{1,0:T(8,128)S(1)}, u32[]{:S(2)}, u32[]{:S(2)}) collective-permute-start(f32[128,3072]{1,0:T(8,128)S(1)} %get-tuple-element.45.k_ref.x0_ref), channel_id=1, source_target_pairs={{0,15},{1,8},{2,9},{3,10},{4,11},{5,12},{6,13},{7,14},{16,31},{17,... | collective-permute-start | bytes 4718600 | tf_op jit(solution)/shard_map/ppermute | solution.py:425
  37.4 1.9 %collective-permute-start = (f32[1,512]{1,0:T(1,128)S(1)}, f32[1,512]{1,0:T(1,128)S(1)}, u32[]{:S(2)}, u32[]{:S(2)}) collective-permute-start(f32[1,512]{1,0:T(1,128)S(1)} %bitcast.8), channel_id=1, source_target_pairs={{0,7},{1,0},{2,1},{3,2},{4,3},{5,4},{6,5},{7,6},{8,15},{9,8},{10,9... | collective-permute-start | bytes 6152 | tf_op jit(solution)/shard_map/ppermute | solution.py:425
  39.3 15.9 %collective-permute-done.refs_1_.thr_ref = f32[1,512]{1,0:T(1,128)S(1)} collective-permute-done((f32[1,512]{1,0:T(1,128)S(1)}, f32[1,512]{1,0:T(1,128)S(1)}, u32[]{:S(2)}, u32[]{:S(2)}) %collective-permute-start) | collective-permute-done | bytes 2080 | tf_op jit(solution)/shard_map/ppermute | solution.py:425
  55.2 0.7 gram_cross.1
  56.0 1.7 collective-permute-start.8
  57.7 0.6 diagonals.1
  58.4 2.0 %collective-permute-done.8 = f32[128,128]{1,0:T(8,128)S(1)} collective-permute-done((f32[128,128]{1,0:T(8,128)S(1)}, f32[128,128]{1,0:T(8,128)S(1)}, u32[]{:S(2)}, u32[]{:S(2)}) %collective-permute-start.8) | collective-permute-done | bytes 65568 | tf_op jit(solution)/shard_map/ppermute | solution.py:425
  60.4 2.1 %collective-permute-start.11 = (f32[128,128]{1,0:T(8,128)S(1)}, f32[128,128]{1,0:T(8,128)S(1)}, u32[]{:S(2)}, u32[]{:S(2)}) collective-permute-start(f32[128,128]{1,0:T(8,128)S(1)} %add.13.refs_0_), channel_id=1, source_target_pairs={{0,96},{1,97},{2,98},{3,99},{4,100},{5,101},{6,102},{7,103},{8,104... | collective-permute-start | bytes 196616 | tf_op jit(solution)/shard_map/ppermute | solution.py:425
  62.5 0.3 collective-permute-start.10
  62.8 1.8 collective-permute-start.9
  64.5 1.8 collective-permute-done.12.refs_5_
  66.3 1.9 %collective-permute-done.10.refs_2_ = f32[128,128]{1,0:T(8,128)S(1)} collective-permute-done((f32[128,128]{1,0:T(8,128)S(1)}, f32[128,128]{1,0:T(8,128)S(1)}, u32[]{:S(2)}, u32[]{:S(2)}) %collective-permute-start.10) | collective-permute-done | bytes 65568 | tf_op jit(solution)/shard_map/ppermute | solution.py:425
  68.2 1.9 %whiten.4 = (f32[128,256]{1,0:T(8,128)S(1)}, f32[128,256]{1,0:T(8,128)S(1)}, f32[256,256]{1,0:T(8,128)S(1)}, f32[256,256]{1,0:T(8,128)S(1)}, f32[256,256]{1,0:T(8,128)S(1)}, /*index=5*/f32[256,128]{1,0:T(8,128)S(1)}) custom-call(f32[128,128]{1,0:T(8,128)S(1)} %add.13.refs_0_, f32[128,128]{1,0:T(8,128)S(1)} %collective-permute-done.9.refs_1_, ...), custom_call_target="tpu_custom_call" | custom-call | flops 30000001024 | bytes 6000000 | tf_op jit(solution)/shard_map/whiten/pallas_call | solution.py:241
  70.2 5.2 %collective-permute-start.13 = (f32[128,256]{1,0:T(8,128)S(1)}, f32[128,256]{1,0:T(8,128)S(1)}, u32[]{:S(2)}, u32[]{:S(2)}) collective-permute-start(f32[128,256]{1,0:T(8,128)S(1)} %get-tuple-element.53.w_ref), channel_id=1, source_target_pairs={{0,15},{1,8},{2,9},{3,10},{4,11},{5,12},{6,13},{7,14},{16,31},{17,... | collective-permute-start | bytes 393224 | tf_op jit(solution)/shard_map/ppermute | solution.py:425
  75.4 1.5 collective-permute-start.14
  76.9 1.3 kept_second.2
  78.2 3.8 %collective-permute-start.19 = (f32[128,384]{1,0:T(8,128)S(1)}, f32[128,384]{1,0:T(8,128)S(1)}, u32[]{:S(2)}, u32[]{:S(2)}) collective-permute-start(f32[128,384]{1,0:T(8,128)S(1)} %get-tuple-element.61), channel_id=1, source_target_pairs={{0,15},{1,8},{2,9},{3,10},{4,11},{5,12},{6,13},{7,14},{8,0},{9,1},... | collective-permute-start | bytes 589832 | tf_op jit(solution)/shard_map/ppermute | solution.py:425
  82.0 0.8 combine.2
  82.9 1.1 collective-permute-start.15
  84.0 0.7 collective-permute-start.21
  84.7 1.2 collective-permute-done.19
  85.9 2.2 %collective-permute-done.15 = f32[128,128]{1,0:T(8,128)S(1)} collective-permute-done((f32[128,128]{1,0:T(8,128)S(1)}, f32[128,128]{1,0:T(8,128)S(1)}, u32[]{:S(2)}, u32[]{:S(2)}) %collective-permute-start.15) | collective-permute-done | bytes 65568 | tf_op jit(solution)/shard_map/ppermute | solution.py:425
  88.1 1.3 collective-permute-start.18
  89.4 1.4 collective-permute-start.17
  90.8 1.4 collective-permute-start.16
  92.3 2.8 %collective-permute-done.18.refs_3_ = f32[128,128]{1,0:T(8,128)S(1)} collective-permute-done((f32[128,128]{1,0:T(8,128)S(1)}, f32[128,128]{1,0:T(8,128)S(1)}, u32[]{:S(2)}, u32[]{:S(2)}) %collective-permute-start.18) | collective-permute-done | bytes 65568 | tf_op jit(solution)/shard_map/ppermute | solution.py:425
  95.1 0.7 collective-permute-done.17.refs_2_
  95.7 0.2 collective-permute-done.16.refs_1_
  96.0 1.9 %whiten.5 = (f32[128,256]{1,0:T(8,128)S(1)}, f32[128,256]{1,0:T(8,128)S(1)}, f32[256,256]{1,0:T(8,128)S(1)}, f32[256,256]{1,0:T(8,128)S(1)}, f32[256,256]{1,0:T(8,128)S(1)}, /*index=5*/f32[256,128]{1,0:T(8,128)S(1)}) custom-call(f32[128,128]{1,0:T(8,128)S(1)} %add.14.refs_0_, f32[128,128]{1,0:T(8,128)S(1)} %collective-permute-done.16.refs_1_, ...), custom_call_target="tpu_custom_call" | custom-call | flops 30000001024 | bytes 6000000 | tf_op jit(solution)/shard_map/whiten/pallas_call | solution.py:241
  97.9 3.6 %collective-permute-start.20 = (f32[128,256]{1,0:T(8,128)S(1)}, f32[128,256]{1,0:T(8,128)S(1)}, u32[]{:S(2)}, u32[]{:S(2)}) collective-permute-start(f32[128,256]{1,0:T(8,128)S(1)} %get-tuple-element.63.w_ref), channel_id=1, source_target_pairs={{0,15},{1,8},{2,9},{3,10},{4,11},{5,12},{6,13},{7,14},{16,31},{17,... | collective-permute-start | bytes 393224 | tf_op jit(solution)/shard_map/ppermute | solution.py:425
  101.5 1.3 collective-permute-start.22
  102.8 1.3 kept_second.3
  104.1 0.5 collective-permute-start.27
  104.6 0.8 collective-permute-done.20.w_ref
  105.4 1.4 collective-permute-done.22.refs_2_
  106.8 0.9 combine.3
  107.7 1.1 collective-permute-start.23
  108.7 3.3 %collective-permute-done.23 = f32[128,128]{1,0:T(8,128)S(1)} collective-permute-done((f32[128,128]{1,0:T(8,128)S(1)}, f32[128,128]{1,0:T(8,128)S(1)}, u32[]{:S(2)}, u32[]{:S(2)}) %collective-permute-start.23) | collective-permute-done | bytes 65568 | tf_op jit(solution)/shard_map/ppermute | solution.py:425
  112.0 1.9 %collective-permute-start.26 = (f32[128,128]{1,0:T(8,128)S(1)}, f32[128,128]{1,0:T(8,128)S(1)}, u32[]{:S(2)}, u32[]{:S(2)}) collective-permute-start(f32[128,128]{1,0:T(8,128)S(1)} %add.15.refs_0_), channel_id=1, source_target_pairs={{0,96},{1,97},{2,98},{3,99},{4,100},{5,101},{6,102},{7,103},{8,104... | collective-permute-start | bytes 196616 | tf_op jit(solution)/shard_map/ppermute | solution.py:425
  114.0 1.1 collective-permute-start.25
  115.0 1.2 collective-permute-start.24
  116.2 1.4 collective-permute-done.26.refs_3_
  117.6 2.2 %collective-permute-done.25.refs_2_ = f32[128,128]{1,0:T(8,128)S(1)} collective-permute-done((f32[128,128]{1,0:T(8,128)S(1)}, f32[128,128]{1,0:T(8,128)S(1)}, u32[]{:S(2)}, u32[]{:S(2)}) %collective-permute-start.25) | collective-permute-done | bytes 65568 | tf_op jit(solution)/shard_map/ppermute | solution.py:425
  119.8 0.3 collective-permute-done.24.refs_1_
  120.1 3.1 %last.1 = (f32[128,3072]{1,0:T(8,128)S(1)}, f32[128,256]{1,0:T(8,128)S(1)}) custom-call(s32[1]{0:T(128)} %bitcast.core_ref, f32[1,512]{1,0:T(1,128)S(1)} %copy-done.1, f32[128,128]{1,0:T(8,128)S(1)} %add.15.refs_0_, f32[128,128]{1,0:T(8,128)S(1)} %collective-permute-done.24.refs_1_, f32[128,128]{1,0:T(8,128)S(1)} %collective-permute-done.25.refs_2_, ...), custom_call_target="tpu_custom_call" | custom-call | flops 30000001024 | bytes 6000000 | tf_op jit(solution)/shard_map/last/pallas_call | solution.py:375
  123.2 0.3 collective-permute-start.28
  123.6 3.2 %collective-permute-done.28.got_ref = f32[128,3072]{1,0:T(8,128)S(1)} collective-permute-done((f32[128,3072]{1,0:T(8,128)S(1)}, f32[128,3072]{1,0:T(8,128)S(1)}, u32[]{:S(2)}, u32[]{:S(2)}) %collective-permute-start.28) | collective-permute-done | bytes 1572896 | tf_op jit(solution)/shard_map/ppermute | solution.py:425
  126.7 1.0 last_kept.1
  127.7 49.9 %all_to_all.5 = f32[64,4,3072]{2,1,0:T(4,128)S(1)} all-to-all(f32[64,4,3072]{2,1,0:T(4,128)S(1)} %last_kept.1), channel_id=1, replica_groups=mesh['zx'=8,'core'=2,'pairs'=8] {'zx','pairs'}, dimensions={0} | all-to-all | bytes 6291456 | tf_op jit(solution)/shard_map/all_to_all | solution.py:489
  177.6 0.2 slice.26
  177.9 1.0 maximum_bitcast_fusion
  178.9 3.5 %copy.5 = f32[4,8,8,3072]{3,1,2,0:T(8,128)} copy(f32[4,8,8,3072]{3,0,1,2:T(4,128)S(1)} %maximum_bitcast_fusion) | data formatting | bytes 6291456 | tf_op jit(solution)/shard_map/transpose | solution.py:491
  (29 shorter events, 0.3 us)
Async XLA Ops:
  4.7 3.5 %collective-permute-start.1 = (f32[256,1536]{1,0:T(8,128)S(1)}, f32[256,1536]{1,0:T(8,128)S(1)}, u32[]{:S(2)}, u32[]{:S(2)}) collective-permute-start(f32[256,1536]{1,0:T(8,128)S(1)} %get-tuple-element.41), channel_id=1, source_target_pairs={{0,8},{1,9},{2,10},{3,11},{4,12},{5,13},{6,14},{7,15},{8,0},{9,1},... | collective-permute-start | bytes 4718600 | tf_op jit(solution)/shard_map/ppermute | solution.py:425
  8.8 5.7 %collective-permute-start.2 = (f32[264,128]{1,0:T(8,128)S(1)}, f32[264,128]{1,0:T(8,128)S(1)}, u32[]{:S(2)}, u32[]{:S(2)}) collective-permute-start(f32[264,128]{1,0:T(8,128)S(1)} %gram_second.1), channel_id=1, source_target_pairs={{0,16},{1,17},{2,18},{3,19},{4,20},{5,21},{6,22},{7,23},{8,24},{9,... | collective-permute-start | bytes 405512 | tf_op jit(solution)/shard_map/ppermute | solution.py:425
  14.6 22.8 %copy-start.2 = (f32[512]{0:T(512)S(1)}, f32[512]{0:T(512)}, u32[]{:S(2)}) copy-start(f32[512]{0:T(512)} %param.7) | copy-start | bytes 6148
  14.6 9.5 %collective-permute-start.5 = (f32[264,128]{1,0:T(8,128)S(1)}, f32[264,128]{1,0:T(8,128)S(1)}, u32[]{:S(2)}, u32[]{:S(2)}) collective-permute-start(f32[264,128]{1,0:T(8,128)S(1)} %add.12.refs_0_), channel_id=1, source_target_pairs={{0,96},{1,97},{2,98},{3,99},{4,100},{5,101},{6,102},{7,103},{8,104... | collective-permute-start | bytes 405512 | tf_op jit(solution)/shard_map/ppermute | solution.py:425
  18.8 7.5 %collective-permute-start.4 = (f32[264,128]{1,0:T(8,128)S(1)}, f32[264,128]{1,0:T(8,128)S(1)}, u32[]{:S(2)}, u32[]{:S(2)}) collective-permute-start(f32[264,128]{1,0:T(8,128)S(1)} %add.12.refs_0_), channel_id=1, source_target_pairs={{0,64},{1,65},{2,66},{3,67},{4,68},{5,69},{6,70},{7,71},{8,72},{9,... | collective-permute-start | bytes 405512 | tf_op jit(solution)/shard_map/ppermute | solution.py:425
  18.8 7.5 %collective-permute-start.3 = (f32[264,128]{1,0:T(8,128)S(1)}, f32[264,128]{1,0:T(8,128)S(1)}, u32[]{:S(2)}, u32[]{:S(2)}) collective-permute-start(f32[264,128]{1,0:T(8,128)S(1)} %add.12.refs_0_), channel_id=1, source_target_pairs={{0,32},{1,33},{2,34},{3,35},{4,36},{5,37},{6,38},{7,39},{8,40},{9,... | collective-permute-start | bytes 405512 | tf_op jit(solution)/shard_map/ppermute | solution.py:425
  30.0 25.3 %collective-permute-start.6 = (f32[128,3072]{1,0:T(8,128)S(1)}, f32[128,3072]{1,0:T(8,128)S(1)}, u32[]{:S(2)}, u32[]{:S(2)}) collective-permute-start(f32[128,3072]{1,0:T(8,128)S(1)} %get-tuple-element.46.refs_1_.x1_ref), channel_id=1, source_target_pairs={{0,8},{1,9},{2,10},{3,11},{4,12},{5,13},{6,14},{7,15},{8,1},{9,2},... | collective-permute-start | bytes 4718600 | tf_op jit(solution)/shard_map/ppermute | solution.py:425
  30.0 25.2 %collective-permute-start.7 = (f32[128,3072]{1,0:T(8,128)S(1)}, f32[128,3072]{1,0:T(8,128)S(1)}, u32[]{:S(2)}, u32[]{:S(2)}) collective-permute-start(f32[128,3072]{1,0:T(8,128)S(1)} %get-tuple-element.45.k_ref.x0_ref), channel_id=1, source_target_pairs={{0,15},{1,8},{2,9},{3,10},{4,11},{5,12},{6,13},{7,14},{16,31},{17,... | collective-permute-start | bytes 4718600 | tf_op jit(solution)/shard_map/ppermute | solution.py:425
  37.4 17.8 %collective-permute-start = (f32[1,512]{1,0:T(1,128)S(1)}, f32[1,512]{1,0:T(1,128)S(1)}, u32[]{:S(2)}, u32[]{:S(2)}) collective-permute-start(f32[1,512]{1,0:T(1,128)S(1)} %bitcast.8), channel_id=1, source_target_pairs={{0,7},{1,0},{2,1},{3,2},{4,3},{5,4},{6,5},{7,6},{8,15},{9,8},{10,9... | collective-permute-start | bytes 6152 | tf_op jit(solution)/shard_map/ppermute | solution.py:425
  55.2 0.8 copy-start
  56.0 4.3 %collective-permute-start.8 = (f32[128,128]{1,0:T(8,128)S(1)}, f32[128,128]{1,0:T(8,128)S(1)}, u32[]{:S(2)}, u32[]{:S(2)}) collective-permute-start(f32[128,128]{1,0:T(8,128)S(1)} %gram_cross.1), channel_id=1, source_target_pairs={{0,16},{1,17},{2,18},{3,19},{4,20},{5,21},{6,22},{7,23},{8,24},{9,... | collective-permute-start | bytes 196616 | tf_op jit(solution)/shard_map/ppermute | solution.py:425
  58.3 8.0 %collective-permute-start.12 = (f32[128,128]{1,0:T(8,128)S(1)}, f32[128,128]{1,0:T(8,128)S(1)}, u32[]{:S(2)}, u32[]{:S(2)}) collective-permute-start(f32[128,128]{1,0:T(8,128)S(1)} %get-tuple-element.52), channel_id=1, source_target_pairs={{0,8},{1,9},{2,10},{3,11},{4,12},{5,13},{6,14},{7,15},{8,1},{9,2},... | collective-permute-start | bytes 196616 | tf_op jit(solution)/shard_map/ppermute | solution.py:425
  60.4 5.9 %collective-permute-start.11 = (f32[128,128]{1,0:T(8,128)S(1)}, f32[128,128]{1,0:T(8,128)S(1)}, u32[]{:S(2)}, u32[]{:S(2)}) collective-permute-start(f32[128,128]{1,0:T(8,128)S(1)} %add.13.refs_0_), channel_id=1, source_target_pairs={{0,96},{1,97},{2,98},{3,99},{4,100},{5,101},{6,102},{7,103},{8,104... | collective-permute-start | bytes 196616 | tf_op jit(solution)/shard_map/ppermute | solution.py:425
  62.5 5.8 %collective-permute-start.10 = (f32[128,128]{1,0:T(8,128)S(1)}, f32[128,128]{1,0:T(8,128)S(1)}, u32[]{:S(2)}, u32[]{:S(2)}) collective-permute-start(f32[128,128]{1,0:T(8,128)S(1)} %add.13.refs_0_), channel_id=1, source_target_pairs={{0,64},{1,65},{2,66},{3,67},{4,68},{5,69},{6,70},{7,71},{8,72},{9,... | collective-permute-start | bytes 196616 | tf_op jit(solution)/shard_map/ppermute | solution.py:425
  62.8 5.4 %collective-permute-start.9 = (f32[128,128]{1,0:T(8,128)S(1)}, f32[128,128]{1,0:T(8,128)S(1)}, u32[]{:S(2)}, u32[]{:S(2)}) collective-permute-start(f32[128,128]{1,0:T(8,128)S(1)} %add.13.refs_0_), channel_id=1, source_target_pairs={{0,32},{1,33},{2,34},{3,35},{4,36},{5,37},{6,38},{7,39},{8,40},{9,... | collective-permute-start | bytes 196616 | tf_op jit(solution)/shard_map/ppermute | solution.py:425
  70.2 11.8 %collective-permute-start.13 = (f32[128,256]{1,0:T(8,128)S(1)}, f32[128,256]{1,0:T(8,128)S(1)}, u32[]{:S(2)}, u32[]{:S(2)}) collective-permute-start(f32[128,256]{1,0:T(8,128)S(1)} %get-tuple-element.53.w_ref), channel_id=1, source_target_pairs={{0,15},{1,8},{2,9},{3,10},{4,11},{5,12},{6,13},{7,14},{16,31},{17,... | collective-permute-start | bytes 393224 | tf_op jit(solution)/shard_map/ppermute | solution.py:425
  75.4 6.6 %collective-permute-start.14 = (f32[128,3072]{1,0:T(8,128)S(1)}, f32[128,3072]{1,0:T(8,128)S(1)}, u32[]{:S(2)}, u32[]{:S(2)}) collective-permute-start(f32[128,3072]{1,0:T(8,128)S(1)} %given.2), channel_id=1, source_target_pairs={{8,0},{9,1},{10,2},{11,3},{12,4},{13,5},{14,6},{15,7},{24,16},{25,... | collective-permute-start | bytes 4718600 | tf_op jit(solution)/shard_map/ppermute | solution.py:425
  78.2 7.7 %collective-permute-start.19 = (f32[128,384]{1,0:T(8,128)S(1)}, f32[128,384]{1,0:T(8,128)S(1)}, u32[]{:S(2)}, u32[]{:S(2)}) collective-permute-start(f32[128,384]{1,0:T(8,128)S(1)} %get-tuple-element.61), channel_id=1, source_target_pairs={{0,15},{1,8},{2,9},{3,10},{4,11},{5,12},{6,13},{7,14},{8,0},{9,1},... | collective-permute-start | bytes 589832 | tf_op jit(solution)/shard_map/ppermute | solution.py:425
  82.9 5.2 %collective-permute-start.15 = (f32[128,128]{1,0:T(8,128)S(1)}, f32[128,128]{1,0:T(8,128)S(1)}, u32[]{:S(2)}, u32[]{:S(2)}) collective-permute-start(f32[128,128]{1,0:T(8,128)S(1)} %get-tuple-element.60), channel_id=1, source_target_pairs={{0,16},{1,17},{2,18},{3,19},{4,20},{5,21},{6,22},{7,23},{8,24},{9,... | collective-permute-start | bytes 196616 | tf_op jit(solution)/shard_map/ppermute | solution.py:425
  84.0 20.6 %collective-permute-start.21 = (f32[128,3072]{1,0:T(8,128)S(1)}, f32[128,3072]{1,0:T(8,128)S(1)}, u32[]{:S(2)}, u32[]{:S(2)}) collective-permute-start(f32[128,3072]{1,0:T(8,128)S(1)} %given.2), channel_id=1, source_target_pairs={{8,15},{9,8},{10,9},{11,10},{12,11},{13,12},{14,13},{15,14},{24,31... | collective-permute-start | bytes 4718600 | tf_op jit(solution)/shard_map/ppermute | solution.py:425
  88.1 7.0 %collective-permute-start.18 = (f32[128,128]{1,0:T(8,128)S(1)}, f32[128,128]{1,0:T(8,128)S(1)}, u32[]{:S(2)}, u32[]{:S(2)}) collective-permute-start(f32[128,128]{1,0:T(8,128)S(1)} %add.14.refs_0_), channel_id=1, source_target_pairs={{0,96},{1,97},{2,98},{3,99},{4,100},{5,101},{6,102},{7,103},{8,104... | collective-permute-start | bytes 196616 | tf_op jit(solution)/shard_map/ppermute | solution.py:425
  89.4 6.3 %collective-permute-start.17 = (f32[128,128]{1,0:T(8,128)S(1)}, f32[128,128]{1,0:T(8,128)S(1)}, u32[]{:S(2)}, u32[]{:S(2)}) collective-permute-start(f32[128,128]{1,0:T(8,128)S(1)} %add.14.refs_0_), channel_id=1, source_target_pairs={{0,64},{1,65},{2,66},{3,67},{4,68},{5,69},{6,70},{7,71},{8,72},{9,... | collective-permute-start | bytes 196616 | tf_op jit(solution)/shard_map/ppermute | solution.py:425
  90.8 5.1 %collective-permute-start.16 = (f32[128,128]{1,0:T(8,128)S(1)}, f32[128,128]{1,0:T(8,128)S(1)}, u32[]{:S(2)}, u32[]{:S(2)}) collective-permute-start(f32[128,128]{1,0:T(8,128)S(1)} %add.14.refs_0_), channel_id=1, source_target_pairs={{0,32},{1,33},{2,34},{3,35},{4,36},{5,37},{6,38},{7,39},{8,40},{9,... | collective-permute-start | bytes 196616 | tf_op jit(solution)/shard_map/ppermute | solution.py:425
  97.9 7.5 %collective-permute-start.20 = (f32[128,256]{1,0:T(8,128)S(1)}, f32[128,256]{1,0:T(8,128)S(1)}, u32[]{:S(2)}, u32[]{:S(2)}) collective-permute-start(f32[128,256]{1,0:T(8,128)S(1)} %get-tuple-element.63.w_ref), channel_id=1, source_target_pairs={{0,15},{1,8},{2,9},{3,10},{4,11},{5,12},{6,13},{7,14},{16,31},{17,... | collective-permute-start | bytes 393224 | tf_op jit(solution)/shard_map/ppermute | solution.py:425
  101.5 5.3 %collective-permute-start.22 = (f32[128,3072]{1,0:T(8,128)S(1)}, f32[128,3072]{1,0:T(8,128)S(1)}, u32[]{:S(2)}, u32[]{:S(2)}) collective-permute-start(f32[128,3072]{1,0:T(8,128)S(1)} %given.3), channel_id=1, source_target_pairs={{8,0},{9,1},{10,2},{11,3},{12,4},{13,5},{14,6},{15,7},{24,16},{25,... | collective-permute-start | bytes 4718600 | tf_op jit(solution)/shard_map/ppermute | solution.py:425
  104.1 12.1 %collective-permute-start.27 = (f32[128,384]{1,0:T(8,128)S(1)}, f32[128,384]{1,0:T(8,128)S(1)}, u32[]{:S(2)}, u32[]{:S(2)}) collective-permute-start(f32[128,384]{1,0:T(8,128)S(1)} %get-tuple-element.72), channel_id=1, source_target_pairs={{0,15},{1,8},{2,9},{3,10},{4,11},{5,12},{6,13},{7,14},{8,0},{9,1},... | collective-permute-start | bytes 589832 | tf_op jit(solution)/shard_map/ppermute | solution.py:425
  106.8 13.3 %copy-start.1 = (f32[1,512]{1,0:T(1,128)S(1)}, f32[1,512]{1,0:T(1,128)}, u32[]{:S(2)}) copy-start(f32[1,512]{1,0:T(1,128)} %copy-done) | copy-start | bytes 6148
  107.7 4.3 %collective-permute-start.23 = (f32[128,128]{1,0:T(8,128)S(1)}, f32[128,128]{1,0:T(8,128)S(1)}, u32[]{:S(2)}, u32[]{:S(2)}) collective-permute-start(f32[128,128]{1,0:T(8,128)S(1)} %get-tuple-element.71), channel_id=1, source_target_pairs={{0,16},{1,17},{2,18},{3,19},{4,20},{5,21},{6,22},{7,23},{8,24},{9,... | collective-permute-start | bytes 196616 | tf_op jit(solution)/shard_map/ppermute | solution.py:425
  112.0 5.6 %collective-permute-start.26 = (f32[128,128]{1,0:T(8,128)S(1)}, f32[128,128]{1,0:T(8,128)S(1)}, u32[]{:S(2)}, u32[]{:S(2)}) collective-permute-start(f32[128,128]{1,0:T(8,128)S(1)} %add.15.refs_0_), channel_id=1, source_target_pairs={{0,96},{1,97},{2,98},{3,99},{4,100},{5,101},{6,102},{7,103},{8,104... | collective-permute-start | bytes 196616 | tf_op jit(solution)/shard_map/ppermute | solution.py:425
  114.0 5.8 %collective-permute-start.25 = (f32[128,128]{1,0:T(8,128)S(1)}, f32[128,128]{1,0:T(8,128)S(1)}, u32[]{:S(2)}, u32[]{:S(2)}) collective-permute-start(f32[128,128]{1,0:T(8,128)S(1)} %add.15.refs_0_), channel_id=1, source_target_pairs={{0,64},{1,65},{2,66},{3,67},{4,68},{5,69},{6,70},{7,71},{8,72},{9,... | collective-permute-start | bytes 196616 | tf_op jit(solution)/shard_map/ppermute | solution.py:425
  115.0 5.1 %collective-permute-start.24 = (f32[128,128]{1,0:T(8,128)S(1)}, f32[128,128]{1,0:T(8,128)S(1)}, u32[]{:S(2)}, u32[]{:S(2)}) collective-permute-start(f32[128,128]{1,0:T(8,128)S(1)} %add.15.refs_0_), channel_id=1, source_target_pairs={{0,32},{1,33},{2,34},{3,35},{4,36},{5,37},{6,38},{7,39},{8,40},{9,... | collective-permute-start | bytes 196616 | tf_op jit(solution)/shard_map/ppermute | solution.py:425
  123.2 3.5 %collective-permute-start.28 = (f32[128,3072]{1,0:T(8,128)S(1)}, f32[128,3072]{1,0:T(8,128)S(1)}, u32[]{:S(2)}, u32[]{:S(2)}) collective-permute-start(f32[128,3072]{1,0:T(8,128)S(1)} %get-tuple-element.76), channel_id=1, source_target_pairs={{0,8},{1,9},{2,10},{3,11},{4,12},{5,13},{6,14},{7,15},{8,0},{9,1},... | collective-permute-start | bytes 4718600 | tf_op jit(solution)/shard_map/ppermute | solution.py:425

commit v6 on v5

--- a/solution.py
+++ b/solution.py
@@ -411,6 +411,26 @@
         cost_estimate=cost(10**9, 6 * 10**6),
         name="last_kept",
     )(core, w, *xs, got)
+
+
+def place_kernel(in_ref, out_ref):
+    for w in range(4):
+        for j in range(0, RB, CH):
+            rows = in_ref[:, w, j : j + CH]
+            out_ref[8 * w : 8 * w + 8, j : j + CH] = jnp.concatenate([rows[7:], rows[:7]], axis=0)
+
+
+def place(landed):
+    return pl.pallas_call(
+        place_kernel,
+        grid=(8,),
+        in_specs=[pl.BlockSpec((8, 4, RB), lambda i: (i, 0, 0))],
+        out_specs=pl.BlockSpec((32, RB), lambda i: (0, i)),
+        out_shape=jax.ShapeDtypeStruct((32, 8 * RB), F32),
+        compiler_params=params(),
+        cost_estimate=cost(10**6, 6 * 10**6),
+        name="place",
+    )(landed)
 
 
 def to(block, where):
@@ -487,9 +507,7 @@
     got = swap_cores(send)
     packed = last_kept(core, w, xs, got)
     landed = lax.all_to_all(packed, ("zx", "pairs"), split_axis=0, concat_axis=0, tiled=True)
-    landed = landed.reshape(8, 8, 4, RB)
-    landed = jnp.roll(landed, 1, axis=1).transpose(2, 1, 0, 3)
-    return landed.reshape(32, 8 * RB)
+    return place(landed)
 
 
 def solution(mesh):

time: 183 us -> 181 us (0.989)
  local copies, waits for them, and re-layouts: 3.79 us -> 0.03 us
  Pallas kernels: 23.3 us -> 26.7 us
    transpose x1 -> x0, local copies, waits for them, and re-layouts: 3.49 us -> none  [on_device(): landed = jnp.roll(landed, 1, axis=1).transpose(2, 1, 0, 3)]
    pallas_call x0 -> x1, Pallas kernels: none -> 3.47 us  [place(): pl.pallas_call(place_kernel, grid=(8,), in_specs=[pl.BlockSpec((8, 4, RB)...]
where the time goes in v6:
time: 181 us
  waiting for transfers between devices  54.5 us (30%)
  blocking collectives  49.9 us (28%)
  starting transfers between devices  49.6 us (27%)
  Pallas kernels  26.7 us (15%)
    ppermute x29, waiting for transfers between devices, to(): return lax.ppermute(block, AXES, route)  54.5 us
    all_to_all x1, blocking collectives, on_device(): lax.all_to_all(packed, ('zx', 'pairs'), split_axis=0, concat_axis=0, tile...  49.9 us
    ppermute x29, starting transfers between devices, to(): return lax.ppermute(block, AXES, route)  49.6 us
    pallas_call x11, Pallas kernels, call(): pl.pallas_call(kernel, in_specs=ins, out_specs=[VMEM] * len(outs), out_sh...  12.5 us
    pallas_call x1, Pallas kernels, fill(): pl.pallas_call(fill_kernel, grid=(RH // step,), in_specs=[SMEM, rows, row...  4.65 us
  transfers between devices with their start and end apart: 29, of which 20 were waited for; matrix products, arithmetic and copies ran while one was open for 0% of the time, Pallas kernels for 4%

profile of v6, /device:TPU:0, one launch (start us, length us, event | category | flops | bytes accessed | tf_op | source)
XLA Modules:
  0.0 181.1 jit_solution(9094970497935556307)
XLA Ops:
  0.0 4.6 %fill.1 = (f32[256,1536]{1,0:T(8,128)S(1)}, f32[256,1536]{1,0:T(8,128)S(1)}) custom-call(s32[1]{0:T(128)} %bitcast.core_ref, f32[1536,512]{1,0:T(8,128)} %obs_ref.1, f32[1536,512]{1,0:T(8,128)} %est_ref.1, s32[1536,512]{1,0:T(8,128)} %mask_ref.1), custom_call_target="tpu_custom_call" | custom-call | flops 30000000 | bytes 15000000 | tf_op jit(solution)/shard_map/fill/pallas_call | solution.py:60
  4.7 0.1 collective-permute-start.1
  4.8 0.6 gram_first.1
  5.4 2.8 %collective-permute-done.1.x_ref.refs_5_ = f32[256,1536]{1,0:T(8,128)S(1)} collective-permute-done((f32[256,1536]{1,0:T(8,128)S(1)}, f32[256,1536]{1,0:T(8,128)S(1)}, u32[]{:S(2)}, u32[]{:S(2)}) %collective-permute-start.1) | collective-permute-done | bytes 1572896 | tf_op jit(solution)/shard_map/ppermute | solution.py:445
  8.1 0.7 gram_second.1
  8.8 1.7 collective-permute-start.2
  10.5 4.0 %collective-permute-done.2 = f32[264,128]{1,0:T(8,128)S(1)} collective-permute-done((f32[264,128]{1,0:T(8,128)S(1)}, f32[264,128]{1,0:T(8,128)S(1)}, u32[]{:S(2)}, u32[]{:S(2)}) %collective-permute-start.2) | collective-permute-done | bytes 135200 | tf_op jit(solution)/shard_map/ppermute | solution.py:445
  14.6 4.2 %collective-permute-start.5 = (f32[264,128]{1,0:T(8,128)S(1)}, f32[264,128]{1,0:T(8,128)S(1)}, u32[]{:S(2)}, u32[]{:S(2)}) collective-permute-start(f32[264,128]{1,0:T(8,128)S(1)} %add.12.refs_0_), channel_id=1, source_target_pairs={{0,96},{1,97},{2,98},{3,99},{4,100},{5,101},{6,102},{7,103},{8,104... | collective-permute-start | bytes 405512 | tf_op jit(solution)/shard_map/ppermute | solution.py:445
  18.8 0.9 collective-permute-start.3
  19.7 4.3 %collective-permute-done.5.refs_3_ = f32[264,128]{1,0:T(8,128)S(1)} collective-permute-done((f32[264,128]{1,0:T(8,128)S(1)}, f32[264,128]{1,0:T(8,128)S(1)}, u32[]{:S(2)}, u32[]{:S(2)}) %collective-permute-start.5) | collective-permute-done | bytes 135200 | tf_op jit(solution)/shard_map/ppermute | solution.py:445
  24.0 2.2 %collective-permute-done.4.refs_2_ = f32[264,128]{1,0:T(8,128)S(1)} collective-permute-done((f32[264,128]{1,0:T(8,128)S(1)}, f32[264,128]{1,0:T(8,128)S(1)}, u32[]{:S(2)}, u32[]{:S(2)}) %collective-permute-start.4) | collective-permute-done | bytes 135200 | tf_op jit(solution)/shard_map/ppermute | solution.py:445
  26.3 3.7 %whiten.3 = (f32[128,3072]{1,0:T(8,128)S(1)}, f32[128,3072]{1,0:T(8,128)S(1)}, f32[256,256]{1,0:T(8,128)S(1)}, f32[256,256]{1,0:T(8,128)S(1)}, f32[256,256]{1,0:T(8,128)S(1)}, /*index=5*/f32[256,128]{1,0:T(8,128)S(1)}) custom-call(f32[264,128]{1,0:T(8,128)S(1)} %add.12.refs_0_, f32[264,128]{1,0:T(8,128)S(1)} %collective-permute-done.3.refs_1_, ...), custom_call_target="tpu_custom_call" | custom-call | flops 30000001024 | bytes 6000000 | tf_op jit(solution)/shard_map/whiten/pallas_call | solution.py:241
  30.0 0.1 collective-permute-start.6
  30.0 7.3 %collective-permute-start.7 = (f32[128,3072]{1,0:T(8,128)S(1)}, f32[128,3072]{1,0:T(8,128)S(1)}, u32[]{:S(2)}, u32[]{:S(2)}) collective-permute-start(f32[128,3072]{1,0:T(8,128)S(1)} %get-tuple-element.45.k_ref.x0_ref), channel_id=1, source_target_pairs={{0,15},{1,8},{2,9},{3,10},{4,11},{5,12},{6,13},{7,14},{16,31},{17,... | collective-permute-start | bytes 4718600 | tf_op jit(solution)/shard_map/ppermute | solution.py:445
  37.4 1.9 %collective-permute-start = (f32[1,512]{1,0:T(1,128)S(1)}, f32[1,512]{1,0:T(1,128)S(1)}, u32[]{:S(2)}, u32[]{:S(2)}) collective-permute-start(f32[1,512]{1,0:T(1,128)S(1)} %bitcast.2), channel_id=1, source_target_pairs={{0,7},{1,0},{2,1},{3,2},{4,3},{5,4},{6,5},{7,6},{8,15},{9,8},{10,9... | collective-permute-start | bytes 6152 | tf_op jit(solution)/shard_map/ppermute | solution.py:445
  39.3 15.9 %collective-permute-done.refs_1_.thr_ref = f32[1,512]{1,0:T(1,128)S(1)} collective-permute-done((f32[1,512]{1,0:T(1,128)S(1)}, f32[1,512]{1,0:T(1,128)S(1)}, u32[]{:S(2)}, u32[]{:S(2)}) %collective-permute-start) | collective-permute-done | bytes 2080 | tf_op jit(solution)/shard_map/ppermute | solution.py:445
  55.2 0.7 gram_cross.1
  56.0 1.7 collective-permute-start.8
  57.7 0.6 diagonals.1
  58.3 0.1 collective-permute-start.12
  58.4 2.0 %collective-permute-done.8 = f32[128,128]{1,0:T(8,128)S(1)} collective-permute-done((f32[128,128]{1,0:T(8,128)S(1)}, f32[128,128]{1,0:T(8,128)S(1)}, u32[]{:S(2)}, u32[]{:S(2)}) %collective-permute-start.8) | collective-permute-done | bytes 65568 | tf_op jit(solution)/shard_map/ppermute | solution.py:445
  60.4 2.1 %collective-permute-start.11 = (f32[128,128]{1,0:T(8,128)S(1)}, f32[128,128]{1,0:T(8,128)S(1)}, u32[]{:S(2)}, u32[]{:S(2)}) collective-permute-start(f32[128,128]{1,0:T(8,128)S(1)} %add.13.refs_0_), channel_id=1, source_target_pairs={{0,96},{1,97},{2,98},{3,99},{4,100},{5,101},{6,102},{7,103},{8,104... | collective-permute-start | bytes 196616 | tf_op jit(solution)/shard_map/ppermute | solution.py:445
  62.5 0.3 collective-permute-start.10
  62.8 1.8 collective-permute-start.9
  64.5 1.8 collective-permute-done.12.refs_5_
  66.3 1.9 %collective-permute-done.10.refs_2_ = f32[128,128]{1,0:T(8,128)S(1)} collective-permute-done((f32[128,128]{1,0:T(8,128)S(1)}, f32[128,128]{1,0:T(8,128)S(1)}, u32[]{:S(2)}, u32[]{:S(2)}) %collective-permute-start.10) | collective-permute-done | bytes 65568 | tf_op jit(solution)/shard_map/ppermute | solution.py:445
  68.2 1.9 %whiten.4 = (f32[128,256]{1,0:T(8,128)S(1)}, f32[128,256]{1,0:T(8,128)S(1)}, f32[256,256]{1,0:T(8,128)S(1)}, f32[256,256]{1,0:T(8,128)S(1)}, f32[256,256]{1,0:T(8,128)S(1)}, /*index=5*/f32[256,128]{1,0:T(8,128)S(1)}) custom-call(f32[128,128]{1,0:T(8,128)S(1)} %add.13.refs_0_, f32[128,128]{1,0:T(8,128)S(1)} %collective-permute-done.9.refs_1_, ...), custom_call_target="tpu_custom_call" | custom-call | flops 30000001024 | bytes 6000000 | tf_op jit(solution)/shard_map/whiten/pallas_call | solution.py:241
  70.2 5.2 %collective-permute-start.13 = (f32[128,256]{1,0:T(8,128)S(1)}, f32[128,256]{1,0:T(8,128)S(1)}, u32[]{:S(2)}, u32[]{:S(2)}) collective-permute-start(f32[128,256]{1,0:T(8,128)S(1)} %get-tuple-element.53.w_ref), channel_id=1, source_target_pairs={{0,15},{1,8},{2,9},{3,10},{4,11},{5,12},{6,13},{7,14},{16,31},{17,... | collective-permute-start | bytes 393224 | tf_op jit(solution)/shard_map/ppermute | solution.py:445
  75.4 1.5 collective-permute-start.14
  76.9 1.3 kept_second.2
  78.2 3.8 %collective-permute-start.19 = (f32[128,384]{1,0:T(8,128)S(1)}, f32[128,384]{1,0:T(8,128)S(1)}, u32[]{:S(2)}, u32[]{:S(2)}) collective-permute-start(f32[128,384]{1,0:T(8,128)S(1)} %get-tuple-element.61), channel_id=1, source_target_pairs={{0,15},{1,8},{2,9},{3,10},{4,11},{5,12},{6,13},{7,14},{8,0},{9,1},... | collective-permute-start | bytes 589832 | tf_op jit(solution)/shard_map/ppermute | solution.py:445
  82.0 0.8 combine.2
  82.9 1.1 collective-permute-start.15
  84.0 0.7 collective-permute-start.21
  84.7 1.2 collective-permute-done.19
  85.9 2.2 %collective-permute-done.15 = f32[128,128]{1,0:T(8,128)S(1)} collective-permute-done((f32[128,128]{1,0:T(8,128)S(1)}, f32[128,128]{1,0:T(8,128)S(1)}, u32[]{:S(2)}, u32[]{:S(2)}) %collective-permute-start.15) | collective-permute-done | bytes 65568 | tf_op jit(solution)/shard_map/ppermute | solution.py:445
  88.1 1.3 collective-permute-start.18
  89.4 1.4 collective-permute-start.17
  90.8 1.4 collective-permute-start.16
  92.3 2.8 %collective-permute-done.18.refs_3_ = f32[128,128]{1,0:T(8,128)S(1)} collective-permute-done((f32[128,128]{1,0:T(8,128)S(1)}, f32[128,128]{1,0:T(8,128)S(1)}, u32[]{:S(2)}, u32[]{:S(2)}) %collective-permute-start.18) | collective-permute-done | bytes 65568 | tf_op jit(solution)/shard_map/ppermute | solution.py:445
  95.1 0.7 collective-permute-done.17.refs_2_
  95.7 0.2 collective-permute-done.16.refs_1_
  96.0 1.9 %whiten.5 = (f32[128,256]{1,0:T(8,128)S(1)}, f32[128,256]{1,0:T(8,128)S(1)}, f32[256,256]{1,0:T(8,128)S(1)}, f32[256,256]{1,0:T(8,128)S(1)}, f32[256,256]{1,0:T(8,128)S(1)}, /*index=5*/f32[256,128]{1,0:T(8,128)S(1)}) custom-call(f32[128,128]{1,0:T(8,128)S(1)} %add.14.refs_0_, f32[128,128]{1,0:T(8,128)S(1)} %collective-permute-done.16.refs_1_, ...), custom_call_target="tpu_custom_call" | custom-call | flops 30000001024 | bytes 6000000 | tf_op jit(solution)/shard_map/whiten/pallas_call | solution.py:241
  97.9 3.6 %collective-permute-start.20 = (f32[128,256]{1,0:T(8,128)S(1)}, f32[128,256]{1,0:T(8,128)S(1)}, u32[]{:S(2)}, u32[]{:S(2)}) collective-permute-start(f32[128,256]{1,0:T(8,128)S(1)} %get-tuple-element.63.w_ref), channel_id=1, source_target_pairs={{0,15},{1,8},{2,9},{3,10},{4,11},{5,12},{6,13},{7,14},{16,31},{17,... | collective-permute-start | bytes 393224 | tf_op jit(solution)/shard_map/ppermute | solution.py:445
  101.5 1.3 collective-permute-start.22
  102.8 1.3 kept_second.3
  104.1 0.5 collective-permute-start.27
  104.6 0.8 collective-permute-done.20.w_ref
  105.4 1.4 collective-permute-done.22.refs_2_
  106.8 0.9 combine.3
  107.7 1.1 collective-permute-start.23
  108.7 3.3 %collective-permute-done.23 = f32[128,128]{1,0:T(8,128)S(1)} collective-permute-done((f32[128,128]{1,0:T(8,128)S(1)}, f32[128,128]{1,0:T(8,128)S(1)}, u32[]{:S(2)}, u32[]{:S(2)}) %collective-permute-start.23) | collective-permute-done | bytes 65568 | tf_op jit(solution)/shard_map/ppermute | solution.py:445
  112.0 1.9 %collective-permute-start.26 = (f32[128,128]{1,0:T(8,128)S(1)}, f32[128,128]{1,0:T(8,128)S(1)}, u32[]{:S(2)}, u32[]{:S(2)}) collective-permute-start(f32[128,128]{1,0:T(8,128)S(1)} %add.15.refs_0_), channel_id=1, source_target_pairs={{0,96},{1,97},{2,98},{3,99},{4,100},{5,101},{6,102},{7,103},{8,104... | collective-permute-start | bytes 196616 | tf_op jit(solution)/shard_map/ppermute | solution.py:445
  114.0 1.1 collective-permute-start.25
  115.0 1.2 collective-permute-start.24
  116.2 1.4 collective-permute-done.26.refs_3_
  117.6 2.2 %collective-permute-done.25.refs_2_ = f32[128,128]{1,0:T(8,128)S(1)} collective-permute-done((f32[128,128]{1,0:T(8,128)S(1)}, f32[128,128]{1,0:T(8,128)S(1)}, u32[]{:S(2)}, u32[]{:S(2)}) %collective-permute-start.25) | collective-permute-done | bytes 65568 | tf_op jit(solution)/shard_map/ppermute | solution.py:445
  119.8 0.3 collective-permute-done.24.refs_1_
  120.1 3.1 %last.1 = (f32[128,3072]{1,0:T(8,128)S(1)}, f32[128,256]{1,0:T(8,128)S(1)}) custom-call(s32[1]{0:T(128)} %bitcast.core_ref, f32[1,512]{1,0:T(1,128)S(1)} %copy-done.1, f32[128,128]{1,0:T(8,128)S(1)} %add.15.refs_0_, f32[128,128]{1,0:T(8,128)S(1)} %collective-permute-done.24.refs_1_, f32[128,128]{1,0:T(8,128)S(1)} %collective-permute-done.25.refs_2_, ...), custom_call_target="tpu_custom_call" | custom-call | flops 30000001024 | bytes 6000000 | tf_op jit(solution)/shard_map/last/pallas_call | solution.py:375
  123.2 0.3 collective-permute-start.28
  123.6 3.2 %collective-permute-done.28.got_ref = f32[128,3072]{1,0:T(8,128)S(1)} collective-permute-done((f32[128,3072]{1,0:T(8,128)S(1)}, f32[128,3072]{1,0:T(8,128)S(1)}, u32[]{:S(2)}, u32[]{:S(2)}) %collective-permute-start.28) | collective-permute-done | bytes 1572896 | tf_op jit(solution)/shard_map/ppermute | solution.py:445
  126.7 1.0 last_kept.1
  127.7 49.9 %all_to_all.5.in_ref = f32[64,4,3072]{2,1,0:T(4,128)S(1)} all-to-all(f32[64,4,3072]{2,1,0:T(4,128)S(1)} %last_kept.1), channel_id=1, replica_groups=mesh['zx'=8,'core'=2,'pairs'=8] {'zx','pairs'}, dimensions={0} | all-to-all | bytes 6291456 | tf_op jit(solution)/shard_map/all_to_all | solution.py:509
  177.6 3.5 %place.1 = f32[32,24576]{1,0:T(8,128)} custom-call(f32[64,4,3072]{2,1,0:T(4,128)S(1)} %all_to_all.5.in_ref), custom_call_target="tpu_custom_call" | custom-call | flops 30000000 | bytes 6000000 | tf_op jit(solution)/shard_map/place/pallas_call | solution.py:424
  (26 shorter events, 0.1 us)
Async XLA Ops:
  4.7 3.5 %collective-permute-start.1 = (f32[256,1536]{1,0:T(8,128)S(1)}, f32[256,1536]{1,0:T(8,128)S(1)}, u32[]{:S(2)}, u32[]{:S(2)}) collective-permute-start(f32[256,1536]{1,0:T(8,128)S(1)} %get-tuple-element.41), channel_id=1, source_target_pairs={{0,8},{1,9},{2,10},{3,11},{4,12},{5,13},{6,14},{7,15},{8,0},{9,1},... | collective-permute-start | bytes 4718600 | tf_op jit(solution)/shard_map/ppermute | solution.py:445
  8.8 5.7 %collective-permute-start.2 = (f32[264,128]{1,0:T(8,128)S(1)}, f32[264,128]{1,0:T(8,128)S(1)}, u32[]{:S(2)}, u32[]{:S(2)}) collective-permute-start(f32[264,128]{1,0:T(8,128)S(1)} %gram_second.1), channel_id=1, source_target_pairs={{0,16},{1,17},{2,18},{3,19},{4,20},{5,21},{6,22},{7,23},{8,24},{9,... | collective-permute-start | bytes 405512 | tf_op jit(solution)/shard_map/ppermute | solution.py:445
  14.6 22.8 %copy-start.2 = (f32[512]{0:T(512)S(1)}, f32[512]{0:T(512)}, u32[]{:S(2)}) copy-start(f32[512]{0:T(512)} %param.7) | copy-start | bytes 6148
  14.6 9.5 %collective-permute-start.5 = (f32[264,128]{1,0:T(8,128)S(1)}, f32[264,128]{1,0:T(8,128)S(1)}, u32[]{:S(2)}, u32[]{:S(2)}) collective-permute-start(f32[264,128]{1,0:T(8,128)S(1)} %add.12.refs_0_), channel_id=1, source_target_pairs={{0,96},{1,97},{2,98},{3,99},{4,100},{5,101},{6,102},{7,103},{8,104... | collective-permute-start | bytes 405512 | tf_op jit(solution)/shard_map/ppermute | solution.py:445
  18.8 7.5 %collective-permute-start.4 = (f32[264,128]{1,0:T(8,128)S(1)}, f32[264,128]{1,0:T(8,128)S(1)}, u32[]{:S(2)}, u32[]{:S(2)}) collective-permute-start(f32[264,128]{1,0:T(8,128)S(1)} %add.12.refs_0_), channel_id=1, source_target_pairs={{0,64},{1,65},{2,66},{3,67},{4,68},{5,69},{6,70},{7,71},{8,72},{9,... | collective-permute-start | bytes 405512 | tf_op jit(solution)/shard_map/ppermute | solution.py:445
  18.8 7.5 %collective-permute-start.3 = (f32[264,128]{1,0:T(8,128)S(1)}, f32[264,128]{1,0:T(8,128)S(1)}, u32[]{:S(2)}, u32[]{:S(2)}) collective-permute-start(f32[264,128]{1,0:T(8,128)S(1)} %add.12.refs_0_), channel_id=1, source_target_pairs={{0,32},{1,33},{2,34},{3,35},{4,36},{5,37},{6,38},{7,39},{8,40},{9,... | collective-permute-start | bytes 405512 | tf_op jit(solution)/shard_map/ppermute | solution.py:445
  30.0 25.3 %collective-permute-start.6 = (f32[128,3072]{1,0:T(8,128)S(1)}, f32[128,3072]{1,0:T(8,128)S(1)}, u32[]{:S(2)}, u32[]{:S(2)}) collective-permute-start(f32[128,3072]{1,0:T(8,128)S(1)} %get-tuple-element.46.refs_1_.x1_ref), channel_id=1, source_target_pairs={{0,8},{1,9},{2,10},{3,11},{4,12},{5,13},{6,14},{7,15},{8,1},{9,2},... | collective-permute-start | bytes 4718600 | tf_op jit(solution)/shard_map/ppermute | solution.py:445
  30.0 25.2 %collective-permute-start.7 = (f32[128,3072]{1,0:T(8,128)S(1)}, f32[128,3072]{1,0:T(8,128)S(1)}, u32[]{:S(2)}, u32[]{:S(2)}) collective-permute-start(f32[128,3072]{1,0:T(8,128)S(1)} %get-tuple-element.45.k_ref.x0_ref), channel_id=1, source_target_pairs={{0,15},{1,8},{2,9},{3,10},{4,11},{5,12},{6,13},{7,14},{16,31},{17,... | collective-permute-start | bytes 4718600 | tf_op jit(solution)/shard_map/ppermute | solution.py:445
  37.4 17.8 %collective-permute-start = (f32[1,512]{1,0:T(1,128)S(1)}, f32[1,512]{1,0:T(1,128)S(1)}, u32[]{:S(2)}, u32[]{:S(2)}) collective-permute-start(f32[1,512]{1,0:T(1,128)S(1)} %bitcast.2), channel_id=1, source_target_pairs={{0,7},{1,0},{2,1},{3,2},{4,3},{5,4},{6,5},{7,6},{8,15},{9,8},{10,9... | collective-permute-start | bytes 6152 | tf_op jit(solution)/shard_map/ppermute | solution.py:445
  55.2 0.8 copy-start
  56.0 4.3 %collective-permute-start.8 = (f32[128,128]{1,0:T(8,128)S(1)}, f32[128,128]{1,0:T(8,128)S(1)}, u32[]{:S(2)}, u32[]{:S(2)}) collective-permute-start(f32[128,128]{1,0:T(8,128)S(1)} %gram_cross.1), channel_id=1, source_target_pairs={{0,16},{1,17},{2,18},{3,19},{4,20},{5,21},{6,22},{7,23},{8,24},{9,... | collective-permute-start | bytes 196616 | tf_op jit(solution)/shard_map/ppermute | solution.py:445
  58.3 8.0 %collective-permute-start.12 = (f32[128,128]{1,0:T(8,128)S(1)}, f32[128,128]{1,0:T(8,128)S(1)}, u32[]{:S(2)}, u32[]{:S(2)}) collective-permute-start(f32[128,128]{1,0:T(8,128)S(1)} %get-tuple-element.52), channel_id=1, source_target_pairs={{0,8},{1,9},{2,10},{3,11},{4,12},{5,13},{6,14},{7,15},{8,1},{9,2},... | collective-permute-start | bytes 196616 | tf_op jit(solution)/shard_map/ppermute | solution.py:445
  60.4 5.9 %collective-permute-start.11 = (f32[128,128]{1,0:T(8,128)S(1)}, f32[128,128]{1,0:T(8,128)S(1)}, u32[]{:S(2)}, u32[]{:S(2)}) collective-permute-start(f32[128,128]{1,0:T(8,128)S(1)} %add.13.refs_0_), channel_id=1, source_target_pairs={{0,96},{1,97},{2,98},{3,99},{4,100},{5,101},{6,102},{7,103},{8,104... | collective-permute-start | bytes 196616 | tf_op jit(solution)/shard_map/ppermute | solution.py:445
  62.5 5.8 %collective-permute-start.10 = (f32[128,128]{1,0:T(8,128)S(1)}, f32[128,128]{1,0:T(8,128)S(1)}, u32[]{:S(2)}, u32[]{:S(2)}) collective-permute-start(f32[128,128]{1,0:T(8,128)S(1)} %add.13.refs_0_), channel_id=1, source_target_pairs={{0,64},{1,65},{2,66},{3,67},{4,68},{5,69},{6,70},{7,71},{8,72},{9,... | collective-permute-start | bytes 196616 | tf_op jit(solution)/shard_map/ppermute | solution.py:445
  62.8 5.4 %collective-permute-start.9 = (f32[128,128]{1,0:T(8,128)S(1)}, f32[128,128]{1,0:T(8,128)S(1)}, u32[]{:S(2)}, u32[]{:S(2)}) collective-permute-start(f32[128,128]{1,0:T(8,128)S(1)} %add.13.refs_0_), channel_id=1, source_target_pairs={{0,32},{1,33},{2,34},{3,35},{4,36},{5,37},{6,38},{7,39},{8,40},{9,... | collective-permute-start | bytes 196616 | tf_op jit(solution)/shard_map/ppermute | solution.py:445
  70.2 11.8 %collective-permute-start.13 = (f32[128,256]{1,0:T(8,128)S(1)}, f32[128,256]{1,0:T(8,128)S(1)}, u32[]{:S(2)}, u32[]{:S(2)}) collective-permute-start(f32[128,256]{1,0:T(8,128)S(1)} %get-tuple-element.53.w_ref), channel_id=1, source_target_pairs={{0,15},{1,8},{2,9},{3,10},{4,11},{5,12},{6,13},{7,14},{16,31},{17,... | collective-permute-start | bytes 393224 | tf_op jit(solution)/shard_map/ppermute | solution.py:445
  75.4 6.6 %collective-permute-start.14 = (f32[128,3072]{1,0:T(8,128)S(1)}, f32[128,3072]{1,0:T(8,128)S(1)}, u32[]{:S(2)}, u32[]{:S(2)}) collective-permute-start(f32[128,3072]{1,0:T(8,128)S(1)} %given.2), channel_id=1, source_target_pairs={{8,0},{9,1},{10,2},{11,3},{12,4},{13,5},{14,6},{15,7},{24,16},{25,... | collective-permute-start | bytes 4718600 | tf_op jit(solution)/shard_map/ppermute | solution.py:445
  78.2 7.7 %collective-permute-start.19 = (f32[128,384]{1,0:T(8,128)S(1)}, f32[128,384]{1,0:T(8,128)S(1)}, u32[]{:S(2)}, u32[]{:S(2)}) collective-permute-start(f32[128,384]{1,0:T(8,128)S(1)} %get-tuple-element.61), channel_id=1, source_target_pairs={{0,15},{1,8},{2,9},{3,10},{4,11},{5,12},{6,13},{7,14},{8,0},{9,1},... | collective-permute-start | bytes 589832 | tf_op jit(solution)/shard_map/ppermute | solution.py:445
  82.9 5.2 %collective-permute-start.15 = (f32[128,128]{1,0:T(8,128)S(1)}, f32[128,128]{1,0:T(8,128)S(1)}, u32[]{:S(2)}, u32[]{:S(2)}) collective-permute-start(f32[128,128]{1,0:T(8,128)S(1)} %get-tuple-element.60), channel_id=1, source_target_pairs={{0,16},{1,17},{2,18},{3,19},{4,20},{5,21},{6,22},{7,23},{8,24},{9,... | collective-permute-start | bytes 196616 | tf_op jit(solution)/shard_map/ppermute | solution.py:445
  84.0 20.6 %collective-permute-start.21 = (f32[128,3072]{1,0:T(8,128)S(1)}, f32[128,3072]{1,0:T(8,128)S(1)}, u32[]{:S(2)}, u32[]{:S(2)}) collective-permute-start(f32[128,3072]{1,0:T(8,128)S(1)} %given.2), channel_id=1, source_target_pairs={{8,15},{9,8},{10,9},{11,10},{12,11},{13,12},{14,13},{15,14},{24,31... | collective-permute-start | bytes 4718600 | tf_op jit(solution)/shard_map/ppermute | solution.py:445
  88.1 7.0 %collective-permute-start.18 = (f32[128,128]{1,0:T(8,128)S(1)}, f32[128,128]{1,0:T(8,128)S(1)}, u32[]{:S(2)}, u32[]{:S(2)}) collective-permute-start(f32[128,128]{1,0:T(8,128)S(1)} %add.14.refs_0_), channel_id=1, source_target_pairs={{0,96},{1,97},{2,98},{3,99},{4,100},{5,101},{6,102},{7,103},{8,104... | collective-permute-start | bytes 196616 | tf_op jit(solution)/shard_map/ppermute | solution.py:445
  89.4 6.3 %collective-permute-start.17 = (f32[128,128]{1,0:T(8,128)S(1)}, f32[128,128]{1,0:T(8,128)S(1)}, u32[]{:S(2)}, u32[]{:S(2)}) collective-permute-start(f32[128,128]{1,0:T(8,128)S(1)} %add.14.refs_0_), channel_id=1, source_target_pairs={{0,64},{1,65},{2,66},{3,67},{4,68},{5,69},{6,70},{7,71},{8,72},{9,... | collective-permute-start | bytes 196616 | tf_op jit(solution)/shard_map/ppermute | solution.py:445
  90.8 5.1 %collective-permute-start.16 = (f32[128,128]{1,0:T(8,128)S(1)}, f32[128,128]{1,0:T(8,128)S(1)}, u32[]{:S(2)}, u32[]{:S(2)}) collective-permute-start(f32[128,128]{1,0:T(8,128)S(1)} %add.14.refs_0_), channel_id=1, source_target_pairs={{0,32},{1,33},{2,34},{3,35},{4,36},{5,37},{6,38},{7,39},{8,40},{9,... | collective-permute-start | bytes 196616 | tf_op jit(solution)/shard_map/ppermute | solution.py:445
  97.9 7.5 %collective-permute-start.20 = (f32[128,256]{1,0:T(8,128)S(1)}, f32[128,256]{1,0:T(8,128)S(1)}, u32[]{:S(2)}, u32[]{:S(2)}) collective-permute-start(f32[128,256]{1,0:T(8,128)S(1)} %get-tuple-element.63.w_ref), channel_id=1, source_target_pairs={{0,15},{1,8},{2,9},{3,10},{4,11},{5,12},{6,13},{7,14},{16,31},{17,... | collective-permute-start | bytes 393224 | tf_op jit(solution)/shard_map/ppermute | solution.py:445
  101.5 5.3 %collective-permute-start.22 = (f32[128,3072]{1,0:T(8,128)S(1)}, f32[128,3072]{1,0:T(8,128)S(1)}, u32[]{:S(2)}, u32[]{:S(2)}) collective-permute-start(f32[128,3072]{1,0:T(8,128)S(1)} %given.3), channel_id=1, source_target_pairs={{8,0},{9,1},{10,2},{11,3},{12,4},{13,5},{14,6},{15,7},{24,16},{25,... | collective-permute-start | bytes 4718600 | tf_op jit(solution)/shard_map/ppermute | solution.py:445
  104.1 12.1 %collective-permute-start.27 = (f32[128,384]{1,0:T(8,128)S(1)}, f32[128,384]{1,0:T(8,128)S(1)}, u32[]{:S(2)}, u32[]{:S(2)}) collective-permute-start(f32[128,384]{1,0:T(8,128)S(1)} %get-tuple-element.72), channel_id=1, source_target_pairs={{0,15},{1,8},{2,9},{3,10},{4,11},{5,12},{6,13},{7,14},{8,0},{9,1},... | collective-permute-start | bytes 589832 | tf_op jit(solution)/shard_map/ppermute | solution.py:445
  106.8 13.3 %copy-start.1 = (f32[1,512]{1,0:T(1,128)S(1)}, f32[1,512]{1,0:T(1,128)}, u32[]{:S(2)}) copy-start(f32[1,512]{1,0:T(1,128)} %copy-done) | copy-start | bytes 6148
  107.7 4.3 %collective-permute-start.23 = (f32[128,128]{1,0:T(8,128)S(1)}, f32[128,128]{1,0:T(8,128)S(1)}, u32[]{:S(2)}, u32[]{:S(2)}) collective-permute-start(f32[128,128]{1,0:T(8,128)S(1)} %get-tuple-element.71), channel_id=1, source_target_pairs={{0,16},{1,17},{2,18},{3,19},{4,20},{5,21},{6,22},{7,23},{8,24},{9,... | collective-permute-start | bytes 196616 | tf_op jit(solution)/shard_map/ppermute | solution.py:445
  112.0 5.6 %collective-permute-start.26 = (f32[128,128]{1,0:T(8,128)S(1)}, f32[128,128]{1,0:T(8,128)S(1)}, u32[]{:S(2)}, u32[]{:S(2)}) collective-permute-start(f32[128,128]{1,0:T(8,128)S(1)} %add.15.refs_0_), channel_id=1, source_target_pairs={{0,96},{1,97},{2,98},{3,99},{4,100},{5,101},{6,102},{7,103},{8,104... | collective-permute-start | bytes 196616 | tf_op jit(solution)/shard_map/ppermute | solution.py:445
  114.0 5.8 %collective-permute-start.25 = (f32[128,128]{1,0:T(8,128)S(1)}, f32[128,128]{1,0:T(8,128)S(1)}, u32[]{:S(2)}, u32[]{:S(2)}) collective-permute-start(f32[128,128]{1,0:T(8,128)S(1)} %add.15.refs_0_), channel_id=1, source_target_pairs={{0,64},{1,65},{2,66},{3,67},{4,68},{5,69},{6,70},{7,71},{8,72},{9,... | collective-permute-start | bytes 196616 | tf_op jit(solution)/shard_map/ppermute | solution.py:445
  115.0 5.1 %collective-permute-start.24 = (f32[128,128]{1,0:T(8,128)S(1)}, f32[128,128]{1,0:T(8,128)S(1)}, u32[]{:S(2)}, u32[]{:S(2)}) collective-permute-start(f32[128,128]{1,0:T(8,128)S(1)} %add.15.refs_0_), channel_id=1, source_target_pairs={{0,32},{1,33},{2,34},{3,35},{4,36},{5,37},{6,38},{7,39},{8,40},{9,... | collective-permute-start | bytes 196616 | tf_op jit(solution)/shard_map/ppermute | solution.py:445
  123.2 3.5 %collective-permute-start.28 = (f32[128,3072]{1,0:T(8,128)S(1)}, f32[128,3072]{1,0:T(8,128)S(1)}, u32[]{:S(2)}, u32[]{:S(2)}) collective-permute-start(f32[128,3072]{1,0:T(8,128)S(1)} %get-tuple-element.76), channel_id=1, source_target_pairs={{0,8},{1,9},{2,10},{3,11},{4,12},{5,13},{6,14},{7,15},{8,0},{9,1},... | collective-permute-start | bytes 4718600 | tf_op jit(solution)/shard_map/ppermute | solution.py:445

commit v7 on v6

--- a/solution.py
+++ b/solution.py
@@ -387,7 +387,7 @@
     core = core_ref[0]
     wh, wl = split(w_ref[...])
     both = jnp.concatenate([wh, wl], axis=0)
-    mine, other = core * 32, 32 - core * 32
+    mine, other = core * 4, 4 - core * 4
     for half in range(2):
         for j in range(0, RH, CH):
             xh, xl = split(columns((k_ref, m_ref), PLAIN, half, j))
@@ -395,10 +395,10 @@
             value = wide[:BW] + (wide[BW:] + mxu(wh, xl))
             at = pl.multiple_of((core * RH if half == 0 else RH - core * RH) + j, 128)
             for d in range(32):
-                out_ref[mine + d, :, pl.ds(at, CH)] = value[4 * d : 4 * d + 4]
+                out_ref[d % 8 * 8 + d // 8 + mine, :, pl.ds(at, CH)] = value[4 * d : 4 * d + 4]
     for j in range(0, RB, CH):
         for d in range(32):
-            out_ref[other + d, :, j : j + CH] = got_ref[4 * d : 4 * d + 4, j : j + CH]
+            out_ref[d % 8 * 8 + d // 8 + other, :, j : j + CH] = got_ref[4 * d : 4 * d + 4, j : j + CH]
 
 
 def last_kept(core, w, xs, got):
@@ -416,7 +416,7 @@
 def place_kernel(in_ref, out_ref):
     for w in range(4):
         for j in range(0, RB, CH):
-            rows = in_ref[:, w, j : j + CH]
+            rows = in_ref[:, 0, w, j : j + CH]
             out_ref[8 * w : 8 * w + 8, j : j + CH] = jnp.concatenate([rows[7:], rows[:7]], axis=0)
 
 
@@ -424,7 +424,7 @@
     return pl.pallas_call(
         place_kernel,
         grid=(8,),
-        in_specs=[pl.BlockSpec((8, 4, RB), lambda i: (i, 0, 0))],
+        in_specs=[pl.BlockSpec((8, 1, 4, RB), lambda i: (0, i, 0, 0))],
         out_specs=pl.BlockSpec((32, RB), lambda i: (0, i)),
         out_shape=jax.ShapeDtypeStruct((32, 8 * RB), F32),
         compiler_params=params(),
@@ -506,8 +506,8 @@
     send, w = last(core, thr, reduced(partial), diags, xs)
     got = swap_cores(send)
     packed = last_kept(core, w, xs, got)
-    landed = lax.all_to_all(packed, ("zx", "pairs"), split_axis=0, concat_axis=0, tiled=True)
-    return place(landed)
+    landed = lax.all_to_all(packed, ("pairs", "zx"), split_axis=0, concat_axis=0, tiled=True)
+    return place(landed.reshape(8, 8, 4, RB))
 
 
 def solution(mesh):

time: 181 us -> 181 us (level)
  no operation moved by 1% of the time
where the time goes in v7:
time: 181 us; the launch traced here: 180 us
  waiting for transfers between devices  54.5 us (30%)
  starting transfers between devices  49.6 us (27%)
  blocking collectives  49 us (27%)
  Pallas kernels  26.9 us (15%)
    ppermute x29, waiting for transfers between devices, to(): return lax.ppermute(block, AXES, route)  54.5 us
    ppermute x29, starting transfers between devices, to(): return lax.ppermute(block, AXES, route)  49.6 us
    all_to_all x1, blocking collectives, on_device(): lax.all_to_all(packed, ('pairs', 'zx'), split_axis=0, concat_axis=0, tile...  49 us
    pallas_call x11, Pallas kernels, call(): pl.pallas_call(kernel, in_specs=ins, out_specs=[VMEM] * len(outs), out_sh...  12.5 us
    pallas_call x1, Pallas kernels, fill(): pl.pallas_call(fill_kernel, grid=(RH // step,), in_specs=[SMEM, rows, row...  4.65 us
  transfers between devices with their start and end apart: 29, of which 20 were waited for; matrix products, arithmetic and copies ran while one was open for 0% of the time, Pallas kernels for 4%

profile of v7, /device:TPU:0, one launch (start us, length us, event | category | flops | bytes accessed | tf_op | source)
XLA Modules:
  0.0 180.3 jit_solution(10936779738048896462)
XLA Ops:
  0.0 4.6 %fill.1 = (f32[256,1536]{1,0:T(8,128)S(1)}, f32[256,1536]{1,0:T(8,128)S(1)}) custom-call(s32[1]{0:T(128)} %bitcast.core_ref, f32[1536,512]{1,0:T(8,128)} %obs_ref.1, f32[1536,512]{1,0:T(8,128)} %est_ref.1, s32[1536,512]{1,0:T(8,128)} %mask_ref.1), custom_call_target="tpu_custom_call" | custom-call | flops 30000000 | bytes 15000000 | tf_op jit(solution)/shard_map/fill/pallas_call | solution.py:60
  4.7 0.1 collective-permute-start.1
  4.8 0.6 gram_first.1
  5.4 2.8 %collective-permute-done.1.x_ref.refs_5_ = f32[256,1536]{1,0:T(8,128)S(1)} collective-permute-done((f32[256,1536]{1,0:T(8,128)S(1)}, f32[256,1536]{1,0:T(8,128)S(1)}, u32[]{:S(2)}, u32[]{:S(2)}) %collective-permute-start.1) | collective-permute-done | bytes 1572896 | tf_op jit(solution)/shard_map/ppermute | solution.py:445
  8.1 0.7 gram_second.1
  8.8 1.7 collective-permute-start.2
  10.5 4.0 %collective-permute-done.2 = f32[264,128]{1,0:T(8,128)S(1)} collective-permute-done((f32[264,128]{1,0:T(8,128)S(1)}, f32[264,128]{1,0:T(8,128)S(1)}, u32[]{:S(2)}, u32[]{:S(2)}) %collective-permute-start.2) | collective-permute-done | bytes 135200 | tf_op jit(solution)/shard_map/ppermute | solution.py:445
  14.6 4.2 %collective-permute-start.5 = (f32[264,128]{1,0:T(8,128)S(1)}, f32[264,128]{1,0:T(8,128)S(1)}, u32[]{:S(2)}, u32[]{:S(2)}) collective-permute-start(f32[264,128]{1,0:T(8,128)S(1)} %add.12.refs_0_), channel_id=1, source_target_pairs={{0,96},{1,97},{2,98},{3,99},{4,100},{5,101},{6,102},{7,103},{8,104... | collective-permute-start | bytes 405512 | tf_op jit(solution)/shard_map/ppermute | solution.py:445
  18.8 0.9 collective-permute-start.3
  19.7 4.3 %collective-permute-done.5.refs_3_ = f32[264,128]{1,0:T(8,128)S(1)} collective-permute-done((f32[264,128]{1,0:T(8,128)S(1)}, f32[264,128]{1,0:T(8,128)S(1)}, u32[]{:S(2)}, u32[]{:S(2)}) %collective-permute-start.5) | collective-permute-done | bytes 135200 | tf_op jit(solution)/shard_map/ppermute | solution.py:445
  24.0 2.2 %collective-permute-done.4.refs_2_ = f32[264,128]{1,0:T(8,128)S(1)} collective-permute-done((f32[264,128]{1,0:T(8,128)S(1)}, f32[264,128]{1,0:T(8,128)S(1)}, u32[]{:S(2)}, u32[]{:S(2)}) %collective-permute-start.4) | collective-permute-done | bytes 135200 | tf_op jit(solution)/shard_map/ppermute | solution.py:445
  26.3 3.7 %whiten.3 = (f32[128,3072]{1,0:T(8,128)S(1)}, f32[128,3072]{1,0:T(8,128)S(1)}, f32[256,256]{1,0:T(8,128)S(1)}, f32[256,256]{1,0:T(8,128)S(1)}, f32[256,256]{1,0:T(8,128)S(1)}, /*index=5*/f32[256,128]{1,0:T(8,128)S(1)}) custom-call(f32[264,128]{1,0:T(8,128)S(1)} %add.12.refs_0_, f32[264,128]{1,0:T(8,128)S(1)} %collective-permute-done.3.refs_1_, ...), custom_call_target="tpu_custom_call" | custom-call | flops 30000001024 | bytes 6000000 | tf_op jit(solution)/shard_map/whiten/pallas_call | solution.py:241
  30.0 0.1 collective-permute-start.6
  30.0 7.3 %collective-permute-start.7 = (f32[128,3072]{1,0:T(8,128)S(1)}, f32[128,3072]{1,0:T(8,128)S(1)}, u32[]{:S(2)}, u32[]{:S(2)}) collective-permute-start(f32[128,3072]{1,0:T(8,128)S(1)} %get-tuple-element.45.k_ref.x0_ref), channel_id=1, source_target_pairs={{0,15},{1,8},{2,9},{3,10},{4,11},{5,12},{6,13},{7,14},{16,31},{17,... | collective-permute-start | bytes 4718600 | tf_op jit(solution)/shard_map/ppermute | solution.py:445
  37.4 1.9 %collective-permute-start = (f32[1,512]{1,0:T(1,128)S(1)}, f32[1,512]{1,0:T(1,128)S(1)}, u32[]{:S(2)}, u32[]{:S(2)}) collective-permute-start(f32[1,512]{1,0:T(1,128)S(1)} %bitcast.4), channel_id=1, source_target_pairs={{0,7},{1,0},{2,1},{3,2},{4,3},{5,4},{6,5},{7,6},{8,15},{9,8},{10,9... | collective-permute-start | bytes 6152 | tf_op jit(solution)/shard_map/ppermute | solution.py:445
  39.3 15.9 %collective-permute-done.refs_1_.thr_ref = f32[1,512]{1,0:T(1,128)S(1)} collective-permute-done((f32[1,512]{1,0:T(1,128)S(1)}, f32[1,512]{1,0:T(1,128)S(1)}, u32[]{:S(2)}, u32[]{:S(2)}) %collective-permute-start) | collective-permute-done | bytes 2080 | tf_op jit(solution)/shard_map/ppermute | solution.py:445
  55.2 0.7 gram_cross.1
  56.0 1.7 collective-permute-start.8
  57.7 0.6 diagonals.1
  58.3 0.1 collective-permute-start.12
  58.4 2.0 %collective-permute-done.8 = f32[128,128]{1,0:T(8,128)S(1)} collective-permute-done((f32[128,128]{1,0:T(8,128)S(1)}, f32[128,128]{1,0:T(8,128)S(1)}, u32[]{:S(2)}, u32[]{:S(2)}) %collective-permute-start.8) | collective-permute-done | bytes 65568 | tf_op jit(solution)/shard_map/ppermute | solution.py:445
  60.4 2.1 %collective-permute-start.11 = (f32[128,128]{1,0:T(8,128)S(1)}, f32[128,128]{1,0:T(8,128)S(1)}, u32[]{:S(2)}, u32[]{:S(2)}) collective-permute-start(f32[128,128]{1,0:T(8,128)S(1)} %add.13.refs_0_), channel_id=1, source_target_pairs={{0,96},{1,97},{2,98},{3,99},{4,100},{5,101},{6,102},{7,103},{8,104... | collective-permute-start | bytes 196616 | tf_op jit(solution)/shard_map/ppermute | solution.py:445
  62.5 0.3 collective-permute-start.10
  62.8 1.8 collective-permute-start.9
  64.5 1.8 collective-permute-done.12.refs_5_
  66.3 1.9 %collective-permute-done.10.refs_2_ = f32[128,128]{1,0:T(8,128)S(1)} collective-permute-done((f32[128,128]{1,0:T(8,128)S(1)}, f32[128,128]{1,0:T(8,128)S(1)}, u32[]{:S(2)}, u32[]{:S(2)}) %collective-permute-start.10) | collective-permute-done | bytes 65568 | tf_op jit(solution)/shard_map/ppermute | solution.py:445
  68.2 1.9 %whiten.4 = (f32[128,256]{1,0:T(8,128)S(1)}, f32[128,256]{1,0:T(8,128)S(1)}, f32[256,256]{1,0:T(8,128)S(1)}, f32[256,256]{1,0:T(8,128)S(1)}, f32[256,256]{1,0:T(8,128)S(1)}, /*index=5*/f32[256,128]{1,0:T(8,128)S(1)}) custom-call(f32[128,128]{1,0:T(8,128)S(1)} %add.13.refs_0_, f32[128,128]{1,0:T(8,128)S(1)} %collective-permute-done.9.refs_1_, ...), custom_call_target="tpu_custom_call" | custom-call | flops 30000001024 | bytes 6000000 | tf_op jit(solution)/shard_map/whiten/pallas_call | solution.py:241
  70.2 5.2 %collective-permute-start.13 = (f32[128,256]{1,0:T(8,128)S(1)}, f32[128,256]{1,0:T(8,128)S(1)}, u32[]{:S(2)}, u32[]{:S(2)}) collective-permute-start(f32[128,256]{1,0:T(8,128)S(1)} %get-tuple-element.53.w_ref), channel_id=1, source_target_pairs={{0,15},{1,8},{2,9},{3,10},{4,11},{5,12},{6,13},{7,14},{16,31},{17,... | collective-permute-start | bytes 393224 | tf_op jit(solution)/shard_map/ppermute | solution.py:445
  75.4 1.5 collective-permute-start.14
  76.9 1.3 kept_second.2
  78.2 3.8 %collective-permute-start.19 = (f32[128,384]{1,0:T(8,128)S(1)}, f32[128,384]{1,0:T(8,128)S(1)}, u32[]{:S(2)}, u32[]{:S(2)}) collective-permute-start(f32[128,384]{1,0:T(8,128)S(1)} %get-tuple-element.61), channel_id=1, source_target_pairs={{0,15},{1,8},{2,9},{3,10},{4,11},{5,12},{6,13},{7,14},{8,0},{9,1},... | collective-permute-start | bytes 589832 | tf_op jit(solution)/shard_map/ppermute | solution.py:445
  82.0 0.8 combine.2
  82.9 1.1 collective-permute-start.15
  84.0 0.7 collective-permute-start.21
  84.7 1.2 collective-permute-done.19
  85.9 2.2 %collective-permute-done.15 = f32[128,128]{1,0:T(8,128)S(1)} collective-permute-done((f32[128,128]{1,0:T(8,128)S(1)}, f32[128,128]{1,0:T(8,128)S(1)}, u32[]{:S(2)}, u32[]{:S(2)}) %collective-permute-start.15) | collective-permute-done | bytes 65568 | tf_op jit(solution)/shard_map/ppermute | solution.py:445
  88.1 1.3 collective-permute-start.18
  89.4 1.4 collective-permute-start.17
  90.8 1.4 collective-permute-start.16
  92.3 2.8 %collective-permute-done.18.refs_3_ = f32[128,128]{1,0:T(8,128)S(1)} collective-permute-done((f32[128,128]{1,0:T(8,128)S(1)}, f32[128,128]{1,0:T(8,128)S(1)}, u32[]{:S(2)}, u32[]{:S(2)}) %collective-permute-start.18) | collective-permute-done | bytes 65568 | tf_op jit(solution)/shard_map/ppermute | solution.py:445
  95.1 0.7 collective-permute-done.17.refs_2_
  95.7 0.2 collective-permute-done.16.refs_1_
  96.0 1.9 %whiten.5 = (f32[128,256]{1,0:T(8,128)S(1)}, f32[128,256]{1,0:T(8,128)S(1)}, f32[256,256]{1,0:T(8,128)S(1)}, f32[256,256]{1,0:T(8,128)S(1)}, f32[256,256]{1,0:T(8,128)S(1)}, /*index=5*/f32[256,128]{1,0:T(8,128)S(1)}) custom-call(f32[128,128]{1,0:T(8,128)S(1)} %add.14.refs_0_, f32[128,128]{1,0:T(8,128)S(1)} %collective-permute-done.16.refs_1_, ...), custom_call_target="tpu_custom_call" | custom-call | flops 30000001024 | bytes 6000000 | tf_op jit(solution)/shard_map/whiten/pallas_call | solution.py:241
  97.9 3.6 %collective-permute-start.20 = (f32[128,256]{1,0:T(8,128)S(1)}, f32[128,256]{1,0:T(8,128)S(1)}, u32[]{:S(2)}, u32[]{:S(2)}) collective-permute-start(f32[128,256]{1,0:T(8,128)S(1)} %get-tuple-element.63.w_ref), channel_id=1, source_target_pairs={{0,15},{1,8},{2,9},{3,10},{4,11},{5,12},{6,13},{7,14},{16,31},{17,... | collective-permute-start | bytes 393224 | tf_op jit(solution)/shard_map/ppermute | solution.py:445
  101.5 1.3 collective-permute-start.22
  102.8 1.3 kept_second.3
  104.1 0.5 collective-permute-start.27
  104.6 0.8 collective-permute-done.20.w_ref
  105.4 1.4 collective-permute-done.22.refs_2_
  106.8 0.9 combine.3
  107.7 1.1 collective-permute-start.23
  108.7 3.3 %collective-permute-done.23 = f32[128,128]{1,0:T(8,128)S(1)} collective-permute-done((f32[128,128]{1,0:T(8,128)S(1)}, f32[128,128]{1,0:T(8,128)S(1)}, u32[]{:S(2)}, u32[]{:S(2)}) %collective-permute-start.23) | collective-permute-done | bytes 65568 | tf_op jit(solution)/shard_map/ppermute | solution.py:445
  112.0 1.9 %collective-permute-start.26 = (f32[128,128]{1,0:T(8,128)S(1)}, f32[128,128]{1,0:T(8,128)S(1)}, u32[]{:S(2)}, u32[]{:S(2)}) collective-permute-start(f32[128,128]{1,0:T(8,128)S(1)} %add.15.refs_0_), channel_id=1, source_target_pairs={{0,96},{1,97},{2,98},{3,99},{4,100},{5,101},{6,102},{7,103},{8,104... | collective-permute-start | bytes 196616 | tf_op jit(solution)/shard_map/ppermute | solution.py:445
  114.0 1.1 collective-permute-start.25
  115.0 1.2 collective-permute-start.24
  116.2 1.4 collective-permute-done.26.refs_3_
  117.6 2.2 %collective-permute-done.25.refs_2_ = f32[128,128]{1,0:T(8,128)S(1)} collective-permute-done((f32[128,128]{1,0:T(8,128)S(1)}, f32[128,128]{1,0:T(8,128)S(1)}, u32[]{:S(2)}, u32[]{:S(2)}) %collective-permute-start.25) | collective-permute-done | bytes 65568 | tf_op jit(solution)/shard_map/ppermute | solution.py:445
  119.8 0.3 collective-permute-done.24.refs_1_
  120.1 3.1 %last.1 = (f32[128,3072]{1,0:T(8,128)S(1)}, f32[128,256]{1,0:T(8,128)S(1)}) custom-call(s32[1]{0:T(128)} %bitcast.core_ref, f32[1,512]{1,0:T(1,128)S(1)} %copy-done.1, f32[128,128]{1,0:T(8,128)S(1)} %add.15.refs_0_, f32[128,128]{1,0:T(8,128)S(1)} %collective-permute-done.24.refs_1_, f32[128,128]{1,0:T(8,128)S(1)} %collective-permute-done.25.refs_2_, ...), custom_call_target="tpu_custom_call" | custom-call | flops 30000001024 | bytes 6000000 | tf_op jit(solution)/shard_map/last/pallas_call | solution.py:375
  123.2 0.3 collective-permute-start.28
  123.6 3.2 %collective-permute-done.28.got_ref = f32[128,3072]{1,0:T(8,128)S(1)} collective-permute-done((f32[128,3072]{1,0:T(8,128)S(1)}, f32[128,3072]{1,0:T(8,128)S(1)}, u32[]{:S(2)}, u32[]{:S(2)}) %collective-permute-start.28) | collective-permute-done | bytes 1572896 | tf_op jit(solution)/shard_map/ppermute | solution.py:445
  126.7 1.0 last_kept.1
  127.7 49.0 %all_to_all.5 = f32[64,4,3072]{2,1,0:T(4,128)S(1)} all-to-all(f32[64,4,3072]{2,1,0:T(4,128)S(1)} %last_kept.1), channel_id=1, replica_groups=mesh['zx'=8,'core'=2,'pairs'=8] {'pairs','zx'}, dimensions={0} | all-to-all | bytes 6291456 | tf_op jit(solution)/shard_map/all_to_all | solution.py:509
  176.7 3.6 %place.1 = f32[32,24576]{1,0:T(8,128)} custom-call(f32[8,8,4,3072]{3,2,1,0:T(4,128)S(1)} %bitcast.3), custom_call_target="tpu_custom_call" | custom-call | flops 30000000 | bytes 6000000 | tf_op jit(solution)/shard_map/place/pallas_call | solution.py:424
  (26 shorter events, 0.1 us)
Async XLA Ops:
  4.7 3.5 %collective-permute-start.1 = (f32[256,1536]{1,0:T(8,128)S(1)}, f32[256,1536]{1,0:T(8,128)S(1)}, u32[]{:S(2)}, u32[]{:S(2)}) collective-permute-start(f32[256,1536]{1,0:T(8,128)S(1)} %get-tuple-element.41), channel_id=1, source_target_pairs={{0,8},{1,9},{2,10},{3,11},{4,12},{5,13},{6,14},{7,15},{8,0},{9,1},... | collective-permute-start | bytes 4718600 | tf_op jit(solution)/shard_map/ppermute | solution.py:445
  8.8 5.7 %collective-permute-start.2 = (f32[264,128]{1,0:T(8,128)S(1)}, f32[264,128]{1,0:T(8,128)S(1)}, u32[]{:S(2)}, u32[]{:S(2)}) collective-permute-start(f32[264,128]{1,0:T(8,128)S(1)} %gram_second.1), channel_id=1, source_target_pairs={{0,16},{1,17},{2,18},{3,19},{4,20},{5,21},{6,22},{7,23},{8,24},{9,... | collective-permute-start | bytes 405512 | tf_op jit(solution)/shard_map/ppermute | solution.py:445
  14.6 22.8 %copy-start.2 = (f32[512]{0:T(512)S(1)}, f32[512]{0:T(512)}, u32[]{:S(2)}) copy-start(f32[512]{0:T(512)} %param.7) | copy-start | bytes 6148
  14.6 9.5 %collective-permute-start.5 = (f32[264,128]{1,0:T(8,128)S(1)}, f32[264,128]{1,0:T(8,128)S(1)}, u32[]{:S(2)}, u32[]{:S(2)}) collective-permute-start(f32[264,128]{1,0:T(8,128)S(1)} %add.12.refs_0_), channel_id=1, source_target_pairs={{0,96},{1,97},{2,98},{3,99},{4,100},{5,101},{6,102},{7,103},{8,104... | collective-permute-start | bytes 405512 | tf_op jit(solution)/shard_map/ppermute | solution.py:445
  18.8 7.5 %collective-permute-start.4 = (f32[264,128]{1,0:T(8,128)S(1)}, f32[264,128]{1,0:T(8,128)S(1)}, u32[]{:S(2)}, u32[]{:S(2)}) collective-permute-start(f32[264,128]{1,0:T(8,128)S(1)} %add.12.refs_0_), channel_id=1, source_target_pairs={{0,64},{1,65},{2,66},{3,67},{4,68},{5,69},{6,70},{7,71},{8,72},{9,... | collective-permute-start | bytes 405512 | tf_op jit(solution)/shard_map/ppermute | solution.py:445
  18.8 7.5 %collective-permute-start.3 = (f32[264,128]{1,0:T(8,128)S(1)}, f32[264,128]{1,0:T(8,128)S(1)}, u32[]{:S(2)}, u32[]{:S(2)}) collective-permute-start(f32[264,128]{1,0:T(8,128)S(1)} %add.12.refs_0_), channel_id=1, source_target_pairs={{0,32},{1,33},{2,34},{3,35},{4,36},{5,37},{6,38},{7,39},{8,40},{9,... | collective-permute-start | bytes 405512 | tf_op jit(solution)/shard_map/ppermute | solution.py:445
  30.0 25.3 %collective-permute-start.6 = (f32[128,3072]{1,0:T(8,128)S(1)}, f32[128,3072]{1,0:T(8,128)S(1)}, u32[]{:S(2)}, u32[]{:S(2)}) collective-permute-start(f32[128,3072]{1,0:T(8,128)S(1)} %get-tuple-element.46.refs_1_.x1_ref), channel_id=1, source_target_pairs={{0,8},{1,9},{2,10},{3,11},{4,12},{5,13},{6,14},{7,15},{8,1},{9,2},... | collective-permute-start | bytes 4718600 | tf_op jit(solution)/shard_map/ppermute | solution.py:445
  30.0 25.2 %collective-permute-start.7 = (f32[128,3072]{1,0:T(8,128)S(1)}, f32[128,3072]{1,0:T(8,128)S(1)}, u32[]{:S(2)}, u32[]{:S(2)}) collective-permute-start(f32[128,3072]{1,0:T(8,128)S(1)} %get-tuple-element.45.k_ref.x0_ref), channel_id=1, source_target_pairs={{0,15},{1,8},{2,9},{3,10},{4,11},{5,12},{6,13},{7,14},{16,31},{17,... | collective-permute-start | bytes 4718600 | tf_op jit(solution)/shard_map/ppermute | solution.py:445
  37.4 17.8 %collective-permute-start = (f32[1,512]{1,0:T(1,128)S(1)}, f32[1,512]{1,0:T(1,128)S(1)}, u32[]{:S(2)}, u32[]{:S(2)}) collective-permute-start(f32[1,512]{1,0:T(1,128)S(1)} %bitcast.4), channel_id=1, source_target_pairs={{0,7},{1,0},{2,1},{3,2},{4,3},{5,4},{6,5},{7,6},{8,15},{9,8},{10,9... | collective-permute-start | bytes 6152 | tf_op jit(solution)/shard_map/ppermute | solution.py:445
  55.2 0.8 copy-start
  56.0 4.3 %collective-permute-start.8 = (f32[128,128]{1,0:T(8,128)S(1)}, f32[128,128]{1,0:T(8,128)S(1)}, u32[]{:S(2)}, u32[]{:S(2)}) collective-permute-start(f32[128,128]{1,0:T(8,128)S(1)} %gram_cross.1), channel_id=1, source_target_pairs={{0,16},{1,17},{2,18},{3,19},{4,20},{5,21},{6,22},{7,23},{8,24},{9,... | collective-permute-start | bytes 196616 | tf_op jit(solution)/shard_map/ppermute | solution.py:445
  58.3 8.0 %collective-permute-start.12 = (f32[128,128]{1,0:T(8,128)S(1)}, f32[128,128]{1,0:T(8,128)S(1)}, u32[]{:S(2)}, u32[]{:S(2)}) collective-permute-start(f32[128,128]{1,0:T(8,128)S(1)} %get-tuple-element.52), channel_id=1, source_target_pairs={{0,8},{1,9},{2,10},{3,11},{4,12},{5,13},{6,14},{7,15},{8,1},{9,2},... | collective-permute-start | bytes 196616 | tf_op jit(solution)/shard_map/ppermute | solution.py:445
  60.4 5.9 %collective-permute-start.11 = (f32[128,128]{1,0:T(8,128)S(1)}, f32[128,128]{1,0:T(8,128)S(1)}, u32[]{:S(2)}, u32[]{:S(2)}) collective-permute-start(f32[128,128]{1,0:T(8,128)S(1)} %add.13.refs_0_), channel_id=1, source_target_pairs={{0,96},{1,97},{2,98},{3,99},{4,100},{5,101},{6,102},{7,103},{8,104... | collective-permute-start | bytes 196616 | tf_op jit(solution)/shard_map/ppermute | solution.py:445
  62.5 5.8 %collective-permute-start.10 = (f32[128,128]{1,0:T(8,128)S(1)}, f32[128,128]{1,0:T(8,128)S(1)}, u32[]{:S(2)}, u32[]{:S(2)}) collective-permute-start(f32[128,128]{1,0:T(8,128)S(1)} %add.13.refs_0_), channel_id=1, source_target_pairs={{0,64},{1,65},{2,66},{3,67},{4,68},{5,69},{6,70},{7,71},{8,72},{9,... | collective-permute-start | bytes 196616 | tf_op jit(solution)/shard_map/ppermute | solution.py:445
  62.8 5.4 %collective-permute-start.9 = (f32[128,128]{1,0:T(8,128)S(1)}, f32[128,128]{1,0:T(8,128)S(1)}, u32[]{:S(2)}, u32[]{:S(2)}) collective-permute-start(f32[128,128]{1,0:T(8,128)S(1)} %add.13.refs_0_), channel_id=1, source_target_pairs={{0,32},{1,33},{2,34},{3,35},{4,36},{5,37},{6,38},{7,39},{8,40},{9,... | collective-permute-start | bytes 196616 | tf_op jit(solution)/shard_map/ppermute | solution.py:445
  70.2 11.8 %collective-permute-start.13 = (f32[128,256]{1,0:T(8,128)S(1)}, f32[128,256]{1,0:T(8,128)S(1)}, u32[]{:S(2)}, u32[]{:S(2)}) collective-permute-start(f32[128,256]{1,0:T(8,128)S(1)} %get-tuple-element.53.w_ref), channel_id=1, source_target_pairs={{0,15},{1,8},{2,9},{3,10},{4,11},{5,12},{6,13},{7,14},{16,31},{17,... | collective-permute-start | bytes 393224 | tf_op jit(solution)/shard_map/ppermute | solution.py:445
  75.4 6.6 %collective-permute-start.14 = (f32[128,3072]{1,0:T(8,128)S(1)}, f32[128,3072]{1,0:T(8,128)S(1)}, u32[]{:S(2)}, u32[]{:S(2)}) collective-permute-start(f32[128,3072]{1,0:T(8,128)S(1)} %given.2), channel_id=1, source_target_pairs={{8,0},{9,1},{10,2},{11,3},{12,4},{13,5},{14,6},{15,7},{24,16},{25,... | collective-permute-start | bytes 4718600 | tf_op jit(solution)/shard_map/ppermute | solution.py:445
  78.2 7.7 %collective-permute-start.19 = (f32[128,384]{1,0:T(8,128)S(1)}, f32[128,384]{1,0:T(8,128)S(1)}, u32[]{:S(2)}, u32[]{:S(2)}) collective-permute-start(f32[128,384]{1,0:T(8,128)S(1)} %get-tuple-element.61), channel_id=1, source_target_pairs={{0,15},{1,8},{2,9},{3,10},{4,11},{5,12},{6,13},{7,14},{8,0},{9,1},... | collective-permute-start | bytes 589832 | tf_op jit(solution)/shard_map/ppermute | solution.py:445
  82.9 5.2 %collective-permute-start.15 = (f32[128,128]{1,0:T(8,128)S(1)}, f32[128,128]{1,0:T(8,128)S(1)}, u32[]{:S(2)}, u32[]{:S(2)}) collective-permute-start(f32[128,128]{1,0:T(8,128)S(1)} %get-tuple-element.60), channel_id=1, source_target_pairs={{0,16},{1,17},{2,18},{3,19},{4,20},{5,21},{6,22},{7,23},{8,24},{9,... | collective-permute-start | bytes 196616 | tf_op jit(solution)/shard_map/ppermute | solution.py:445
  84.0 20.6 %collective-permute-start.21 = (f32[128,3072]{1,0:T(8,128)S(1)}, f32[128,3072]{1,0:T(8,128)S(1)}, u32[]{:S(2)}, u32[]{:S(2)}) collective-permute-start(f32[128,3072]{1,0:T(8,128)S(1)} %given.2), channel_id=1, source_target_pairs={{8,15},{9,8},{10,9},{11,10},{12,11},{13,12},{14,13},{15,14},{24,31... | collective-permute-start | bytes 4718600 | tf_op jit(solution)/shard_map/ppermute | solution.py:445
  88.1 7.0 %collective-permute-start.18 = (f32[128,128]{1,0:T(8,128)S(1)}, f32[128,128]{1,0:T(8,128)S(1)}, u32[]{:S(2)}, u32[]{:S(2)}) collective-permute-start(f32[128,128]{1,0:T(8,128)S(1)} %add.14.refs_0_), channel_id=1, source_target_pairs={{0,96},{1,97},{2,98},{3,99},{4,100},{5,101},{6,102},{7,103},{8,104... | collective-permute-start | bytes 196616 | tf_op jit(solution)/shard_map/ppermute | solution.py:445
  89.4 6.3 %collective-permute-start.17 = (f32[128,128]{1,0:T(8,128)S(1)}, f32[128,128]{1,0:T(8,128)S(1)}, u32[]{:S(2)}, u32[]{:S(2)}) collective-permute-start(f32[128,128]{1,0:T(8,128)S(1)} %add.14.refs_0_), channel_id=1, source_target_pairs={{0,64},{1,65},{2,66},{3,67},{4,68},{5,69},{6,70},{7,71},{8,72},{9,... | collective-permute-start | bytes 196616 | tf_op jit(solution)/shard_map/ppermute | solution.py:445
  90.8 5.1 %collective-permute-start.16 = (f32[128,128]{1,0:T(8,128)S(1)}, f32[128,128]{1,0:T(8,128)S(1)}, u32[]{:S(2)}, u32[]{:S(2)}) collective-permute-start(f32[128,128]{1,0:T(8,128)S(1)} %add.14.refs_0_), channel_id=1, source_target_pairs={{0,32},{1,33},{2,34},{3,35},{4,36},{5,37},{6,38},{7,39},{8,40},{9,... | collective-permute-start | bytes 196616 | tf_op jit(solution)/shard_map/ppermute | solution.py:445
  97.9 7.5 %collective-permute-start.20 = (f32[128,256]{1,0:T(8,128)S(1)}, f32[128,256]{1,0:T(8,128)S(1)}, u32[]{:S(2)}, u32[]{:S(2)}) collective-permute-start(f32[128,256]{1,0:T(8,128)S(1)} %get-tuple-element.63.w_ref), channel_id=1, source_target_pairs={{0,15},{1,8},{2,9},{3,10},{4,11},{5,12},{6,13},{7,14},{16,31},{17,... | collective-permute-start | bytes 393224 | tf_op jit(solution)/shard_map/ppermute | solution.py:445
  101.5 5.3 %collective-permute-start.22 = (f32[128,3072]{1,0:T(8,128)S(1)}, f32[128,3072]{1,0:T(8,128)S(1)}, u32[]{:S(2)}, u32[]{:S(2)}) collective-permute-start(f32[128,3072]{1,0:T(8,128)S(1)} %given.3), channel_id=1, source_target_pairs={{8,0},{9,1},{10,2},{11,3},{12,4},{13,5},{14,6},{15,7},{24,16},{25,... | collective-permute-start | bytes 4718600 | tf_op jit(solution)/shard_map/ppermute | solution.py:445
  104.1 12.1 %collective-permute-start.27 = (f32[128,384]{1,0:T(8,128)S(1)}, f32[128,384]{1,0:T(8,128)S(1)}, u32[]{:S(2)}, u32[]{:S(2)}) collective-permute-start(f32[128,384]{1,0:T(8,128)S(1)} %get-tuple-element.72), channel_id=1, source_target_pairs={{0,15},{1,8},{2,9},{3,10},{4,11},{5,12},{6,13},{7,14},{8,0},{9,1},... | collective-permute-start | bytes 589832 | tf_op jit(solution)/shard_map/ppermute | solution.py:445
  106.8 13.3 %copy-start.1 = (f32[1,512]{1,0:T(1,128)S(1)}, f32[1,512]{1,0:T(1,128)}, u32[]{:S(2)}) copy-start(f32[1,512]{1,0:T(1,128)} %copy-done) | copy-start | bytes 6148
  107.7 4.3 %collective-permute-start.23 = (f32[128,128]{1,0:T(8,128)S(1)}, f32[128,128]{1,0:T(8,128)S(1)}, u32[]{:S(2)}, u32[]{:S(2)}) collective-permute-start(f32[128,128]{1,0:T(8,128)S(1)} %get-tuple-element.71), channel_id=1, source_target_pairs={{0,16},{1,17},{2,18},{3,19},{4,20},{5,21},{6,22},{7,23},{8,24},{9,... | collective-permute-start | bytes 196616 | tf_op jit(solution)/shard_map/ppermute | solution.py:445
  112.0 5.6 %collective-permute-start.26 = (f32[128,128]{1,0:T(8,128)S(1)}, f32[128,128]{1,0:T(8,128)S(1)}, u32[]{:S(2)}, u32[]{:S(2)}) collective-permute-start(f32[128,128]{1,0:T(8,128)S(1)} %add.15.refs_0_), channel_id=1, source_target_pairs={{0,96},{1,97},{2,98},{3,99},{4,100},{5,101},{6,102},{7,103},{8,104... | collective-permute-start | bytes 196616 | tf_op jit(solution)/shard_map/ppermute | solution.py:445
  114.0 5.8 %collective-permute-start.25 = (f32[128,128]{1,0:T(8,128)S(1)}, f32[128,128]{1,0:T(8,128)S(1)}, u32[]{:S(2)}, u32[]{:S(2)}) collective-permute-start(f32[128,128]{1,0:T(8,128)S(1)} %add.15.refs_0_), channel_id=1, source_target_pairs={{0,64},{1,65},{2,66},{3,67},{4,68},{5,69},{6,70},{7,71},{8,72},{9,... | collective-permute-start | bytes 196616 | tf_op jit(solution)/shard_map/ppermute | solution.py:445
  115.0 5.1 %collective-permute-start.24 = (f32[128,128]{1,0:T(8,128)S(1)}, f32[128,128]{1,0:T(8,128)S(1)}, u32[]{:S(2)}, u32[]{:S(2)}) collective-permute-start(f32[128,128]{1,0:T(8,128)S(1)} %add.15.refs_0_), channel_id=1, source_target_pairs={{0,32},{1,33},{2,34},{3,35},{4,36},{5,37},{6,38},{7,39},{8,40},{9,... | collective-permute-start | bytes 196616 | tf_op jit(solution)/shard_map/ppermute | solution.py:445
  123.2 3.5 %collective-permute-start.28 = (f32[128,3072]{1,0:T(8,128)S(1)}, f32[128,3072]{1,0:T(8,128)S(1)}, u32[]{:S(2)}, u32[]{:S(2)}) collective-permute-start(f32[128,3072]{1,0:T(8,128)S(1)} %get-tuple-element.76), channel_id=1, source_target_pairs={{0,8},{1,9},{2,10},{3,11},{4,12},{5,13},{6,14},{7,15},{8,0},{9,1},... | collective-permute-start | bytes 4718600 | tf_op jit(solution)/shard_map/ppermute | solution.py:445

commit v8 on v7

--- a/solution.py
+++ b/solution.py
@@ -11,7 +11,7 @@
 PW = 2 * BW
 RH = 1536
 RB = 2 * RH
-CH = 512
+CH = 768
 AXES = ("zx", "core", "pairs")
 F32 = jnp.float32
 BF16 = jnp.bfloat16

time: 181 us -> 180 us (level)
  no operation moved by 1% of the time
where the time goes in v8:
time: 180 us
  waiting for transfers between devices  54.8 us (30%)
  starting transfers between devices  49.4 us (27%)
  blocking collectives  48.7 us (27%)
  Pallas kernels  26.8 us (15%)
    ppermute x29, waiting for transfers between devices, to(): return lax.ppermute(block, AXES, route)  54.8 us
    ppermute x29, starting transfers between devices, to(): return lax.ppermute(block, AXES, route)  49.4 us
    all_to_all x1, blocking collectives, on_device(): lax.all_to_all(packed, ('pairs', 'zx'), split_axis=0, concat_axis=0, tile...  48.7 us
    pallas_call x11, Pallas kernels, call(): pl.pallas_call(kernel, in_specs=ins, out_specs=[VMEM] * len(outs), out_sh...  12.3 us
    pallas_call x1, Pallas kernels, fill(): pl.pallas_call(fill_kernel, grid=(RH // step,), in_specs=[SMEM, rows, row...  4.65 us
    pallas_call x1, Pallas kernels, place(): pl.pallas_call(place_kernel, grid=(8,), in_specs=[pl.BlockSpec((8, 1, 4,...  3.67 us
  transfers between devices with their start and end apart: 29, of which 20 were waited for; matrix products, arithmetic and copies ran while one was open for 0% of the time, Pallas kernels for 4%

profile of v8, /device:TPU:0, one launch (start us, length us, event | category | flops | bytes accessed | tf_op | source)
XLA Modules:
  0.0 180.0 jit_solution(16191663682814167242)
XLA Ops:
  0.0 4.6 %fill.1 = (f32[256,1536]{1,0:T(8,128)S(1)}, f32[256,1536]{1,0:T(8,128)S(1)}) custom-call(s32[1]{0:T(128)} %bitcast.core_ref, f32[1536,512]{1,0:T(8,128)} %obs_ref.1, f32[1536,512]{1,0:T(8,128)} %est_ref.1, s32[1536,512]{1,0:T(8,128)} %mask_ref.1), custom_call_target="tpu_custom_call" | custom-call | flops 30000000 | bytes 15000000 | tf_op jit(solution)/shard_map/fill/pallas_call | solution.py:60
  4.7 0.1 collective-permute-start.1
  4.8 0.6 gram_first.1
  5.4 2.8 %collective-permute-done.1.x_ref.refs_5_ = f32[256,1536]{1,0:T(8,128)S(1)} collective-permute-done((f32[256,1536]{1,0:T(8,128)S(1)}, f32[256,1536]{1,0:T(8,128)S(1)}, u32[]{:S(2)}, u32[]{:S(2)}) %collective-permute-start.1) | collective-permute-done | bytes 1572896 | tf_op jit(solution)/shard_map/ppermute | solution.py:445
  8.1 0.7 gram_second.1
  8.9 1.7 collective-permute-start.2
  10.5 4.0 %collective-permute-done.2 = f32[264,128]{1,0:T(8,128)S(1)} collective-permute-done((f32[264,128]{1,0:T(8,128)S(1)}, f32[264,128]{1,0:T(8,128)S(1)}, u32[]{:S(2)}, u32[]{:S(2)}) %collective-permute-start.2) | collective-permute-done | bytes 135200 | tf_op jit(solution)/shard_map/ppermute | solution.py:445
  14.6 4.2 %collective-permute-start.5 = (f32[264,128]{1,0:T(8,128)S(1)}, f32[264,128]{1,0:T(8,128)S(1)}, u32[]{:S(2)}, u32[]{:S(2)}) collective-permute-start(f32[264,128]{1,0:T(8,128)S(1)} %add.12.refs_0_), channel_id=1, source_target_pairs={{0,96},{1,97},{2,98},{3,99},{4,100},{5,101},{6,102},{7,103},{8,104... | collective-permute-start | bytes 405512 | tf_op jit(solution)/shard_map/ppermute | solution.py:445
  18.8 0.9 collective-permute-start.3
  19.7 4.3 %collective-permute-done.5.refs_3_ = f32[264,128]{1,0:T(8,128)S(1)} collective-permute-done((f32[264,128]{1,0:T(8,128)S(1)}, f32[264,128]{1,0:T(8,128)S(1)}, u32[]{:S(2)}, u32[]{:S(2)}) %collective-permute-start.5) | collective-permute-done | bytes 135200 | tf_op jit(solution)/shard_map/ppermute | solution.py:445
  24.0 2.2 %collective-permute-done.4.refs_2_ = f32[264,128]{1,0:T(8,128)S(1)} collective-permute-done((f32[264,128]{1,0:T(8,128)S(1)}, f32[264,128]{1,0:T(8,128)S(1)}, u32[]{:S(2)}, u32[]{:S(2)}) %collective-permute-start.4) | collective-permute-done | bytes 135200 | tf_op jit(solution)/shard_map/ppermute | solution.py:445
  26.3 3.5 %whiten.3 = (f32[128,3072]{1,0:T(8,128)S(1)}, f32[128,3072]{1,0:T(8,128)S(1)}, f32[256,256]{1,0:T(8,128)S(1)}, f32[256,256]{1,0:T(8,128)S(1)}, f32[256,256]{1,0:T(8,128)S(1)}, /*index=5*/f32[256,128]{1,0:T(8,128)S(1)}) custom-call(f32[264,128]{1,0:T(8,128)S(1)} %add.12.refs_0_, f32[264,128]{1,0:T(8,128)S(1)} %collective-permute-done.3.refs_1_, ...), custom_call_target="tpu_custom_call" | custom-call | flops 30000001024 | bytes 6000000 | tf_op jit(solution)/shard_map/whiten/pallas_call | solution.py:241
  29.8 0.1 collective-permute-start.6
  29.9 7.3 %collective-permute-start.7 = (f32[128,3072]{1,0:T(8,128)S(1)}, f32[128,3072]{1,0:T(8,128)S(1)}, u32[]{:S(2)}, u32[]{:S(2)}) collective-permute-start(f32[128,3072]{1,0:T(8,128)S(1)} %get-tuple-element.45.k_ref.x0_ref), channel_id=1, source_target_pairs={{0,15},{1,8},{2,9},{3,10},{4,11},{5,12},{6,13},{7,14},{16,31},{17,... | collective-permute-start | bytes 4718600 | tf_op jit(solution)/shard_map/ppermute | solution.py:445
  37.2 1.9 %collective-permute-start = (f32[1,512]{1,0:T(1,128)S(1)}, f32[1,512]{1,0:T(1,128)S(1)}, u32[]{:S(2)}, u32[]{:S(2)}) collective-permute-start(f32[1,512]{1,0:T(1,128)S(1)} %bitcast.4), channel_id=1, source_target_pairs={{0,7},{1,0},{2,1},{3,2},{4,3},{5,4},{6,5},{7,6},{8,15},{9,8},{10,9... | collective-permute-start | bytes 6152 | tf_op jit(solution)/shard_map/ppermute | solution.py:445
  39.1 15.9 %collective-permute-done.refs_1_.thr_ref = f32[1,512]{1,0:T(1,128)S(1)} collective-permute-done((f32[1,512]{1,0:T(1,128)S(1)}, f32[1,512]{1,0:T(1,128)S(1)}, u32[]{:S(2)}, u32[]{:S(2)}) %collective-permute-start) | collective-permute-done | bytes 2080 | tf_op jit(solution)/shard_map/ppermute | solution.py:445
  55.1 0.8 gram_cross.1
  55.8 1.6 collective-permute-start.8
  57.5 0.6 diagonals.1
  58.1 0.1 collective-permute-start.12
  58.2 2.0 %collective-permute-done.8 = f32[128,128]{1,0:T(8,128)S(1)} collective-permute-done((f32[128,128]{1,0:T(8,128)S(1)}, f32[128,128]{1,0:T(8,128)S(1)}, u32[]{:S(2)}, u32[]{:S(2)}) %collective-permute-start.8) | collective-permute-done | bytes 65568 | tf_op jit(solution)/shard_map/ppermute | solution.py:445
  60.2 2.1 %collective-permute-start.11 = (f32[128,128]{1,0:T(8,128)S(1)}, f32[128,128]{1,0:T(8,128)S(1)}, u32[]{:S(2)}, u32[]{:S(2)}) collective-permute-start(f32[128,128]{1,0:T(8,128)S(1)} %add.13.refs_0_), channel_id=1, source_target_pairs={{0,96},{1,97},{2,98},{3,99},{4,100},{5,101},{6,102},{7,103},{8,104... | collective-permute-start | bytes 196616 | tf_op jit(solution)/shard_map/ppermute | solution.py:445
  62.3 0.3 collective-permute-start.10
  62.6 1.8 collective-permute-start.9
  64.4 1.7 collective-permute-done.12.refs_5_
  66.0 2.0 %collective-permute-done.10.refs_2_ = f32[128,128]{1,0:T(8,128)S(1)} collective-permute-done((f32[128,128]{1,0:T(8,128)S(1)}, f32[128,128]{1,0:T(8,128)S(1)}, u32[]{:S(2)}, u32[]{:S(2)}) %collective-permute-start.10) | collective-permute-done | bytes 65568 | tf_op jit(solution)/shard_map/ppermute | solution.py:445
  68.0 1.9 %whiten.4 = (f32[128,256]{1,0:T(8,128)S(1)}, f32[128,256]{1,0:T(8,128)S(1)}, f32[256,256]{1,0:T(8,128)S(1)}, f32[256,256]{1,0:T(8,128)S(1)}, f32[256,256]{1,0:T(8,128)S(1)}, /*index=5*/f32[256,128]{1,0:T(8,128)S(1)}) custom-call(f32[128,128]{1,0:T(8,128)S(1)} %add.13.refs_0_, f32[128,128]{1,0:T(8,128)S(1)} %collective-permute-done.9.refs_1_, ...), custom_call_target="tpu_custom_call" | custom-call | flops 30000001024 | bytes 6000000 | tf_op jit(solution)/shard_map/whiten/pallas_call | solution.py:241
  70.0 5.2 %collective-permute-start.13 = (f32[128,256]{1,0:T(8,128)S(1)}, f32[128,256]{1,0:T(8,128)S(1)}, u32[]{:S(2)}, u32[]{:S(2)}) collective-permute-start(f32[128,256]{1,0:T(8,128)S(1)} %get-tuple-element.53.w_ref), channel_id=1, source_target_pairs={{0,15},{1,8},{2,9},{3,10},{4,11},{5,12},{6,13},{7,14},{16,31},{17,... | collective-permute-start | bytes 393224 | tf_op jit(solution)/shard_map/ppermute | solution.py:445
  75.2 1.5 collective-permute-start.14
  76.7 1.3 kept_second.2
  78.0 3.8 %collective-permute-start.19 = (f32[128,384]{1,0:T(8,128)S(1)}, f32[128,384]{1,0:T(8,128)S(1)}, u32[]{:S(2)}, u32[]{:S(2)}) collective-permute-start(f32[128,384]{1,0:T(8,128)S(1)} %get-tuple-element.61), channel_id=1, source_target_pairs={{0,15},{1,8},{2,9},{3,10},{4,11},{5,12},{6,13},{7,14},{8,0},{9,1},... | collective-permute-start | bytes 589832 | tf_op jit(solution)/shard_map/ppermute | solution.py:445
  81.8 0.9 combine.2
  82.7 1.1 collective-permute-start.15
  83.8 0.7 collective-permute-start.21
  84.5 1.1 collective-permute-done.19
  85.7 2.2 %collective-permute-done.15 = f32[128,128]{1,0:T(8,128)S(1)} collective-permute-done((f32[128,128]{1,0:T(8,128)S(1)}, f32[128,128]{1,0:T(8,128)S(1)}, u32[]{:S(2)}, u32[]{:S(2)}) %collective-permute-start.15) | collective-permute-done | bytes 65568 | tf_op jit(solution)/shard_map/ppermute | solution.py:445
  87.9 1.3 collective-permute-start.18
  89.2 1.4 collective-permute-start.17
  90.6 1.5 collective-permute-start.16
  92.1 2.6 %collective-permute-done.18.refs_3_ = f32[128,128]{1,0:T(8,128)S(1)} collective-permute-done((f32[128,128]{1,0:T(8,128)S(1)}, f32[128,128]{1,0:T(8,128)S(1)}, u32[]{:S(2)}, u32[]{:S(2)}) %collective-permute-start.18) | collective-permute-done | bytes 65568 | tf_op jit(solution)/shard_map/ppermute | solution.py:445
  94.7 0.8 collective-permute-done.17.refs_2_
  95.5 0.2 collective-permute-done.16.refs_1_
  95.7 1.9 %whiten.5 = (f32[128,256]{1,0:T(8,128)S(1)}, f32[128,256]{1,0:T(8,128)S(1)}, f32[256,256]{1,0:T(8,128)S(1)}, f32[256,256]{1,0:T(8,128)S(1)}, f32[256,256]{1,0:T(8,128)S(1)}, /*index=5*/f32[256,128]{1,0:T(8,128)S(1)}) custom-call(f32[128,128]{1,0:T(8,128)S(1)} %add.14.refs_0_, f32[128,128]{1,0:T(8,128)S(1)} %collective-permute-done.16.refs_1_, ...), custom_call_target="tpu_custom_call" | custom-call | flops 30000001024 | bytes 6000000 | tf_op jit(solution)/shard_map/whiten/pallas_call | solution.py:241
  97.6 3.7 %collective-permute-start.20 = (f32[128,256]{1,0:T(8,128)S(1)}, f32[128,256]{1,0:T(8,128)S(1)}, u32[]{:S(2)}, u32[]{:S(2)}) collective-permute-start(f32[128,256]{1,0:T(8,128)S(1)} %get-tuple-element.63.w_ref), channel_id=1, source_target_pairs={{0,15},{1,8},{2,9},{3,10},{4,11},{5,12},{6,13},{7,14},{16,31},{17,... | collective-permute-start | bytes 393224 | tf_op jit(solution)/shard_map/ppermute | solution.py:445
  101.3 1.3 collective-permute-start.22
  102.6 1.3 kept_second.3
  103.9 0.4 collective-permute-start.27
  104.3 0.9 collective-permute-done.20.w_ref
  105.2 1.4 collective-permute-done.22.refs_2_
  106.6 0.8 combine.3
  107.5 1.1 collective-permute-start.23
  108.6 3.2 %collective-permute-done.23 = f32[128,128]{1,0:T(8,128)S(1)} collective-permute-done((f32[128,128]{1,0:T(8,128)S(1)}, f32[128,128]{1,0:T(8,128)S(1)}, u32[]{:S(2)}, u32[]{:S(2)}) %collective-permute-start.23) | collective-permute-done | bytes 65568 | tf_op jit(solution)/shard_map/ppermute | solution.py:445
  111.8 1.9 %collective-permute-start.26 = (f32[128,128]{1,0:T(8,128)S(1)}, f32[128,128]{1,0:T(8,128)S(1)}, u32[]{:S(2)}, u32[]{:S(2)}) collective-permute-start(f32[128,128]{1,0:T(8,128)S(1)} %add.15.refs_0_), channel_id=1, source_target_pairs={{0,96},{1,97},{2,98},{3,99},{4,100},{5,101},{6,102},{7,103},{8,104... | collective-permute-start | bytes 196616 | tf_op jit(solution)/shard_map/ppermute | solution.py:445
  113.7 1.1 collective-permute-start.25
  114.8 1.2 collective-permute-start.24
  116.0 1.5 collective-permute-done.26.refs_3_
  117.5 2.0 %collective-permute-done.25.refs_2_ = f32[128,128]{1,0:T(8,128)S(1)} collective-permute-done((f32[128,128]{1,0:T(8,128)S(1)}, f32[128,128]{1,0:T(8,128)S(1)}, u32[]{:S(2)}, u32[]{:S(2)}) %collective-permute-start.25) | collective-permute-done | bytes 65568 | tf_op jit(solution)/shard_map/ppermute | solution.py:445
  119.5 0.6 collective-permute-done.24.refs_1_
  120.1 3.1 %last.1 = (f32[128,3072]{1,0:T(8,128)S(1)}, f32[128,256]{1,0:T(8,128)S(1)}) custom-call(s32[1]{0:T(128)} %bitcast.core_ref, f32[1,512]{1,0:T(1,128)S(1)} %copy-done.1, f32[128,128]{1,0:T(8,128)S(1)} %add.15.refs_0_, f32[128,128]{1,0:T(8,128)S(1)} %collective-permute-done.24.refs_1_, f32[128,128]{1,0:T(8,128)S(1)} %collective-permute-done.25.refs_2_, ...), custom_call_target="tpu_custom_call" | custom-call | flops 30000001024 | bytes 6000000 | tf_op jit(solution)/shard_map/last/pallas_call | solution.py:375
  123.2 0.2 collective-permute-start.28
  123.4 3.3 %collective-permute-done.28.got_ref = f32[128,3072]{1,0:T(8,128)S(1)} collective-permute-done((f32[128,3072]{1,0:T(8,128)S(1)}, f32[128,3072]{1,0:T(8,128)S(1)}, u32[]{:S(2)}, u32[]{:S(2)}) %collective-permute-start.28) | collective-permute-done | bytes 1572896 | tf_op jit(solution)/shard_map/ppermute | solution.py:445
  126.7 1.0 last_kept.1
  127.6 48.7 %all_to_all.5 = f32[64,4,3072]{2,1,0:T(4,128)S(1)} all-to-all(f32[64,4,3072]{2,1,0:T(4,128)S(1)} %last_kept.1), channel_id=1, replica_groups=mesh['zx'=8,'core'=2,'pairs'=8] {'pairs','zx'}, dimensions={0} | all-to-all | bytes 6291456 | tf_op jit(solution)/shard_map/all_to_all | solution.py:509
  176.4 3.7 %place.1 = f32[32,24576]{1,0:T(8,128)} custom-call(f32[8,8,4,3072]{3,2,1,0:T(4,128)S(1)} %bitcast.3), custom_call_target="tpu_custom_call" | custom-call | flops 30000000 | bytes 6000000 | tf_op jit(solution)/shard_map/place/pallas_call | solution.py:424
  (26 shorter events, 0.1 us)
Async XLA Ops:
  4.7 3.5 %collective-permute-start.1 = (f32[256,1536]{1,0:T(8,128)S(1)}, f32[256,1536]{1,0:T(8,128)S(1)}, u32[]{:S(2)}, u32[]{:S(2)}) collective-permute-start(f32[256,1536]{1,0:T(8,128)S(1)} %get-tuple-element.41), channel_id=1, source_target_pairs={{0,8},{1,9},{2,10},{3,11},{4,12},{5,13},{6,14},{7,15},{8,0},{9,1},... | collective-permute-start | bytes 4718600 | tf_op jit(solution)/shard_map/ppermute | solution.py:445
  8.9 5.7 %collective-permute-start.2 = (f32[264,128]{1,0:T(8,128)S(1)}, f32[264,128]{1,0:T(8,128)S(1)}, u32[]{:S(2)}, u32[]{:S(2)}) collective-permute-start(f32[264,128]{1,0:T(8,128)S(1)} %gram_second.1), channel_id=1, source_target_pairs={{0,16},{1,17},{2,18},{3,19},{4,20},{5,21},{6,22},{7,23},{8,24},{9,... | collective-permute-start | bytes 405512 | tf_op jit(solution)/shard_map/ppermute | solution.py:445
  14.6 22.6 %copy-start.2 = (f32[512]{0:T(512)S(1)}, f32[512]{0:T(512)}, u32[]{:S(2)}) copy-start(f32[512]{0:T(512)} %param.7) | copy-start | bytes 6148
  14.6 9.5 %collective-permute-start.5 = (f32[264,128]{1,0:T(8,128)S(1)}, f32[264,128]{1,0:T(8,128)S(1)}, u32[]{:S(2)}, u32[]{:S(2)}) collective-permute-start(f32[264,128]{1,0:T(8,128)S(1)} %add.12.refs_0_), channel_id=1, source_target_pairs={{0,96},{1,97},{2,98},{3,99},{4,100},{5,101},{6,102},{7,103},{8,104... | collective-permute-start | bytes 405512 | tf_op jit(solution)/shard_map/ppermute | solution.py:445
  18.8 7.5 %collective-permute-start.4 = (f32[264,128]{1,0:T(8,128)S(1)}, f32[264,128]{1,0:T(8,128)S(1)}, u32[]{:S(2)}, u32[]{:S(2)}) collective-permute-start(f32[264,128]{1,0:T(8,128)S(1)} %add.12.refs_0_), channel_id=1, source_target_pairs={{0,64},{1,65},{2,66},{3,67},{4,68},{5,69},{6,70},{7,71},{8,72},{9,... | collective-permute-start | bytes 405512 | tf_op jit(solution)/shard_map/ppermute | solution.py:445
  18.8 7.5 %collective-permute-start.3 = (f32[264,128]{1,0:T(8,128)S(1)}, f32[264,128]{1,0:T(8,128)S(1)}, u32[]{:S(2)}, u32[]{:S(2)}) collective-permute-start(f32[264,128]{1,0:T(8,128)S(1)} %add.12.refs_0_), channel_id=1, source_target_pairs={{0,32},{1,33},{2,34},{3,35},{4,36},{5,37},{6,38},{7,39},{8,40},{9,... | collective-permute-start | bytes 405512 | tf_op jit(solution)/shard_map/ppermute | solution.py:445
  29.8 25.3 %collective-permute-start.6 = (f32[128,3072]{1,0:T(8,128)S(1)}, f32[128,3072]{1,0:T(8,128)S(1)}, u32[]{:S(2)}, u32[]{:S(2)}) collective-permute-start(f32[128,3072]{1,0:T(8,128)S(1)} %get-tuple-element.46.refs_1_.x1_ref), channel_id=1, source_target_pairs={{0,8},{1,9},{2,10},{3,11},{4,12},{5,13},{6,14},{7,15},{8,1},{9,2},... | collective-permute-start | bytes 4718600 | tf_op jit(solution)/shard_map/ppermute | solution.py:445
  29.9 25.2 %collective-permute-start.7 = (f32[128,3072]{1,0:T(8,128)S(1)}, f32[128,3072]{1,0:T(8,128)S(1)}, u32[]{:S(2)}, u32[]{:S(2)}) collective-permute-start(f32[128,3072]{1,0:T(8,128)S(1)} %get-tuple-element.45.k_ref.x0_ref), channel_id=1, source_target_pairs={{0,15},{1,8},{2,9},{3,10},{4,11},{5,12},{6,13},{7,14},{16,31},{17,... | collective-permute-start | bytes 4718600 | tf_op jit(solution)/shard_map/ppermute | solution.py:445
  37.2 17.8 %collective-permute-start = (f32[1,512]{1,0:T(1,128)S(1)}, f32[1,512]{1,0:T(1,128)S(1)}, u32[]{:S(2)}, u32[]{:S(2)}) collective-permute-start(f32[1,512]{1,0:T(1,128)S(1)} %bitcast.4), channel_id=1, source_target_pairs={{0,7},{1,0},{2,1},{3,2},{4,3},{5,4},{6,5},{7,6},{8,15},{9,8},{10,9... | collective-permute-start | bytes 6152 | tf_op jit(solution)/shard_map/ppermute | solution.py:445
  55.0 0.8 copy-start
  55.8 4.3 %collective-permute-start.8 = (f32[128,128]{1,0:T(8,128)S(1)}, f32[128,128]{1,0:T(8,128)S(1)}, u32[]{:S(2)}, u32[]{:S(2)}) collective-permute-start(f32[128,128]{1,0:T(8,128)S(1)} %gram_cross.1), channel_id=1, source_target_pairs={{0,16},{1,17},{2,18},{3,19},{4,20},{5,21},{6,22},{7,23},{8,24},{9,... | collective-permute-start | bytes 196616 | tf_op jit(solution)/shard_map/ppermute | solution.py:445
  58.1 8.0 %collective-permute-start.12 = (f32[128,128]{1,0:T(8,128)S(1)}, f32[128,128]{1,0:T(8,128)S(1)}, u32[]{:S(2)}, u32[]{:S(2)}) collective-permute-start(f32[128,128]{1,0:T(8,128)S(1)} %get-tuple-element.52), channel_id=1, source_target_pairs={{0,8},{1,9},{2,10},{3,11},{4,12},{5,13},{6,14},{7,15},{8,1},{9,2},... | collective-permute-start | bytes 196616 | tf_op jit(solution)/shard_map/ppermute | solution.py:445
  60.2 5.9 %collective-permute-start.11 = (f32[128,128]{1,0:T(8,128)S(1)}, f32[128,128]{1,0:T(8,128)S(1)}, u32[]{:S(2)}, u32[]{:S(2)}) collective-permute-start(f32[128,128]{1,0:T(8,128)S(1)} %add.13.refs_0_), channel_id=1, source_target_pairs={{0,96},{1,97},{2,98},{3,99},{4,100},{5,101},{6,102},{7,103},{8,104... | collective-permute-start | bytes 196616 | tf_op jit(solution)/shard_map/ppermute | solution.py:445
  62.3 5.8 %collective-permute-start.10 = (f32[128,128]{1,0:T(8,128)S(1)}, f32[128,128]{1,0:T(8,128)S(1)}, u32[]{:S(2)}, u32[]{:S(2)}) collective-permute-start(f32[128,128]{1,0:T(8,128)S(1)} %add.13.refs_0_), channel_id=1, source_target_pairs={{0,64},{1,65},{2,66},{3,67},{4,68},{5,69},{6,70},{7,71},{8,72},{9,... | collective-permute-start | bytes 196616 | tf_op jit(solution)/shard_map/ppermute | solution.py:445
  62.6 5.5 %collective-permute-start.9 = (f32[128,128]{1,0:T(8,128)S(1)}, f32[128,128]{1,0:T(8,128)S(1)}, u32[]{:S(2)}, u32[]{:S(2)}) collective-permute-start(f32[128,128]{1,0:T(8,128)S(1)} %add.13.refs_0_), channel_id=1, source_target_pairs={{0,32},{1,33},{2,34},{3,35},{4,36},{5,37},{6,38},{7,39},{8,40},{9,... | collective-permute-start | bytes 196616 | tf_op jit(solution)/shard_map/ppermute | solution.py:445
  70.0 11.8 %collective-permute-start.13 = (f32[128,256]{1,0:T(8,128)S(1)}, f32[128,256]{1,0:T(8,128)S(1)}, u32[]{:S(2)}, u32[]{:S(2)}) collective-permute-start(f32[128,256]{1,0:T(8,128)S(1)} %get-tuple-element.53.w_ref), channel_id=1, source_target_pairs={{0,15},{1,8},{2,9},{3,10},{4,11},{5,12},{6,13},{7,14},{16,31},{17,... | collective-permute-start | bytes 393224 | tf_op jit(solution)/shard_map/ppermute | solution.py:445
  75.2 6.6 %collective-permute-start.14 = (f32[128,3072]{1,0:T(8,128)S(1)}, f32[128,3072]{1,0:T(8,128)S(1)}, u32[]{:S(2)}, u32[]{:S(2)}) collective-permute-start(f32[128,3072]{1,0:T(8,128)S(1)} %given.2), channel_id=1, source_target_pairs={{8,0},{9,1},{10,2},{11,3},{12,4},{13,5},{14,6},{15,7},{24,16},{25,... | collective-permute-start | bytes 4718600 | tf_op jit(solution)/shard_map/ppermute | solution.py:445
  78.0 7.7 %collective-permute-start.19 = (f32[128,384]{1,0:T(8,128)S(1)}, f32[128,384]{1,0:T(8,128)S(1)}, u32[]{:S(2)}, u32[]{:S(2)}) collective-permute-start(f32[128,384]{1,0:T(8,128)S(1)} %get-tuple-element.61), channel_id=1, source_target_pairs={{0,15},{1,8},{2,9},{3,10},{4,11},{5,12},{6,13},{7,14},{8,0},{9,1},... | collective-permute-start | bytes 589832 | tf_op jit(solution)/shard_map/ppermute | solution.py:445
  82.7 5.2 %collective-permute-start.15 = (f32[128,128]{1,0:T(8,128)S(1)}, f32[128,128]{1,0:T(8,128)S(1)}, u32[]{:S(2)}, u32[]{:S(2)}) collective-permute-start(f32[128,128]{1,0:T(8,128)S(1)} %get-tuple-element.60), channel_id=1, source_target_pairs={{0,16},{1,17},{2,18},{3,19},{4,20},{5,21},{6,22},{7,23},{8,24},{9,... | collective-permute-start | bytes 196616 | tf_op jit(solution)/shard_map/ppermute | solution.py:445
  83.8 20.5 %collective-permute-start.21 = (f32[128,3072]{1,0:T(8,128)S(1)}, f32[128,3072]{1,0:T(8,128)S(1)}, u32[]{:S(2)}, u32[]{:S(2)}) collective-permute-start(f32[128,3072]{1,0:T(8,128)S(1)} %given.2), channel_id=1, source_target_pairs={{8,15},{9,8},{10,9},{11,10},{12,11},{13,12},{14,13},{15,14},{24,31... | collective-permute-start | bytes 4718600 | tf_op jit(solution)/shard_map/ppermute | solution.py:445
  87.9 6.8 %collective-permute-start.18 = (f32[128,128]{1,0:T(8,128)S(1)}, f32[128,128]{1,0:T(8,128)S(1)}, u32[]{:S(2)}, u32[]{:S(2)}) collective-permute-start(f32[128,128]{1,0:T(8,128)S(1)} %add.14.refs_0_), channel_id=1, source_target_pairs={{0,96},{1,97},{2,98},{3,99},{4,100},{5,101},{6,102},{7,103},{8,104... | collective-permute-start | bytes 196616 | tf_op jit(solution)/shard_map/ppermute | solution.py:445
  89.2 6.3 %collective-permute-start.17 = (f32[128,128]{1,0:T(8,128)S(1)}, f32[128,128]{1,0:T(8,128)S(1)}, u32[]{:S(2)}, u32[]{:S(2)}) collective-permute-start(f32[128,128]{1,0:T(8,128)S(1)} %add.14.refs_0_), channel_id=1, source_target_pairs={{0,64},{1,65},{2,66},{3,67},{4,68},{5,69},{6,70},{7,71},{8,72},{9,... | collective-permute-start | bytes 196616 | tf_op jit(solution)/shard_map/ppermute | solution.py:445
  90.6 5.1 %collective-permute-start.16 = (f32[128,128]{1,0:T(8,128)S(1)}, f32[128,128]{1,0:T(8,128)S(1)}, u32[]{:S(2)}, u32[]{:S(2)}) collective-permute-start(f32[128,128]{1,0:T(8,128)S(1)} %add.14.refs_0_), channel_id=1, source_target_pairs={{0,32},{1,33},{2,34},{3,35},{4,36},{5,37},{6,38},{7,39},{8,40},{9,... | collective-permute-start | bytes 196616 | tf_op jit(solution)/shard_map/ppermute | solution.py:445
  97.6 7.6 %collective-permute-start.20 = (f32[128,256]{1,0:T(8,128)S(1)}, f32[128,256]{1,0:T(8,128)S(1)}, u32[]{:S(2)}, u32[]{:S(2)}) collective-permute-start(f32[128,256]{1,0:T(8,128)S(1)} %get-tuple-element.63.w_ref), channel_id=1, source_target_pairs={{0,15},{1,8},{2,9},{3,10},{4,11},{5,12},{6,13},{7,14},{16,31},{17,... | collective-permute-start | bytes 393224 | tf_op jit(solution)/shard_map/ppermute | solution.py:445
  101.3 5.3 %collective-permute-start.22 = (f32[128,3072]{1,0:T(8,128)S(1)}, f32[128,3072]{1,0:T(8,128)S(1)}, u32[]{:S(2)}, u32[]{:S(2)}) collective-permute-start(f32[128,3072]{1,0:T(8,128)S(1)} %given.3), channel_id=1, source_target_pairs={{8,0},{9,1},{10,2},{11,3},{12,4},{13,5},{14,6},{15,7},{24,16},{25,... | collective-permute-start | bytes 4718600 | tf_op jit(solution)/shard_map/ppermute | solution.py:445
  103.9 12.1 %collective-permute-start.27 = (f32[128,384]{1,0:T(8,128)S(1)}, f32[128,384]{1,0:T(8,128)S(1)}, u32[]{:S(2)}, u32[]{:S(2)}) collective-permute-start(f32[128,384]{1,0:T(8,128)S(1)} %get-tuple-element.72), channel_id=1, source_target_pairs={{0,15},{1,8},{2,9},{3,10},{4,11},{5,12},{6,13},{7,14},{8,0},{9,1},... | collective-permute-start | bytes 589832 | tf_op jit(solution)/shard_map/ppermute | solution.py:445
  106.6 13.5 %copy-start.1 = (f32[1,512]{1,0:T(1,128)S(1)}, f32[1,512]{1,0:T(1,128)}, u32[]{:S(2)}) copy-start(f32[1,512]{1,0:T(1,128)} %copy-done) | copy-start | bytes 6148
  107.5 4.3 %collective-permute-start.23 = (f32[128,128]{1,0:T(8,128)S(1)}, f32[128,128]{1,0:T(8,128)S(1)}, u32[]{:S(2)}, u32[]{:S(2)}) collective-permute-start(f32[128,128]{1,0:T(8,128)S(1)} %get-tuple-element.71), channel_id=1, source_target_pairs={{0,16},{1,17},{2,18},{3,19},{4,20},{5,21},{6,22},{7,23},{8,24},{9,... | collective-permute-start | bytes 196616 | tf_op jit(solution)/shard_map/ppermute | solution.py:445
  111.8 5.7 %collective-permute-start.26 = (f32[128,128]{1,0:T(8,128)S(1)}, f32[128,128]{1,0:T(8,128)S(1)}, u32[]{:S(2)}, u32[]{:S(2)}) collective-permute-start(f32[128,128]{1,0:T(8,128)S(1)} %add.15.refs_0_), channel_id=1, source_target_pairs={{0,96},{1,97},{2,98},{3,99},{4,100},{5,101},{6,102},{7,103},{8,104... | collective-permute-start | bytes 196616 | tf_op jit(solution)/shard_map/ppermute | solution.py:445
  113.7 5.8 %collective-permute-start.25 = (f32[128,128]{1,0:T(8,128)S(1)}, f32[128,128]{1,0:T(8,128)S(1)}, u32[]{:S(2)}, u32[]{:S(2)}) collective-permute-start(f32[128,128]{1,0:T(8,128)S(1)} %add.15.refs_0_), channel_id=1, source_target_pairs={{0,64},{1,65},{2,66},{3,67},{4,68},{5,69},{6,70},{7,71},{8,72},{9,... | collective-permute-start | bytes 196616 | tf_op jit(solution)/shard_map/ppermute | solution.py:445
  114.8 5.3 %collective-permute-start.24 = (f32[128,128]{1,0:T(8,128)S(1)}, f32[128,128]{1,0:T(8,128)S(1)}, u32[]{:S(2)}, u32[]{:S(2)}) collective-permute-start(f32[128,128]{1,0:T(8,128)S(1)} %add.15.refs_0_), channel_id=1, source_target_pairs={{0,32},{1,33},{2,34},{3,35},{4,36},{5,37},{6,38},{7,39},{8,40},{9,... | collective-permute-start | bytes 196616 | tf_op jit(solution)/shard_map/ppermute | solution.py:445
  123.2 3.5 %collective-permute-start.28 = (f32[128,3072]{1,0:T(8,128)S(1)}, f32[128,3072]{1,0:T(8,128)S(1)}, u32[]{:S(2)}, u32[]{:S(2)}) collective-permute-start(f32[128,3072]{1,0:T(8,128)S(1)} %get-tuple-element.76), channel_id=1, source_target_pairs={{0,8},{1,9},{2,10},{3,11},{4,12},{5,13},{6,14},{7,15},{8,0},{9,1},... | collective-permute-start | bytes 4718600 | tf_op jit(solution)/shard_map/ppermute | solution.py:445
